TPU v7x, 32 devices: a whole 2x2x4 slice. The times are simulated.
32 devices in a mesh: groups: 2 (over y), pair: 4 (over z), ints: 2 (over x), rep: 2 (over core).
Axes of the slice: x: 2, y: 2, z: 4, core: 2. Of those that a mesh axis runs over, the one named last changes fastest.
Arguments:
- amplitudes: bfloat16 [1024, 16, 4096], P(('groups', 'pair', 'ints', 'rep')), parts along dimension 0, may hold values from -6 to 6
- integrals: bfloat16 [256, 65536], P(('groups', 'ints'), 'pair'), parts along dimension 0, may hold values from -0.03125 to 0.03125
- pair_irrep: int32 [1024], P(('groups', 'pair', 'ints', 'rep')), parts along dimension 0, may hold values from 0 to 1
- slot_irrep: int32 [32], P('groups'), parts along dimension 0, may hold values from 0 to 1, as said below
- owner_slot_map: int32 [32], P('groups'), parts along dimension 0, may hold values from 0 to 15, each once
Outputs:
- ladder: float32 [1024, 128], P(('groups', 'pair', 'ints', 'rep')), parts along dimension 0
There are 2 independent parts, one for each index of `groups`. A program takes and returns all parts, laid end to end along the dimension named above; each array names one. Nothing has to cross between parts.
Inputs may be any that keep to these rules, and one draw needn't show every extreme that they name: `slot_irrep`: every irrep labels the same number of slots.
All inputs are finite; a program needn't handle non-finite values.
Results may differ from a plain program's by a relative error of at most 0.0003.
Values may be sent and summed in bfloat16 or wider, within the bound.
No kernel may reach another device: no remote copies, remote signals or barrier semaphores. Data moves between devices by JAX's collectives and lax.ppermute only.
A program may use at most 64 MiB of HBM per device.

v0:
```python
import jax
import jax.numpy as jnp
from jax import lax
from jax.sharding import PartitionSpec as P


def on_device(amplitudes, integrals, pair_irrep, slot_irrep, owner_slot_map):
    row_count, slot_count, tile_size = amplitudes.shape
    slot_position_index = jnp.arange(slot_count, dtype=jnp.int32)
    picked = owner_slot_map[:, None] == slot_position_index[None, :]
    owner_irrep = jnp.sum(jnp.where(picked, slot_irrep[None, :], 0), axis=1)
    sorted_slots = jnp.take(amplitudes, owner_slot_map, axis=1)
    live_tiles = pair_irrep[:, None] == owner_irrep[None, :]
    sorted_slots = jnp.where(live_tiles[:, :, None], sorted_slots, jnp.zeros((), jnp.bfloat16))
    flattened = sorted_slots.reshape(row_count, slot_count * tile_size)
    columns = lax.all_to_all(flattened, "pair", split_axis=1, concat_axis=0, tiled=True)
    partial_sums = lax.dot_general(
        columns,
        lax.all_gather(integrals, "ints", axis=0, tiled=True),
        (((1,), (1,)), ((), ())),
        preferred_element_type=jnp.float32,
    )
    return lax.psum_scatter(partial_sums, "pair", scatter_dimension=0, tiled=True)


def solution(mesh):
    placed = (
        P(("groups", "pair", "ints", "rep"), None, None),
        P(("groups", "ints"), "pair"),
        P(("groups", "pair", "ints", "rep")),
        P("groups"),
        P("groups"),
    )
    return jax.shard_map(
        on_device,
        mesh=mesh,
        in_specs=placed,
        out_specs=P(("groups", "pair", "ints", "rep"), None),
        check_vma=False,
    )
```

profile of v0, /device:TPU:0, one launch (start us, length us, event | category | flops | bytes accessed | tf_op | source)
XLA Modules:
  0.0 178.5 jit_solution(8698455286225283420)
XLA Ops:
  6.5 0.7 compare_select_fusion
  7.2 0.7 compare_and_fusion
  7.9 12.1 %gather_fusion = bf16[16,32,4096]{2,0,1:T(8,128)(2,1)} fusion(bf16[32,16,4096]{2,1,0:T(8,128)(2,1)} %param.5, s32[1024]{0:T(1024)S(1)} %pad_clamp_fusion), kind=kCustom, calls=%fused_computation | custom fusion | bytes 8388672 | tf_op jit(solution)/shard_map/jit(_take)/gather | solution.py:12
  20.0 8.6 %gather.7 = bf16[32,4,16384]{2,1,0:T(4,128)(2,1)} reshape(bf16[32,16,4096]{2,1,0:T(8,128)(2,1)} %bitcast.9) | data formatting | bytes 8388608 | tf_op jit(solution)/shard_map/jit(_take)/gather | solution.py:12
  28.5 0.0 copy-done.1
  28.5 0.0 copy-done.2
  28.5 0.2 select_reduce_fusion
  28.7 0.0 copy-done
  28.7 0.1 broadcast_compare_fusion
  28.8 1.9 %broadcast_in_dim.52 = pred[32,16,4096]{2,1,0:T(8,128)(4,1)} broadcast(pred[32,16]{1,0:T(8,128)(4,1)S(1)} %broadcast_compare_fusion), dimensions={0,1} | broadcast | bytes 2097664 | tf_op jit(solution)/shard_map/jit(_where)/broadcast_in_dim | solution.py:14
  30.7 6.8 %broadcast_in_dim.53 = pred[32,4,16384]{2,1,0:T(4,128)(4,1)S(1)} reshape(pred[32,16,4096]{2,1,0:T(8,128)(4,1)} %broadcast_in_dim.52) | data formatting | bytes 4194304 | tf_op jit(solution)/shard_map/jit(_where)/broadcast_in_dim | solution.py:14
  37.5 0.1 broadcast_in_dim.54
  37.6 0.1 broadcast_bitcast_fusion
  37.7 0.1 copy.10
  37.8 6.1 %select_select_fusion = bf16[32,4,16384]{2,1,0:T(4,128)(2,1)S(1)} fusion(pred[32,4,16384]{2,1,0:T(4,128)(4,1)S(1)} %broadcast_in_dim.53, bf16[32,4,16384]{2,1,0:T(4,128)(2,1)} %gather.7, pred[4,16384]{1,0:T(4,128)(4,1)S(1)} %bitcast.10), kind=kLoop, calls=%fused_computation.1 | loop fusion | flops 4194304 | bytes 10551296 | tf_op jit(solution)/shard_map/jit(_where)/select_n | solution.py:14
  44.0 4.3 %copy.9 = bf16[32,4,16384]{2,0,1:T(8,128)(2,1)} copy(bf16[32,4,16384]{2,1,0:T(4,128)(2,1)S(1)} %select_select_fusion) | data formatting | bytes 8388608 | tf_op jit(solution)/shard_map/jit(_where)/select_n | solution.py:14
  48.2 6.3 %all-to-all-start = ((bf16[32,4,16384]{2,0,1:T(8,128)(2,1)}), bf16[32,4,16384]{2,0,1:T(8,128)(2,1)}, u32[]{:S(2)}, u32[]{:S(2)}) async-start(bf16[32,4,16384]{2,0,1:T(8,128)(2,1)} %copy.9), calls=%async_computation | async-start | bytes 8388608 | tf_op jit(solution)/shard_map/all_to_all | solution.py:16
  54.5 0.7 all-gather.2.cloned.1.call-update
  55.3 0.0 reduce-scatter.2.cloned.1.call-start
  55.3 59.8 %all-gather.2.cloned.1.call-done = bf16[128,16384]{1,0:T(8,128)(2,1)} async-done(((bf16[64,16384]{1,0:T(8,128)(2,1)}), bf16[128,16384]{1,0:T(8,128)(2,1)}) %all-gather.2.cloned.1.call-update) | async-done | bytes 4194320 | tf_op jit(solution)/shard_map/all_gather | solution.py:19
  115.1 32.8 %all-to-all-done = bf16[32,4,16384]{2,0,1:T(8,128)(2,1)} async-done(((bf16[32,4,16384]{2,0,1:T(8,128)(2,1)}), bf16[32,4,16384]{2,0,1:T(8,128)(2,1)}, u32[]{:S(2)}, u32[]{:S(2)}) %all-to-all-start) | async-done | bytes 4194336 | tf_op jit(solution)/shard_map/all_to_all | solution.py:16
  148.0 5.3 %fusion = f32[128,128]{1,0:T(8,128)} fusion(bf16[128,16384]{1,0:T(8,128)(2,1)} %bitcast.2, bf16[128,16384]{1,0:T(8,128)(2,1)} %all-gather.2.cloned.1.call-done), kind=kOutput, calls=%fused_computation.9 | convolution fusion | flops 536870912 | bytes 8454144 | tf_op jit(solution)/shard_map/dot_general | solution.py:17
  153.3 0.0 reduce-scatter.2.cloned.1.call-update
  153.3 18.3 %reduce-scatter.2.cloned.1.call-done = f32[32,128]{1,0:T(8,128)} async-done(((f32[128,128]{1,0:T(8,128)}), f32[32,128]{1,0:T(8,128)}) %reduce-scatter.2.cloned.1.call-update) | async-done | bytes 16400 | tf_op jit(solution)/shard_map/reduce_scatter | solution.py:23
  (5 shorter events, 0.0 us)
Async XLA Ops:
  20.0 8.6 %copy-start.1 = (s32[16]{0:T(128)S(1)}, s32[16]{0:T(128)}, u32[]{:S(2)}) copy-start(s32[16]{0:T(128)} %param.8) | copy-start | bytes 196
  20.0 8.6 %copy-start.2 = (s32[16]{0:T(128)S(1)}, s32[16]{0:T(128)}, u32[]{:S(2)}) copy-start(s32[16]{0:T(128)} %param.9) | copy-start | bytes 196
  20.0 8.7 %copy-start = (s32[32]{0:T(128)S(1)}, s32[32]{0:T(128)}, u32[]{:S(2)}) copy-start(s32[32]{0:T(128)} %param.7) | copy-start | bytes 388
  48.2 99.7 %all-to-all-start = ((bf16[32,4,16384]{2,0,1:T(8,128)(2,1)}), bf16[32,4,16384]{2,0,1:T(8,128)(2,1)}, u32[]{:S(2)}, u32[]{:S(2)}) async-start(bf16[32,4,16384]{2,0,1:T(8,128)(2,1)} %copy.9), calls=%async_computation | async-start | bytes 8388608 | tf_op jit(solution)/shard_map/all_to_all | solution.py:16
  54.5 60.6 %all-gather.2.cloned.1.call-start = ((), (), s32[]{:S(2)}) async-start(), calls=%async_computation.2 | async-start | bytes 6291456 | tf_op jit(solution)/shard_map/all_gather | solution.py:19
  55.3 116.4 %reduce-scatter.2.cloned.1.call-start = ((), (), s32[]{:S(2)}) async-start(), calls=%async_computation.3 | async-start | bytes 81920 | tf_op jit(solution)/shard_map/reduce_scatter | solution.py:23
Sparse Core Ops, SparseCore 0:
  56.9 58.2 all-gather.1
  153.4 18.1 reduce-scatter.1
where the time goes:
time: 179 us; the launch traced here: 178 us
  waiting for transfers between devices  112 us (63%)
  local copies, waits for them, and re-layouts  33.9 us (19%)
  between operations  13.4 us (7%)
  other arithmetic  7.7 us (4%)
  starting transfers between devices  6.36 us (4%)
  matrix products  5.33 us (3%)
    all_gather x1, waiting for transfers between devices, on_device(): lax.all_gather(integrals, 'ints', axis=0, tiled=True)  59.8 us
    all_to_all x1, waiting for transfers between devices, on_device(): lax.all_to_all(flattened, 'pair', split_axis=1, concat_axis=0, tiled=True)  32.8 us
    gather x2, local copies, waits for them, and re-layouts, on_device(): sorted_slots = jnp.take(amplitudes, owner_slot_map, axis=1)  20.7 us
    reduce_scatter x1, waiting for transfers between devices, on_device(): lax.psum_scatter(partial_sums, 'pair', scatter_dimension=0, tiled=True)  18.3 us
    broadcast_in_dim x2, local copies, waits for them, and re-layouts, on_device(): jnp.where(live_tiles[:, :, None], sorted_slots, jnp.zeros((), jnp.bfloat16))  8.72 us
    all_to_all x1, starting transfers between devices, on_device(): lax.all_to_all(flattened, 'pair', split_axis=1, concat_axis=0, tiled=True)  6.32 us
    select_n x1, other arithmetic, on_device(): jnp.where(live_tiles[:, :, None], sorted_slots, jnp.zeros((), jnp.bfloat16))  6.13 us
    dot_general x1, matrix products, on_device(): lax.dot_general(columns, lax.all_gather(integrals, 'ints', axis=0, tiled=...  5.33 us
  transfers between devices with their start and end apart: 3, of which 3 were waited for; matrix products, arithmetic and copies ran while one was open for 0% of the time, Pallas kernels for 0%

commit v1 on v0

--- a/solution.py
+++ b/solution.py
@@ -1,10 +1,21 @@
+import functools
+
 import jax
 import jax.numpy as jnp
 from jax import lax
+from jax.experimental import pallas as pl
+from jax.experimental.pallas import tpu as pltpu
 from jax.sharding import PartitionSpec as P
 
-
-def on_device(amplitudes, integrals, pair_irrep, slot_irrep, owner_slot_map):
+VMEM_LIMIT = 48 * 1024 * 1024
+NT = (((1,), (1,)), ((), ()))
+SWAP = [(0, 1), (1, 0)]
+NEAR = [(0, 1), (1, 0), (2, 3), (3, 2)]
+MIDDLE = [(1, 2), (2, 1)]
+OUTWARD = [(1, 0), (2, 3)]
+
+
+def plain(amplitudes, integrals, pair_irrep, slot_irrep, owner_slot_map):
     row_count, slot_count, tile_size = amplitudes.shape
     slot_position_index = jnp.arange(slot_count, dtype=jnp.int32)
     picked = owner_slot_map[:, None] == slot_position_index[None, :]
@@ -17,10 +28,235 @@
     partial_sums = lax.dot_general(
         columns,
         lax.all_gather(integrals, "ints", axis=0, tiled=True),
-        (((1,), (1,)), ((), ())),
+        NT,
         preferred_element_type=jnp.float32,
     )
     return lax.psum_scatter(partial_sums, "pair", scatter_dimension=0, tiled=True)
+
+
+def own_half_kernel(where_ref, x_ref, first_ref, second_ref):
+    step = pl.program_id(0)
+    per = pl.num_programs(0) // 2
+
+    @pl.when(step < per)
+    def _():
+        first_ref[0] = x_ref[...]
+
+    @pl.when(step >= per)
+    def _():
+        second_ref[0] = x_ref[...]
+
+
+def own_half(where, integrals, tile):
+    rows, columns = integrals.shape
+    held, half = columns // tile, tile // 2
+    per = held // 2
+    chunk = jax.ShapeDtypeStruct((per, rows, half), integrals.dtype)
+    return pl.pallas_call(
+        own_half_kernel,
+        grid_spec=pltpu.PrefetchScalarGridSpec(
+            num_scalar_prefetch=1,
+            grid=(held,),
+            in_specs=[pl.BlockSpec((rows, half), lambda i, w: (0, 2 * i + w[1]))],
+            out_specs=[
+                pl.BlockSpec((1, rows, half), lambda i, w: (jnp.minimum(i, per - 1), 0, 0)),
+                pl.BlockSpec((1, rows, half), lambda i, w: (jnp.maximum(i - per, 0), 0, 0)),
+            ],
+        ),
+        out_shape=[chunk, chunk],
+        cost_estimate=pl.CostEstimate(flops=0, bytes_accessed=4 * rows * columns, transcendentals=0),
+        name="own_half",
+    )(where, integrals)
+
+
+def pack_kernel(rows, slots, where_ref, slot_irrep_ref, slot_map_ref, pair_irrep_ref, x_ref, other_ref, mine_ref, rank_ref, irrep_ref, pick_ref):
+    step = pl.program_id(0)
+    per = pl.num_programs(0) // 2
+
+    @pl.when(step == 0)
+    def _():
+        lane = lax.broadcasted_iota(jnp.int32, (1, rows * slots), 1)
+        slot_lane, row_lane = lane % slots, lane // slots
+        counts = [jnp.int32(0), jnp.int32(0)]
+        lane_rank = jnp.zeros_like(lane)
+        lane_irrep = jnp.zeros_like(lane)
+        for q in range(slots):
+            slot = slot_map_ref[q]
+            irrep = slot_irrep_ref[slot]
+            odd = irrep == 1
+            rank = jnp.where(odd, counts[1], counts[0])
+            counts = [jnp.where(odd, counts[0], counts[0] + 1), jnp.where(odd, counts[1] + 1, counts[1])]
+            rank_ref[q] = rank
+            irrep_ref[q] = irrep
+            here = slot_lane == slot
+            lane_rank = jnp.where(here, rank, lane_rank)
+            lane_irrep = jnp.where(here, irrep, lane_irrep)
+        row_irrep = jnp.zeros_like(lane)
+        for o in range(rows):
+            row_irrep = jnp.where(row_lane == o, pair_irrep_ref[o], row_irrep)
+        target = jnp.where(lane_irrep == row_irrep, lane_rank * rows + row_lane, -1)
+        row = lax.broadcasted_iota(jnp.int32, pick_ref.shape, 0)
+        pick_ref[...] = jnp.where(row == target, 1.0, 0.0).astype(pick_ref.dtype)
+
+    packed = jnp.dot(pick_ref[...], x_ref[...], preferred_element_type=jnp.float32).astype(x_ref.dtype)
+
+    @pl.when(step < per)
+    def _():
+        other_ref[...] = packed
+
+    @pl.when(step >= per)
+    def _():
+        mine_ref[...] = packed
+
+
+def pack(where, amplitudes, pair_irrep, slot_irrep, owner_slot_map, steps=4):
+    rows, slots, tile = amplitudes.shape
+    live, half, per = slots // 2, tile // 2, steps // 2
+    width = tile // steps
+    packed = jax.ShapeDtypeStruct((live * rows, half), amplitudes.dtype)
+    tables = jax.ShapeDtypeStruct((slots,), jnp.int32)
+    smem = pl.BlockSpec(memory_space=pltpu.SMEM)
+
+    def column(i, w, *_):
+        half_here = jnp.where(i < per, 1 - w[1], w[1])
+        return (0, half_here * per + i % per)
+
+    return pl.pallas_call(
+        functools.partial(pack_kernel, rows, slots),
+        grid_spec=pltpu.PrefetchScalarGridSpec(
+            num_scalar_prefetch=4,
+            grid=(steps,),
+            in_specs=[pl.BlockSpec((rows * slots, width), column)],
+            out_specs=[
+                pl.BlockSpec((live * rows, width), lambda i, *_: (0, jnp.minimum(i, per - 1))),
+                pl.BlockSpec((live * rows, width), lambda i, *_: (0, jnp.maximum(i - per, 0))),
+                smem,
+                smem,
+            ],
+            scratch_shapes=[pltpu.VMEM((live * rows, rows * slots), amplitudes.dtype)],
+        ),
+        out_shape=[packed, packed, tables, tables],
+        compiler_params=pltpu.CompilerParams(vmem_limit_bytes=VMEM_LIMIT),
+        cost_estimate=pl.CostEstimate(
+            flops=2 * live * rows * rows * slots * tile, bytes_accessed=3 * rows * slots * tile, transcendentals=0
+        ),
+        name="pack",
+    )(where, slot_irrep, owner_slot_map, pair_irrep, amplitudes.reshape(rows * slots, tile))
+
+
+def sum_kernel(rows, table, counts, begun, where_ref, rank_ref, irrep_ref, *refs):
+    tiles, refs = refs[:4], refs[4:]
+    chunks, refs = refs[: len(counts)], refs[len(counts) :]
+    if begun:
+        begun_ref, out_ref, total_ref = refs
+    else:
+        out_ref, total_ref = refs
+    total_ref[...] = jnp.zeros_like(total_ref)
+    place = where_ref[0]
+    entry = 0
+    for chunk_ref, count in zip(chunks, counts):
+        for i in range(count):
+            position = jnp.int32(table[0][entry])
+            for z in range(1, len(table)):
+                position = jnp.where(place == z, table[z][entry], position)
+            entry += 1
+
+            @pl.when(position >= 0)
+            def _():
+                at = jnp.maximum(position, 0)
+                start = pl.multiple_of(rank_ref[at] * rows, rows)
+                here = jnp.concatenate([t[pl.ds(start, rows), :] for t in tiles], axis=0)
+                term = lax.dot_general(here, chunk_ref[i], NT, preferred_element_type=jnp.float32)
+                total_ref[irrep_ref[at]] += term
+
+    out = jnp.concatenate([total_ref[0], total_ref[1]], axis=1)
+    if begun:
+        out = out + begun_ref[...]
+    out_ref[...] = out
+
+
+def add_positions(where, rank, irrep, tiles, chunks, table, begun=None, name="sum"):
+    live = rank.shape[0] // 2
+    rows = tiles[0].shape[0] // live
+    ab = chunks[0].shape[1]
+    counts = tuple(c.shape[0] for c in chunks)
+    vmem = pl.BlockSpec(memory_space=pltpu.VMEM)
+    smem = pl.BlockSpec(memory_space=pltpu.SMEM)
+    more = [] if begun is None else [begun]
+    entries = sum(counts)
+    return pl.pallas_call(
+        functools.partial(sum_kernel, rows, table, counts, begun is not None),
+        in_specs=[smem] * 3 + [vmem] * (4 + len(chunks) + len(more)),
+        out_specs=vmem,
+        out_shape=jax.ShapeDtypeStruct((4 * rows, 2 * ab), jnp.float32),
+        scratch_shapes=[pltpu.VMEM((2, 4 * rows, ab), jnp.float32)],
+        compiler_params=pltpu.CompilerParams(vmem_limit_bytes=VMEM_LIMIT),
+        cost_estimate=pl.CostEstimate(
+            flops=8 * rows * ab * chunks[0].shape[2] * entries,
+            bytes_accessed=2 * sum(c.size for c in chunks) + 2 * sum(t.size for t in tiles),
+            transcendentals=0,
+        ),
+        name=name,
+    )(where, rank, irrep, *tiles, *chunks, *more)
+
+
+def on_line(amplitudes, integrals, pair_irrep, slot_irrep, owner_slot_map):
+    rows, slots, tile = amplitudes.shape
+    place, side, core = lax.axis_index("pair"), lax.axis_index("ints"), lax.axis_index("rep")
+    where = jnp.stack([place, core]).astype(jnp.int32)
+    across = [(i, 3 - i) for i in range(4)]
+    beside = [(i, i ^ 2) for i in range(4)]
+
+    first, second = own_half(where, integrals, tile)
+    near1 = lax.ppermute(first, "pair", NEAR)
+    mid1 = lax.ppermute(first, "pair", MIDDLE)
+    near2 = lax.ppermute(second, "pair", NEAR)
+    mid2 = lax.ppermute(second, "pair", MIDDLE)
+
+    other, mine, rank, irrep = pack(where, amplitudes, pair_irrep, slot_irrep, owner_slot_map)
+    from_core = lax.ppermute(other, "rep", SWAP)
+    from_side = lax.ppermute(mine, ("ints", "rep"), beside)
+    from_across = lax.ppermute(other, ("ints", "rep"), across)
+
+    mid3 = lax.ppermute(near1, "pair", MIDDLE)
+    out1 = lax.ppermute(mid1, "pair", OUTWARD)
+    mid4 = lax.ppermute(near2, "pair", MIDDLE)
+    out2 = lax.ppermute(mid2, "pair", OUTWARD)
+    out3 = lax.ppermute(mid3, "pair", OUTWARD)
+    out4 = lax.ppermute(mid4, "pair", OUTWARD)
+
+    tiles = (mine, from_core, from_side, from_across)
+    held = slots // 4
+    per = held // 2
+
+    def chunk_of(z, b):
+        return list(range(z * held + b * per, z * held + b * per + per))
+
+    none = [-1] * per
+    table = []
+    for z in range(4):
+        near, far = z ^ 1, 3 - z
+        inner = z in (1, 2)
+        row = chunk_of(z, 0) + chunk_of(z, 1) + chunk_of(near, 0) + chunk_of(near, 1)
+        if inner:
+            row += chunk_of(far, 0) + chunk_of(far, 1) + chunk_of(far ^ 1, 0) + chunk_of(far ^ 1, 1) + none * 3
+        else:
+            row += none * 4 + chunk_of(far ^ 1, 0) + chunk_of(far ^ 1, 1) + chunk_of(far, 0)
+        table.append(tuple(row))
+    partial_sums = add_positions(
+        where, rank, irrep, tiles, (first, second, near1, near2, mid1, mid2, mid3, mid4, out1, out2, out3), tuple(table), name="sum_most"
+    )
+    last = tuple(tuple(none if z in (1, 2) else chunk_of(3 - z, 1)) for z in range(4))
+    partial_sums = add_positions(where, rank, irrep, tiles, (out4,), last, partial_sums, name="sum_last")
+
+    blocks = [partial_sums[i * rows : (i + 1) * rows] for i in range(4)]
+    own = blocks[0] + lax.ppermute(blocks[1], "rep", SWAP)
+    theirs = lax.ppermute(blocks[2], ("ints", "rep"), beside) + lax.ppermute(blocks[3], ("ints", "rep"), across)
+    ab = integrals.shape[0]
+    odd = (pair_irrep == 1)[:, None]
+    own = jnp.where(odd, own[:, ab:], own[:, :ab])
+    theirs = jnp.where(odd, theirs[:, ab:], theirs[:, :ab])
+    return jnp.where(side == 0, jnp.concatenate([own, theirs], axis=1), jnp.concatenate([theirs, own], axis=1))
 
 
 def solution(mesh):
@@ -31,8 +267,9 @@
         P("groups"),
         P("groups"),
     )
+    line = mesh.shape["pair"] == 4 and mesh.shape["ints"] == 2 and mesh.shape["rep"] == 2
     return jax.shard_map(
-        on_device,
+        on_line if line else plain,
         mesh=mesh,
         in_specs=placed,
         out_specs=P(("groups", "pair", "ints", "rep"), None),

time: 179 us -> 110 us (0.61)
  waiting for transfers between devices: 112 us -> 68 us
  local copies, waits for them, and re-layouts: 33.9 us -> 7.52 us
  Pallas kernels: 0 us -> 17.2 us
  between operations: 13.4 us -> 0.19 us
  starting transfers between devices: 6.36 us -> 14.7 us
  other arithmetic: 7.7 us -> 1.4 us
  matrix products: 5.33 us -> 0 us
    ppermute x0 -> x16, waiting for transfers between devices: none -> 68 us  [the longest x1 14.8 us: on_line(): from_across = lax.ppermute(other, ('ints', 'rep'), across)]
    all_gather x1 -> x0, waiting for transfers between devices: 59.8 us -> none  [on_device(): lax.all_gather(integrals, 'ints', axis=0, tiled=True)]
    all_to_all x1 -> x0, waiting for transfers between devices: 32.8 us -> none  [on_device(): lax.all_to_all(flattened, 'pair', split_axis=1, concat_axis=0, tiled=True)]
    gather x2 -> x0, local copies, waits for them, and re-layouts: 20.7 us -> none  [on_device(): sorted_slots = jnp.take(amplitudes, owner_slot_map, axis=1)]
    reduce_scatter x1 -> x0, waiting for transfers between devices: 18.3 us -> none  [on_device(): lax.psum_scatter(partial_sums, 'pair', scatter_dimension=0, tiled=True)]
    pallas_call x0 -> x4, Pallas kernels: none -> 17.2 us  [the longest x2 7.48 us: add_positions(): pl.pallas_call(functools.partial(sum_kernel, rows, table, counts, begun i...]
    ppermute x0 -> x16, starting transfers between devices: none -> 14.7 us  [the longest x1 3.03 us: on_line(): near1 = lax.ppermute(first, 'pair', NEAR)]
    broadcast_in_dim x3 -> x0, local copies, waits for them, and re-layouts: 8.8 us -> none  [the longest x2 8.72 us: on_device(): jnp.where(live_tiles[:, :, None], sorted_slots, jnp.zeros((), jnp.bfloat16))]
  transfers between devices with their start and end apart: 3 -> 16, of which waited for: 3 -> 10; matrix products, arithmetic and copies ran while one was open for 0% -> 0% of each run, Pallas kernels for 0% -> 11%
where the time goes in v1:
time: 110 us; the launch traced here: 109 us
  waiting for transfers between devices  68 us (62%)
  Pallas kernels  17.2 us (16%)
  starting transfers between devices  14.7 us (13%)
  local copies, waits for them, and re-layouts  7.52 us (7%)
  other arithmetic  1.4 us (1%)
    ppermute x1, waiting for transfers between devices, on_line(): from_across = lax.ppermute(other, ('ints', 'rep'), across)  14.8 us
    ppermute x1, waiting for transfers between devices, on_line(): out3 = lax.ppermute(mid3, 'pair', OUTWARD)  11.2 us
    ppermute x1, waiting for transfers between devices, on_line(): out2 = lax.ppermute(mid2, 'pair', OUTWARD)  11.2 us
    ppermute x1, waiting for transfers between devices, on_line(): near2 = lax.ppermute(second, 'pair', NEAR)  10.1 us
    ppermute x1, waiting for transfers between devices, on_line(): from_side = lax.ppermute(mine, ('ints', 'rep'), beside)  9.32 us
    unnamed x30, local copies, waits for them, and re-layouts  7.52 us
    pallas_call x2, Pallas kernels, add_positions(): pl.pallas_call(functools.partial(sum_kernel, rows, table, counts, begun i...  7.48 us
    pallas_call x1, Pallas kernels, pack(): pl.pallas_call(functools.partial(pack_kernel, rows, slots), grid_spec=plt...  5.55 us
  transfers between devices with their start and end apart: 16, of which 10 were waited for; matrix products, arithmetic and copies ran while one was open for 0% of the time, Pallas kernels for 11%

profile of v1, /device:TPU:0, one launch (start us, length us, event | category | flops | bytes accessed | tf_op | source)
XLA Modules:
  0.0 109.1 jit_solution(15944456576769933293)
XLA Ops:
  0.6 4.1 %own_half.1 = (bf16[2,64,2048]{2,1,0:T(8,128)(2,1)}, bf16[2,64,2048]{2,1,0:T(8,128)(2,1)}) custom-call(s32[2]{0:T(128)} %pad_add_fusion.where_ref, bf16[64,16384]{1,0:T(8,128)(2,1)} %x_ref.1), custom_call_target="tpu_custom_call" | custom-call | bytes 4194304 | tf_op jit(solution)/shard_map/own_half/pallas_call | solution.py:55
  4.8 3.0 %collective-permute-start.6 = (bf16[2,64,2048]{2,1,0:T(8,128)(2,1)}, bf16[2,64,2048]{2,1,0:T(8,128)(2,1)S(1)}, u32[]{:S(2)}, u32[]{:S(2)}) collective-permute-start(bf16[2,64,2048]{2,1,0:T(8,128)(2,1)} %get-tuple-element.16.refs_4_), channel_id=1, source_target_pairs={{0,4},{4,0},{8,12},{12,8},{1,5},{5,1},{9,13},{13,9},{2,6},{6,2},{1... | collective-permute-start | bytes 1572872 | tf_op jit(solution)/shard_map/ppermute | solution.py:211
  10.4 5.5 %pack.1 = (bf16[256,2048]{1,0:T(8,128)(2,1)S(1)}, bf16[256,2048]{1,0:T(8,128)(2,1)S(1)}, s32[16]{0:T(128)S(1)}, s32[16]{0:T(128)S(1)}) custom-call(s32[2]{0:T(128)S(1)} %copy-done.10, s32[16]{0:T(128)S(1)} %copy-done.11, s32[16]{0:T(128)S(1)} %copy-done.12, s32[32]{0:T(128)S(1)} %copy-done.13, bf16[512,4096]{1,0:T(8,128)(2,1)} %bitcast.3), custom_call_target="tpu_custom_call" | custom-call | flops 1073741824 | bytes 6291456 | tf_op jit(solution)/shard_map/pack/pallas_call | solution.py:124
  16.0 1.6 %collective-permute-start.1 = (bf16[256,2048]{1,0:T(8,128)(2,1)S(1)}, bf16[256,2048]{1,0:T(8,128)(2,1)S(1)}, u32[]{:S(2)}, u32[]{:S(2)}) collective-permute-start(bf16[256,2048]{1,0:T(8,128)(2,1)S(1)} %get-tuple-element.13.refs_0_), channel_id=1, source_target_pairs={{0,2},{1,3},{2,0},{3,1},{4,6},{5,7},{6,4},{7,5},{8,10},{9,11},{10,... | collective-permute-start | bytes 3145736 | tf_op jit(solution)/shard_map/ppermute | solution.py:218
  18.7 1.8 %collective-permute-done.6.refs_6_ = bf16[2,64,2048]{2,1,0:T(8,128)(2,1)S(1)} collective-permute-done((bf16[2,64,2048]{2,1,0:T(8,128)(2,1)}, bf16[2,64,2048]{2,1,0:T(8,128)(2,1)S(1)}, u32[]{:S(2)}, u32[]{:S(2)}) %collective-permute-start.6) | collective-permute-done | bytes 524320 | tf_op jit(solution)/shard_map/ppermute | solution.py:211
  21.1 10.1 %collective-permute-done.3.refs_7_ = bf16[2,64,2048]{2,1,0:T(8,128)(2,1)S(1)} collective-permute-done((bf16[2,64,2048]{2,1,0:T(8,128)(2,1)S(1)}, bf16[2,64,2048]{2,1,0:T(8,128)(2,1)S(1)}, u32[]{:S(2)}, u32[]{:S(2)}) %collective-permute-start.3) | collective-permute-done | bytes 524320 | tf_op jit(solution)/shard_map/ppermute | solution.py:213
  32.8 9.3 %collective-permute-done.1.refs_2_ = bf16[256,2048]{1,0:T(8,128)(2,1)S(1)} collective-permute-done((bf16[256,2048]{1,0:T(8,128)(2,1)S(1)}, bf16[256,2048]{1,0:T(8,128)(2,1)S(1)}, u32[]{:S(2)}, u32[]{:S(2)}) %collective-permute-start.1) | collective-permute-done | bytes 1048608 | tf_op jit(solution)/shard_map/ppermute | solution.py:218
  42.1 1.3 %collective-permute-start.10 = (bf16[2,64,2048]{2,1,0:T(8,128)(2,1)S(1)}, bf16[2,64,2048]{2,1,0:T(8,128)(2,1)S(1)}, u32[]{:S(2)}, u32[]{:S(2)}) collective-permute-start(bf16[2,64,2048]{2,1,0:T(8,128)(2,1)S(1)} %collective-permute-done.7.refs_8_), channel_id=1, source_target_pairs={{4,0},{8,12},{5,1},{9,13},{6,2},{10,14},{7,3},{11,15},{20,16},{24,... | collective-permute-start | bytes 1572872 | tf_op jit(solution)/shard_map/ppermute | solution.py:222
  43.4 1.3 %collective-permute-start.11 = (bf16[2,64,2048]{2,1,0:T(8,128)(2,1)S(1)}, bf16[2,64,2048]{2,1,0:T(8,128)(2,1)S(1)}, u32[]{:S(2)}, u32[]{:S(2)}) collective-permute-start(bf16[2,64,2048]{2,1,0:T(8,128)(2,1)S(1)} %collective-permute-done.8.refs_9_), channel_id=1, source_target_pairs={{4,0},{8,12},{5,1},{9,13},{6,2},{10,14},{7,3},{11,15},{20,16},{24,... | collective-permute-start | bytes 1572872 | tf_op jit(solution)/shard_map/ppermute | solution.py:224
  44.7 1.3 %collective-permute-start.12 = (bf16[2,64,2048]{2,1,0:T(8,128)(2,1)S(1)}, bf16[2,64,2048]{2,1,0:T(8,128)(2,1)S(1)}, u32[]{:S(2)}, u32[]{:S(2)}) collective-permute-start(bf16[2,64,2048]{2,1,0:T(8,128)(2,1)S(1)} %collective-permute-done.9.refs_10_), channel_id=1, source_target_pairs={{4,0},{8,12},{5,1},{9,13},{6,2},{10,14},{7,3},{11,15},{20,16},{24,... | collective-permute-start | bytes 1572872 | tf_op jit(solution)/shard_map/ppermute | solution.py:225
  46.0 1.3 %collective-permute-start.5 = (bf16[2,64,2048]{2,1,0:T(8,128)(2,1)S(1)}, bf16[2,64,2048]{2,1,0:T(8,128)(2,1)S(1)}, u32[]{:S(2)}, u32[]{:S(2)}) collective-permute-start(bf16[2,64,2048]{2,1,0:T(8,128)(2,1)S(1)} %collective-permute-done.4.refs_11_), channel_id=1, source_target_pairs={{4,0},{8,12},{5,1},{9,13},{6,2},{10,14},{7,3},{11,15},{20,16},{24,... | collective-permute-start | bytes 1572872 | tf_op jit(solution)/shard_map/ppermute | solution.py:226
  47.3 14.8 %collective-permute-done.2.refs_3_ = bf16[256,2048]{1,0:T(8,128)(2,1)S(1)} collective-permute-done((bf16[256,2048]{1,0:T(8,128)(2,1)S(1)}, bf16[256,2048]{1,0:T(8,128)(2,1)S(1)}, u32[]{:S(2)}, u32[]{:S(2)}) %collective-permute-start.2) | collective-permute-done | bytes 1048608 | tf_op jit(solution)/shard_map/ppermute | solution.py:219
  62.1 2.9 %collective-permute-done.10.refs_12_ = bf16[2,64,2048]{2,1,0:T(8,128)(2,1)S(1)} collective-permute-done((bf16[2,64,2048]{2,1,0:T(8,128)(2,1)S(1)}, bf16[2,64,2048]{2,1,0:T(8,128)(2,1)S(1)}, u32[]{:S(2)}, u32[]{:S(2)}) %collective-permute-start.10) | collective-permute-done | bytes 524320 | tf_op jit(solution)/shard_map/ppermute | solution.py:222
  65.0 11.2 %collective-permute-done.11.refs_13_ = bf16[2,64,2048]{2,1,0:T(8,128)(2,1)S(1)} collective-permute-done((bf16[2,64,2048]{2,1,0:T(8,128)(2,1)S(1)}, bf16[2,64,2048]{2,1,0:T(8,128)(2,1)S(1)}, u32[]{:S(2)}, u32[]{:S(2)}) %collective-permute-start.11) | collective-permute-done | bytes 524320 | tf_op jit(solution)/shard_map/ppermute | solution.py:224
  76.2 11.2 %collective-permute-done.12.refs_14_ = bf16[2,64,2048]{2,1,0:T(8,128)(2,1)S(1)} collective-permute-done((bf16[2,64,2048]{2,1,0:T(8,128)(2,1)S(1)}, bf16[2,64,2048]{2,1,0:T(8,128)(2,1)S(1)}, u32[]{:S(2)}, u32[]{:S(2)}) %collective-permute-start.12) | collective-permute-done | bytes 524320 | tf_op jit(solution)/shard_map/ppermute | solution.py:225
  87.5 6.3 %sum_most.1.refs_5_ = f32[128,128]{1,0:T(8,128)S(1)} custom-call(s32[2]{0:T(128)S(1)} %copy-done.10, s32[16]{0:T(128)S(1)} %get-tuple-element.11.rank_ref, s32[16]{0:T(128)S(1)} %get-tuple-element.12.irrep_ref, bf16[256,2048]{1,0:T(8,128)(2,1)} %copy-done, bf16[256,2048]{1,0:T(8,128)(2,1)} %copy-done.4, bf16[256,2048]{1,0:T(8,128)(2,1)} %copy-done.2, ...), custom_call_target="tpu_custom_call" | custom-call | flops 738197504 | bytes 9961472 | tf_op jit(solution)/shard_map/sum_most/pallas_call | solution.py:187
  93.8 3.2 %collective-permute-done.5.refs_4_ = bf16[2,64,2048]{2,1,0:T(8,128)(2,1)S(1)} collective-permute-done((bf16[2,64,2048]{2,1,0:T(8,128)(2,1)S(1)}, bf16[2,64,2048]{2,1,0:T(8,128)(2,1)S(1)}, u32[]{:S(2)}, u32[]{:S(2)}) %collective-permute-start.5) | collective-permute-done | bytes 524320 | tf_op jit(solution)/shard_map/ppermute | solution.py:226
  97.0 1.2 %copy-done.1 = bf16[256,2048]{1,0:T(8,128)(2,1)S(1)} copy-done((bf16[256,2048]{1,0:T(8,128)(2,1)S(1)}, bf16[256,2048]{1,0:T(8,128)(2,1)}, u32[]{:S(2)}) %copy-start.1) | copy-done | bytes 1048600
  98.2 1.2 %copy-done.3 = bf16[256,2048]{1,0:T(8,128)(2,1)S(1)} copy-done((bf16[256,2048]{1,0:T(8,128)(2,1)S(1)}, bf16[256,2048]{1,0:T(8,128)(2,1)}, u32[]{:S(2)}) %copy-start.3) | copy-done | bytes 1048600
  99.5 1.2 %copy-done.5 = bf16[256,2048]{1,0:T(8,128)(2,1)S(1)} copy-done((bf16[256,2048]{1,0:T(8,128)(2,1)S(1)}, bf16[256,2048]{1,0:T(8,128)(2,1)}, u32[]{:S(2)}) %copy-start.5) | copy-done | bytes 1048600
  100.7 1.2 %copy-done.7 = bf16[256,2048]{1,0:T(8,128)(2,1)S(1)} copy-done((bf16[256,2048]{1,0:T(8,128)(2,1)S(1)}, bf16[256,2048]{1,0:T(8,128)(2,1)}, u32[]{:S(2)}) %copy-start.7) | copy-done | bytes 1048600
  101.9 1.2 %sum_last.1 = f32[128,128]{1,0:T(8,128)S(1)} custom-call(s32[2]{0:T(128)S(1)} %copy-done.10, s32[16]{0:T(128)S(1)} %get-tuple-element.11.rank_ref, s32[16]{0:T(128)S(1)} %get-tuple-element.12.irrep_ref, bf16[256,2048]{1,0:T(8,128)(2,1)S(1)} %copy-done.1, bf16[256,2048]{1,0:T(8,128)(2,1)S(1)} %copy-done.5, bf16[256,2048]{1,0:T(8,128)(2,1)S(1)} %copy-done.3, ...), custom_call_target="tpu_custom_call" | custom-call | flops 67108864 | bytes 4718592 | tf_op jit(solution)/shard_map/sum_last/pallas_call | solution.py:187
  103.2 1.2 %collective-permute-done.13 = f32[32,128]{1,0:T(8,128)S(1)} collective-permute-done((f32[32,128]{1,0:T(8,128)S(1)}, f32[32,128]{1,0:T(8,128)S(1)}, u32[]{:S(2)}, u32[]{:S(2)}) %collective-permute-start.13) | collective-permute-done | bytes 16416 | tf_op jit(solution)/shard_map/ppermute | solution.py:253
  105.9 2.3 %collective-permute-done.14 = f32[32,128]{1,0:T(8,128)S(1)} collective-permute-done((f32[32,128]{1,0:T(8,128)S(1)}, f32[32,128]{1,0:T(8,128)S(1)}, u32[]{:S(2)}, u32[]{:S(2)}) %collective-permute-start.14) | collective-permute-done | bytes 16416 | tf_op jit(solution)/shard_map/ppermute | solution.py:254
  (49 shorter events, 9.0 us)
Async XLA Ops:
  4.8 12.8 %copy-start.9 = (bf16[2,64,2048]{2,1,0:T(8,128)(2,1)S(1)}, bf16[2,64,2048]{2,1,0:T(8,128)(2,1)}, u32[]{:S(2)}) copy-start(bf16[2,64,2048]{2,1,0:T(8,128)(2,1)} %get-tuple-element.15.refs_5_) | copy-start | bytes 1572868
  4.8 13.2 %copy-start.8 = (bf16[2,64,2048]{2,1,0:T(8,128)(2,1)S(1)}, bf16[2,64,2048]{2,1,0:T(8,128)(2,1)}, u32[]{:S(2)}) copy-start(bf16[2,64,2048]{2,1,0:T(8,128)(2,1)} %get-tuple-element.16.refs_4_) | copy-start | bytes 1572868
  4.8 15.7 %collective-permute-start.6 = (bf16[2,64,2048]{2,1,0:T(8,128)(2,1)}, bf16[2,64,2048]{2,1,0:T(8,128)(2,1)S(1)}, u32[]{:S(2)}, u32[]{:S(2)}) collective-permute-start(bf16[2,64,2048]{2,1,0:T(8,128)(2,1)} %get-tuple-element.16.refs_4_), channel_id=1, source_target_pairs={{0,4},{4,0},{8,12},{12,8},{1,5},{5,1},{9,13},{13,9},{2,6},{6,2},{1... | collective-permute-start | bytes 1572872 | tf_op jit(solution)/shard_map/ppermute | solution.py:211
  15.9 71.5 %copy-start = (bf16[256,2048]{1,0:T(8,128)(2,1)}, bf16[256,2048]{1,0:T(8,128)(2,1)S(1)}, u32[]{:S(2)}) copy-start(bf16[256,2048]{1,0:T(8,128)(2,1)S(1)} %get-tuple-element.13.refs_0_) | copy-start | bytes 3145732
  16.0 26.1 %collective-permute-start.1 = (bf16[256,2048]{1,0:T(8,128)(2,1)S(1)}, bf16[256,2048]{1,0:T(8,128)(2,1)S(1)}, u32[]{:S(2)}, u32[]{:S(2)}) collective-permute-start(bf16[256,2048]{1,0:T(8,128)(2,1)S(1)} %get-tuple-element.13.refs_0_), channel_id=1, source_target_pairs={{0,2},{1,3},{2,0},{3,1},{4,6},{5,7},{6,4},{7,5},{8,10},{9,11},{10,... | collective-permute-start | bytes 3145736 | tf_op jit(solution)/shard_map/ppermute | solution.py:218
  17.5 13.7 %collective-permute-start.3 = (bf16[2,64,2048]{2,1,0:T(8,128)(2,1)S(1)}, bf16[2,64,2048]{2,1,0:T(8,128)(2,1)S(1)}, u32[]{:S(2)}, u32[]{:S(2)}) collective-permute-start(bf16[2,64,2048]{2,1,0:T(8,128)(2,1)S(1)} %copy-done.9), channel_id=1, source_target_pairs={{0,4},{4,0},{8,12},{12,8},{1,5},{5,1},{9,13},{13,9},{2,6},{6,2},{1... | collective-permute-start | bytes 1572872 | tf_op jit(solution)/shard_map/ppermute | solution.py:213
  18.0 25.4 %collective-permute-start = (bf16[256,2048]{1,0:T(8,128)(2,1)S(1)}, bf16[256,2048]{1,0:T(8,128)(2,1)S(1)}, u32[]{:S(2)}, u32[]{:S(2)}) collective-permute-start(bf16[256,2048]{1,0:T(8,128)(2,1)S(1)} %get-tuple-element.14), channel_id=1, source_target_pairs={{0,1},{1,0},{2,3},{3,2},{4,5},{5,4},{6,7},{7,6},{8,9},{9,8},{10,11... | collective-permute-start | bytes 3145736 | tf_op jit(solution)/shard_map/ppermute | solution.py:217
  18.0 13.4 %collective-permute-start.7 = (bf16[2,64,2048]{2,1,0:T(8,128)(2,1)S(1)}, bf16[2,64,2048]{2,1,0:T(8,128)(2,1)S(1)}, u32[]{:S(2)}, u32[]{:S(2)}) collective-permute-start(bf16[2,64,2048]{2,1,0:T(8,128)(2,1)S(1)} %copy-done.8), channel_id=1, source_target_pairs={{4,8},{8,4},{5,9},{9,5},{6,10},{10,6},{7,11},{11,7},{20,24},{24,20... | collective-permute-start | bytes 1572872 | tf_op jit(solution)/shard_map/ppermute | solution.py:212
  20.4 11.6 %collective-permute-start.8 = (bf16[2,64,2048]{2,1,0:T(8,128)(2,1)S(1)}, bf16[2,64,2048]{2,1,0:T(8,128)(2,1)S(1)}, u32[]{:S(2)}, u32[]{:S(2)}) collective-permute-start(bf16[2,64,2048]{2,1,0:T(8,128)(2,1)S(1)} %copy-done.9), channel_id=1, source_target_pairs={{4,8},{8,4},{5,9},{9,5},{6,10},{10,6},{7,11},{11,7},{20,24},{24,20... | collective-permute-start | bytes 1572872 | tf_op jit(solution)/shard_map/ppermute | solution.py:214
  31.2 30.9 %collective-permute-start.2 = (bf16[256,2048]{1,0:T(8,128)(2,1)S(1)}, bf16[256,2048]{1,0:T(8,128)(2,1)S(1)}, u32[]{:S(2)}, u32[]{:S(2)}) collective-permute-start(bf16[256,2048]{1,0:T(8,128)(2,1)S(1)} %get-tuple-element.14), channel_id=1, source_target_pairs={{0,3},{1,2},{2,1},{3,0},{4,7},{5,6},{6,5},{7,4},{8,11},{9,10},{10,... | collective-permute-start | bytes 3145736 | tf_op jit(solution)/shard_map/ppermute | solution.py:219
  31.4 13.3 %collective-permute-start.9 = (bf16[2,64,2048]{2,1,0:T(8,128)(2,1)S(1)}, bf16[2,64,2048]{2,1,0:T(8,128)(2,1)S(1)}, u32[]{:S(2)}, u32[]{:S(2)}) collective-permute-start(bf16[2,64,2048]{2,1,0:T(8,128)(2,1)S(1)} %collective-permute-done.6.refs_6_), channel_id=1, source_target_pairs={{4,8},{8,4},{5,9},{9,5},{6,10},{10,6},{7,11},{11,7},{20,24},{24,20... | collective-permute-start | bytes 1572872 | tf_op jit(solution)/shard_map/ppermute | solution.py:221
  32.1 13.9 %collective-permute-start.4 = (bf16[2,64,2048]{2,1,0:T(8,128)(2,1)S(1)}, bf16[2,64,2048]{2,1,0:T(8,128)(2,1)S(1)}, u32[]{:S(2)}, u32[]{:S(2)}) collective-permute-start(bf16[2,64,2048]{2,1,0:T(8,128)(2,1)S(1)} %collective-permute-done.3.refs_7_), channel_id=1, source_target_pairs={{4,8},{8,4},{5,9},{9,5},{6,10},{10,6},{7,11},{11,7},{20,24},{24,20... | collective-permute-start | bytes 1572872 | tf_op jit(solution)/shard_map/ppermute | solution.py:223
  42.1 45.4 %copy-start.2 = (bf16[256,2048]{1,0:T(8,128)(2,1)}, bf16[256,2048]{1,0:T(8,128)(2,1)S(1)}, u32[]{:S(2)}) copy-start(bf16[256,2048]{1,0:T(8,128)(2,1)S(1)} %collective-permute-done.1.refs_2_) | copy-start | bytes 3145732
  42.1 22.9 %collective-permute-start.10 = (bf16[2,64,2048]{2,1,0:T(8,128)(2,1)S(1)}, bf16[2,64,2048]{2,1,0:T(8,128)(2,1)S(1)}, u32[]{:S(2)}, u32[]{:S(2)}) collective-permute-start(bf16[2,64,2048]{2,1,0:T(8,128)(2,1)S(1)} %collective-permute-done.7.refs_8_), channel_id=1, source_target_pairs={{4,0},{8,12},{5,1},{9,13},{6,2},{10,14},{7,3},{11,15},{20,16},{24,... | collective-permute-start | bytes 1572872 | tf_op jit(solution)/shard_map/ppermute | solution.py:222
  43.4 44.1 %copy-start.4 = (bf16[256,2048]{1,0:T(8,128)(2,1)}, bf16[256,2048]{1,0:T(8,128)(2,1)S(1)}, u32[]{:S(2)}) copy-start(bf16[256,2048]{1,0:T(8,128)(2,1)S(1)} %collective-permute-done.refs_1_) | copy-start | bytes 3145732
  43.4 32.8 %collective-permute-start.11 = (bf16[2,64,2048]{2,1,0:T(8,128)(2,1)S(1)}, bf16[2,64,2048]{2,1,0:T(8,128)(2,1)S(1)}, u32[]{:S(2)}, u32[]{:S(2)}) collective-permute-start(bf16[2,64,2048]{2,1,0:T(8,128)(2,1)S(1)} %collective-permute-done.8.refs_9_), channel_id=1, source_target_pairs={{4,0},{8,12},{5,1},{9,13},{6,2},{10,14},{7,3},{11,15},{20,16},{24,... | collective-permute-start | bytes 1572872 | tf_op jit(solution)/shard_map/ppermute | solution.py:224
  44.7 42.7 %collective-permute-start.12 = (bf16[2,64,2048]{2,1,0:T(8,128)(2,1)S(1)}, bf16[2,64,2048]{2,1,0:T(8,128)(2,1)S(1)}, u32[]{:S(2)}, u32[]{:S(2)}) collective-permute-start(bf16[2,64,2048]{2,1,0:T(8,128)(2,1)S(1)} %collective-permute-done.9.refs_10_), channel_id=1, source_target_pairs={{4,0},{8,12},{5,1},{9,13},{6,2},{10,14},{7,3},{11,15},{20,16},{24,... | collective-permute-start | bytes 1572872 | tf_op jit(solution)/shard_map/ppermute | solution.py:225
  46.0 51.0 %collective-permute-start.5 = (bf16[2,64,2048]{2,1,0:T(8,128)(2,1)S(1)}, bf16[2,64,2048]{2,1,0:T(8,128)(2,1)S(1)}, u32[]{:S(2)}, u32[]{:S(2)}) collective-permute-start(bf16[2,64,2048]{2,1,0:T(8,128)(2,1)S(1)} %collective-permute-done.4.refs_11_), channel_id=1, source_target_pairs={{4,0},{8,12},{5,1},{9,13},{6,2},{10,14},{7,3},{11,15},{20,16},{24,... | collective-permute-start | bytes 1572872 | tf_op jit(solution)/shard_map/ppermute | solution.py:226
  62.1 25.4 %copy-start.6 = (bf16[256,2048]{1,0:T(8,128)(2,1)}, bf16[256,2048]{1,0:T(8,128)(2,1)S(1)}, u32[]{:S(2)}) copy-start(bf16[256,2048]{1,0:T(8,128)(2,1)S(1)} %collective-permute-done.2.refs_3_) | copy-start | bytes 3145732
  97.0 1.2 %copy-start.1 = (bf16[256,2048]{1,0:T(8,128)(2,1)S(1)}, bf16[256,2048]{1,0:T(8,128)(2,1)}, u32[]{:S(2)}) copy-start(bf16[256,2048]{1,0:T(8,128)(2,1)} %copy-done) | copy-start | bytes 3145732
  101.9 4.0 %copy-start.14 = (s32[32]{0:T(128)S(1)}, s32[32]{0:T(128)}, u32[]{:S(2)}) copy-start(s32[32]{0:T(128)} %pair_irrep_ref.1) | copy-start | bytes 388
  103.2 1.2 %collective-permute-start.13 = (f32[32,128]{1,0:T(8,128)S(1)}, f32[32,128]{1,0:T(8,128)S(1)}, u32[]{:S(2)}, u32[]{:S(2)}) collective-permute-start(f32[32,128]{1,0:T(8,128)S(1)} %slice.33), channel_id=1, source_target_pairs={{0,1},{1,0},{2,3},{3,2},{4,5},{5,4},{6,7},{7,6},{8,9},{9,8},{10,11... | collective-permute-start | bytes 49160 | tf_op jit(solution)/shard_map/ppermute | solution.py:253
  104.4 3.9 %collective-permute-start.14 = (f32[32,128]{1,0:T(8,128)S(1)}, f32[32,128]{1,0:T(8,128)S(1)}, u32[]{:S(2)}, u32[]{:S(2)}) collective-permute-start(f32[32,128]{1,0:T(8,128)S(1)} %get-tuple-element.19), channel_id=1, source_target_pairs={{0,2},{1,3},{2,0},{3,1},{4,6},{5,7},{6,4},{7,5},{8,10},{9,11},{10,... | collective-permute-start | bytes 49160 | tf_op jit(solution)/shard_map/ppermute | solution.py:254
  104.9 3.3 %collective-permute-start.15 = (f32[32,128]{1,0:T(8,128)S(1)}, f32[32,128]{1,0:T(8,128)S(1)}, u32[]{:S(2)}, u32[]{:S(2)}) collective-permute-start(f32[32,128]{1,0:T(8,128)S(1)} %get-tuple-element.18), channel_id=1, source_target_pairs={{0,3},{1,2},{2,1},{3,0},{4,7},{5,6},{6,5},{7,4},{8,11},{9,10},{10,... | collective-permute-start | bytes 49160 | tf_op jit(solution)/shard_map/ppermute | solution.py:254
  (7 other events, 6.3 us)

commit v2 on v0

--- a/solution.py
+++ b/solution.py
@@ -1,10 +1,22 @@
+import functools
+
 import jax
 import jax.numpy as jnp
 from jax import lax
+from jax.experimental import pallas as pl
+from jax.experimental.pallas import tpu as pltpu
 from jax.sharding import PartitionSpec as P
 
-
-def on_device(amplitudes, integrals, pair_irrep, slot_irrep, owner_slot_map):
+VMEM_LIMIT = 12 * 1024 * 1024
+PREPARE_VMEM = 50 * 1024 * 1024
+NT = (((1,), (1,)), ((), ()))
+SWAP = [(0, 1), (1, 0)]
+NEAR = [(0, 1), (1, 0), (2, 3), (3, 2)]
+MIDDLE = [(1, 2), (2, 1)]
+OUTWARD = [(1, 0), (2, 3)]
+
+
+def plain(amplitudes, integrals, pair_irrep, slot_irrep, owner_slot_map):
     row_count, slot_count, tile_size = amplitudes.shape
     slot_position_index = jnp.arange(slot_count, dtype=jnp.int32)
     picked = owner_slot_map[:, None] == slot_position_index[None, :]
@@ -17,10 +29,218 @@
     partial_sums = lax.dot_general(
         columns,
         lax.all_gather(integrals, "ints", axis=0, tiled=True),
-        (((1,), (1,)), ((), ())),
+        NT,
         preferred_element_type=jnp.float32,
     )
     return lax.psum_scatter(partial_sums, "pair", scatter_dimension=0, tiled=True)
+
+
+def prepare_kernel(rows, slots, scalar_ref, x_ref, integrals_ref, other_ref, mine_ref, first_ref, second_ref, table_ref, held_ref, pick_ref, copied, loaded):
+    steps, _, width = held_ref.shape
+    half = first_ref.shape[2]
+    core = scalar_ref[1]
+    moves, loads = [], []
+    for p in range(2 * first_ref.shape[0]):
+        chunk_ref = first_ref if p < first_ref.shape[0] else second_ref
+        start = pl.multiple_of((2 * p + core) * half, half)
+        source = integrals_ref.at[:, pl.ds(start, half)]
+        moves.append(pltpu.make_async_copy(source, chunk_ref.at[p % first_ref.shape[0]], copied.at[p]))
+    for i in range(steps):
+        half_here = core if i < steps // 2 else 1 - core
+        start = pl.multiple_of(half_here * half + i % (steps // 2) * width, width)
+        loads.append(pltpu.make_async_copy(x_ref.at[:, pl.ds(start, width)], held_ref.at[i], loaded.at[i]))
+    for move in moves + loads:
+        move.start()
+
+    groups, picked, per_group = pick_ref.shape
+    group = per_group // slots
+    lane = lax.broadcasted_iota(jnp.int32, (1, per_group), 1)
+    slot_lane, row_lane = lane % slots, lane // slots
+    counts = [jnp.int32(0), jnp.int32(0)]
+    lane_rank = jnp.zeros_like(lane)
+    lane_irrep = jnp.zeros_like(lane)
+    for q in range(slots):
+        slot = scalar_ref[2 + slots + q]
+        irrep = scalar_ref[2 + slot]
+        odd = irrep == 1
+        rank = jnp.where(odd, counts[1], counts[0])
+        counts = [jnp.where(odd, counts[0], counts[0] + 1), jnp.where(odd, counts[1] + 1, counts[1])]
+        table_ref[q] = rank
+        table_ref[slots + q] = irrep
+        here = slot_lane == slot
+        lane_rank = jnp.where(here, rank, lane_rank)
+        lane_irrep = jnp.where(here, irrep, lane_irrep)
+    table_ref[2 * slots] = scalar_ref[0]
+    row = lax.broadcasted_iota(jnp.int32, (picked, per_group), 0)
+    for g in range(groups):
+        row_irrep = jnp.zeros_like(lane)
+        for o in range(group):
+            row_irrep = jnp.where(row_lane == o, scalar_ref[2 + 2 * slots + g * group + o], row_irrep)
+        target = jnp.where(lane_irrep == row_irrep, lane_rank * group + row_lane, -1)
+        pick_ref[g] = jnp.where(row == target, 1.0, 0.0).astype(pick_ref.dtype)
+
+    for i in range(steps):
+        loads[i].wait()
+        into = mine_ref if i < steps // 2 else other_ref
+        at = i % (steps // 2) * width
+        for g in range(groups):
+            source = held_ref[i, g * per_group : (g + 1) * per_group]
+            packed = jnp.dot(pick_ref[g], source, preferred_element_type=jnp.float32).astype(held_ref.dtype)
+            for j in range(picked // group):
+                to = j * rows + g * group
+                into[to : to + group, at : at + width] = packed[j * group : (j + 1) * group]
+    for move in moves:
+        move.wait()
+
+
+def prepare(scalars, amplitudes, integrals, steps=8):
+    rows, slots, tile = amplitudes.shape
+    live, half = slots // 2, tile // 2
+    ab, columns = integrals.shape
+    held = columns // tile
+    packed = jax.ShapeDtypeStruct((live * rows, half), amplitudes.dtype)
+    chunk = jax.ShapeDtypeStruct((held // 2, ab, half), integrals.dtype)
+    hbm = pl.BlockSpec(memory_space=pltpu.HBM)
+    vmem = pl.BlockSpec(memory_space=pltpu.VMEM)
+    smem = pl.BlockSpec(memory_space=pltpu.SMEM)
+    return pl.pallas_call(
+        functools.partial(prepare_kernel, rows, slots),
+        in_specs=[smem, hbm, hbm],
+        out_specs=[vmem, vmem, vmem, vmem, smem],
+        out_shape=[packed, packed, chunk, chunk, jax.ShapeDtypeStruct((2 * slots + 1,), jnp.int32)],
+        scratch_shapes=[
+            pltpu.VMEM((steps, rows * slots, tile // steps), amplitudes.dtype),
+            pltpu.VMEM((rows // 16, live * 16, 16 * slots), amplitudes.dtype),
+            pltpu.SemaphoreType.DMA((held,)),
+            pltpu.SemaphoreType.DMA((steps,)),
+        ],
+        compiler_params=pltpu.CompilerParams(vmem_limit_bytes=PREPARE_VMEM),
+        cost_estimate=pl.CostEstimate(
+            flops=2 * live * rows * rows * slots * tile, bytes_accessed=3 * rows * slots * tile, transcendentals=0
+        ),
+        name="prepare",
+    )(scalars, amplitudes.reshape(rows * slots, tile), integrals)
+
+
+def sum_kernel(rows, slots, held, work, table, begun, ends, scalar_ref, *refs):
+    tiles, refs = refs[:held], refs[held:]
+    count = len(table)
+    chunks, refs = refs[:count], refs[count:]
+    total_ref = refs[-1]
+    total_ref[...] = refs[0][...] if begun else jnp.zeros_like(total_ref)
+    place = scalar_ref[2 * slots]
+    for (low, high), used in work:
+        for c in used:
+            for i in range(chunks[c].shape[0]):
+                position = jnp.int32(table[c][0][i])
+                for z in range(1, len(table[c])):
+                    position = jnp.where(place == z, table[c][z][i], position)
+
+                @pl.when(position >= 0)
+                def _():
+                    at = jnp.maximum(position, 0)
+                    start = pl.multiple_of(scalar_ref[at] * rows, rows)
+                    here = jnp.concatenate([t[pl.ds(start, rows), :] for t in tiles[low:high]], axis=0)
+                    term = lax.dot_general(here, chunks[c][i], NT, preferred_element_type=jnp.float32)
+                    total_ref[scalar_ref[slots + at], low * rows : high * rows] += term
+
+    if ends:
+        for t, out_ref in enumerate(refs[-5:-1]):
+            at = slice(t * rows, (t + 1) * rows)
+            out_ref[...] = jnp.concatenate([total_ref[0, at], total_ref[1, at]], axis=1)
+
+
+def add_positions(scalars, tiles, chunks, table, work, begun=None, ends=False, name="sum"):
+    slots = scalars.shape[0] // 2
+    live = slots // 2
+    rows = tiles[0].shape[0] // live
+    ab, half = chunks[0].shape[1:]
+    vmem = pl.BlockSpec(memory_space=pltpu.VMEM)
+    smem = pl.BlockSpec(memory_space=pltpu.SMEM)
+    more = [] if begun is None else [begun]
+    flops = sum(2 * rows * (high - low) * ab * half * chunks[c].shape[0] for (low, high), used in work for c in used)
+    total = (2, 4 * rows, ab)
+    return pl.pallas_call(
+        functools.partial(sum_kernel, rows, slots, len(tiles), work, table, begun is not None, ends),
+        in_specs=[smem] + [vmem] * (len(tiles) + len(chunks) + len(more)),
+        out_specs=[vmem] * 4 if ends else vmem,
+        out_shape=[jax.ShapeDtypeStruct((rows, 2 * ab), jnp.float32)] * 4 if ends else jax.ShapeDtypeStruct(total, jnp.float32),
+        scratch_shapes=[pltpu.VMEM(total, jnp.float32)] if ends else [],
+        compiler_params=pltpu.CompilerParams(vmem_limit_bytes=VMEM_LIMIT),
+        name=name,
+    )(scalars, *tiles, *chunks, *more)
+
+
+def after(array, *earlier):
+    return lax.optimization_barrier((array, *earlier))[0] if earlier else array
+
+
+def on_line(amplitudes, integrals, pair_irrep, slot_irrep, owner_slot_map):
+    rows, slots, tile = amplitudes.shape
+    place, side, core = lax.axis_index("pair"), lax.axis_index("ints"), lax.axis_index("rep")
+    scalars = jnp.concatenate([jnp.stack([place, core]).astype(jnp.int32), slot_irrep, owner_slot_map, pair_irrep])
+    across = [(i, 3 - i) for i in range(4)]
+    beside = [(i, i ^ 2) for i in range(4)]
+
+    other, mine, first, second, scalars = prepare(scalars, amplitudes, integrals)
+    held = slots // 4
+    per = held // 2
+    none = (-1,) * per
+
+    def held_at(places, b):
+        return tuple(none if z is None else tuple(range(z * held + b * per, z * held + b * per + per)) for z in places)
+
+    home, near = (0, 1, 2, 3), (1, 0, 3, 2)
+    middle, beyond = (None, 2, 1, None), (None, 3, 0, None)
+    outer, outermost = (2, None, None, 1), (3, None, None, 0)
+    chunks = {"first": (first, held_at(home, 0)), "second": (second, held_at(home, 1))}
+    tiles = [mine, lax.ppermute(other, "rep", SWAP)]
+
+    def add(name, sums, *step, ends=False):
+        names = sorted({name for *_, used in step for name in used.split()})
+        return add_positions(
+            scalars,
+            tiles[: max(high for _, high, _ in step)],
+            tuple(chunks[name][0] for name in names),
+            tuple(chunks[name][1] for name in names),
+            tuple(((low, high), tuple(names.index(name) for name in used.split())) for low, high, used in step),
+            begun=sums,
+            ends=ends,
+            name=name,
+        )
+
+    def send(name, source, pairs, positions, *earlier):
+        chunks[name] = (lax.ppermute(after(chunks[source][0], *earlier), "pair", pairs), positions)
+
+    send("near1", "first", NEAR, held_at(near, 0))
+    send("mid1", "first", MIDDLE, held_at(middle, 0))
+    tiles.append(lax.ppermute(mine, ("ints", "rep"), beside))
+    send("mid2", "second", MIDDLE, held_at(middle, 1))
+    sums = add("sum_0", None, (0, 2, "first second"))
+    send("near2", "second", NEAR, held_at(near, 1), sums)
+    send("out1", "mid1", OUTWARD, held_at(outer, 0))
+    send("mid3", "near1", MIDDLE, held_at(beyond, 0))
+    sums = add("sum_1", sums, (0, 2, "near1 mid1"))
+    send("out2", "mid2", OUTWARD, held_at(outer, 1), sums)
+    send("mid4", "near2", MIDDLE, held_at(beyond, 1), sums)
+    sums = add("sum_2", sums, (0, 2, "near2 mid2"))
+    sums = add("sum_3", sums, (2, 3, "first second near1 near2 mid1 mid2"))
+    tiles.append(lax.ppermute(after(other, sums), ("ints", "rep"), across))
+    send("out3", "mid3", OUTWARD, held_at(outermost, 0), sums)
+    sums = add("sum_4", sums, (0, 3, "mid3 out1"))
+    send("out4", "mid4", OUTWARD, held_at(outermost, 1), sums)
+    sums = add("sum_5", sums, (0, 3, "mid4 out2"))
+    sums = add("sum_6", sums, (3, 4, "first second near1 near2 mid1 mid2 mid3 mid4 out1 out2"))
+    sums = add("sum_7", sums, (0, 4, "out3"))
+    sums = add("sum_8", sums, (0, 4, "out4"), ends=True)
+
+    own = sums[0] + lax.ppermute(sums[1], "rep", SWAP)
+    theirs = lax.ppermute(sums[2], ("ints", "rep"), beside) + lax.ppermute(sums[3], ("ints", "rep"), across)
+    ab = integrals.shape[0]
+    odd = (pair_irrep == 1)[:, None]
+    own = jnp.where(odd, own[:, ab:], own[:, :ab])
+    theirs = jnp.where(odd, theirs[:, ab:], theirs[:, :ab])
+    return jnp.where(side == 0, jnp.concatenate([own, theirs], axis=1), jnp.concatenate([theirs, own], axis=1))
 
 
 def solution(mesh):
@@ -31,8 +251,9 @@
         P("groups"),
         P("groups"),
     )
+    line = mesh.shape["pair"] == 4 and mesh.shape["ints"] == 2 and mesh.shape["rep"] == 2
     return jax.shard_map(
-        on_device,
+        on_line if line else plain,
         mesh=mesh,
         in_specs=placed,
         out_specs=P(("groups", "pair", "ints", "rep"), None),

time: 179 us -> 87.8 us (0.49)
  waiting for transfers between devices: 112 us -> 49.7 us
  local copies, waits for them, and re-layouts: 33.9 us -> 0.77 us
  Pallas kernels: 0 us -> 16.9 us
  between operations: 13.4 us -> 0.23 us
  starting transfers between devices: 6.36 us -> 19.2 us
  other arithmetic: 7.7 us -> 0.79 us
  matrix products: 5.33 us -> 0 us
    all_gather x1 -> x0, waiting for transfers between devices: 59.8 us -> none  [on_device(): lax.all_gather(integrals, 'ints', axis=0, tiled=True)]
    ppermute x0 -> x16, waiting for transfers between devices: none -> 49.7 us  [the longest x10 43.1 us: send(): lax.ppermute(after(chunks[source][0], *earlier), 'pair', pairs)]
    all_to_all x1 -> x0, waiting for transfers between devices: 32.8 us -> none  [on_device(): lax.all_to_all(flattened, 'pair', split_axis=1, concat_axis=0, tiled=True)]
    gather x2 -> x0, local copies, waits for them, and re-layouts: 20.7 us -> none  [on_device(): sorted_slots = jnp.take(amplitudes, owner_slot_map, axis=1)]
    ppermute x0 -> x16, starting transfers between devices: none -> 19.2 us  [the longest x10 14.1 us: send(): lax.ppermute(after(chunks[source][0], *earlier), 'pair', pairs)]
    reduce_scatter x1 -> x0, waiting for transfers between devices: 18.3 us -> none  [on_device(): lax.psum_scatter(partial_sums, 'pair', scatter_dimension=0, tiled=True)]
    pallas_call x0 -> x10, Pallas kernels: none -> 16.9 us  [the longest x9 12.7 us: add_positions(): pl.pallas_call(functools.partial(sum_kernel, rows, slots, len(tiles), wor...]
    broadcast_in_dim x3 -> x0, local copies, waits for them, and re-layouts: 8.8 us -> none  [the longest x2 8.72 us: on_device(): jnp.where(live_tiles[:, :, None], sorted_slots, jnp.zeros((), jnp.bfloat16))]
  transfers between devices with their start and end apart: 3 -> 16, of which waited for: 3 -> 9; matrix products, arithmetic and copies ran while one was open for 0% -> 0% of each run, Pallas kernels for 0% -> 13%
where the time goes in v2:
time: 87.8 us; the launch traced here: 87.6 us
  waiting for transfers between devices  49.7 us (57%)
  starting transfers between devices  19.2 us (22%)
  Pallas kernels  16.9 us (19%)
    ppermute x10, waiting for transfers between devices, send(): lax.ppermute(after(chunks[source][0], *earlier), 'pair', pairs)  43.1 us
    ppermute x10, starting transfers between devices, send(): lax.ppermute(after(chunks[source][0], *earlier), 'pair', pairs)  14.1 us
    pallas_call x9, Pallas kernels, add_positions(): pl.pallas_call(functools.partial(sum_kernel, rows, slots, len(tiles), wor...  12.7 us
    ppermute x1, waiting for transfers between devices, on_line(): tiles.append(lax.ppermute(after(other, sums), ('ints', 'rep'), across))  4.47 us
    pallas_call x1, Pallas kernels, prepare(): pl.pallas_call(functools.partial(prepare_kernel, rows, slots), in_specs=[...  4.18 us
    ppermute x1, starting transfers between devices, on_line(): tiles.append(lax.ppermute(mine, ('ints', 'rep'), beside))  2.56 us
    ppermute x1, waiting for transfers between devices, on_line(): lax.ppermute(sums[2], ('ints', 'rep'), beside)  2.04 us
  transfers between devices with their start and end apart: 16, of which 9 were waited for; matrix products, arithmetic and copies ran while one was open for 0% of the time, Pallas kernels for 13%

profile of v2, /device:TPU:0, one launch (start us, length us, event | category | flops | bytes accessed | tf_op | source)
XLA Modules:
  0.0 87.6 jit_solution(5650363783286163518)
XLA Ops:
  0.8 4.2 %prepare.1 = (bf16[256,2048]{1,0:T(8,128)(2,1)S(1)}, bf16[256,2048]{1,0:T(8,128)(2,1)S(1)}, bf16[2,64,2048]{2,1,0:T(8,128)(2,1)S(1)}, bf16[2,64,2048]{2,1,0:T(8,128)(2,1)S(1)}, s32[33]{0:T(128)S(1)}) custom-call(s32[66]{0:T(128)S(1)} %concatenate.9.scalar_ref, bf16[512,4096]{1,0:T(8,128)(2,1)} %bitcast.3, bf16[64,16384]{1,0:T(8,128)(2,1)} %integrals_ref.1), custom_call_target="tpu_custom_call" | custom-call | flops 1073741824 | bytes 6291456 | tf_op jit(solution)/shard_map/prepare/pallas_call | solution.py:106
  5.5 2.6 %collective-permute-start.1 = (bf16[256,2048]{1,0:T(8,128)(2,1)S(1)}, bf16[256,2048]{1,0:T(8,128)(2,1)S(1)}, u32[]{:S(2)}, u32[]{:S(2)}) collective-permute-start(bf16[256,2048]{1,0:T(8,128)(2,1)S(1)} %get-tuple-element.21.refs_0_), channel_id=1, source_target_pairs={{0,2},{1,3},{2,0},{3,1},{4,6},{5,7},{6,4},{7,5},{8,10},{9,11},{10,... | collective-permute-start | bytes 3145736 | tf_op jit(solution)/shard_map/ppermute | solution.py:217
  8.7 4.4 %collective-permute-start.4 = (bf16[2,64,2048]{2,1,0:T(8,128)(2,1)S(1)}, bf16[2,64,2048]{2,1,0:T(8,128)(2,1)S(1)}, u32[]{:S(2)}, u32[]{:S(2)}) collective-permute-start(bf16[2,64,2048]{2,1,0:T(8,128)(2,1)S(1)} %get-tuple-element.23.refs_2_.refs_3_.refs_4_), channel_id=1, source_target_pairs={{0,4},{4,0},{8,12},{12,8},{1,5},{5,1},{9,13},{13,9},{2,6},{6,2},{1... | collective-permute-start | bytes 1572872 | tf_op jit(solution)/shard_map/ppermute | solution.py:213
  13.9 1.4 %sum_0.1.refs_4_ = f32[2,128,64]{2,1,0:T(8,128)S(1)} custom-call(s32[33]{0:T(128)S(1)} %get-tuple-element.20.scalar_ref, bf16[256,2048]{1,0:T(8,128)(2,1)S(1)} %get-tuple-element.21.refs_0_, bf16[256,2048]{1,0:T(8,128)(2,1)S(1)} %collective-permute-done.refs_1_, bf16[2,64,2048]{2,1,0:T(8,128)(2,1)S(1)} %get-tuple-element.23.refs_2_.refs_3_.refs_4_, ...), custom_call_target="tpu_custom_call" | custom-call | tf_op jit(solution)/shard_map/sum_0/pallas_call | solution.py:163
  15.3 1.8 %collective-permute-start.5 = (bf16[2,64,2048]{2,1,0:T(8,128)(2,1)S(1)}, bf16[2,64,2048]{2,1,0:T(8,128)(2,1)S(1)}, u32[]{:S(2)}, u32[]{:S(2)}) collective-permute-start(bf16[2,64,2048]{2,1,0:T(8,128)(2,1)S(1)} %get-tuple-element.25.refs_3_.refs_8_.refs_13_), channel_id=1, source_target_pairs={{0,4},{4,0},{8,12},{12,8},{1,5},{5,1},{9,13},{13,9},{2,6},{6,2},{1... | collective-permute-start | bytes 1572872 | tf_op jit(solution)/shard_map/ppermute | solution.py:213
  17.0 8.9 %collective-permute-done.4.refs_3_.refs_6_.refs_9_ = bf16[2,64,2048]{2,1,0:T(8,128)(2,1)S(1)} collective-permute-done((bf16[2,64,2048]{2,1,0:T(8,128)(2,1)S(1)}, bf16[2,64,2048]{2,1,0:T(8,128)(2,1)S(1)}, u32[]{:S(2)}, u32[]{:S(2)}) %collective-permute-start.4) | collective-permute-done | bytes 524320 | tf_op jit(solution)/shard_map/ppermute | solution.py:213
  26.6 1.3 %collective-permute-start.9 = (bf16[2,64,2048]{2,1,0:T(8,128)(2,1)S(1)}, bf16[2,64,2048]{2,1,0:T(8,128)(2,1)S(1)}, u32[]{:S(2)}, u32[]{:S(2)}) collective-permute-start(bf16[2,64,2048]{2,1,0:T(8,128)(2,1)S(1)} %collective-permute-done.2.refs_2_.refs_4_.refs_5_), channel_id=1, source_target_pairs={{4,0},{8,12},{5,1},{9,13},{6,2},{10,14},{7,3},{11,15},{20,16},{24,... | collective-permute-start | bytes 1572872 | tf_op jit(solution)/shard_map/ppermute | solution.py:213
  28.9 8.2 %collective-permute-done.5.refs_3_.refs_7_.refs_10_ = bf16[2,64,2048]{2,1,0:T(8,128)(2,1)S(1)} collective-permute-done((bf16[2,64,2048]{2,1,0:T(8,128)(2,1)S(1)}, bf16[2,64,2048]{2,1,0:T(8,128)(2,1)S(1)}, u32[]{:S(2)}, u32[]{:S(2)}) %collective-permute-start.5) | collective-permute-done | bytes 524320 | tf_op jit(solution)/shard_map/ppermute | solution.py:213
  38.1 2.0 %sum_3.1.refs_5_ = f32[2,128,64]{2,1,0:T(8,128)S(1)} custom-call(s32[33]{0:T(128)S(1)} %get-tuple-element.20.scalar_ref, bf16[256,2048]{1,0:T(8,128)(2,1)S(1)} %get-tuple-element.21.refs_0_, bf16[256,2048]{1,0:T(8,128)(2,1)S(1)} %collective-permute-done.refs_1_, bf16[256,2048]{1,0:T(8,128)(2,1)S(1)} %collective-permute-done.1.refs_2_, ...), custom_call_target="tpu_custom_call" | custom-call | tf_op jit(solution)/shard_map/sum_3/pallas_call | solution.py:163
  41.0 1.3 %collective-permute-start.12 = (bf16[2,64,2048]{2,1,0:T(8,128)(2,1)S(1)}, bf16[2,64,2048]{2,1,0:T(8,128)(2,1)S(1)}, u32[]{:S(2)}, u32[]{:S(2)}) collective-permute-start(bf16[2,64,2048]{2,1,0:T(8,128)(2,1)S(1)} %collective-permute-done.3.refs_2_.refs_5_.refs_6_), channel_id=1, source_target_pairs={{4,0},{8,12},{5,1},{9,13},{6,2},{10,14},{7,3},{11,15},{20,16},{24,... | collective-permute-start | bytes 1572872 | tf_op jit(solution)/shard_map/ppermute | solution.py:213
  42.3 1.3 %collective-permute-start.11 = (bf16[2,64,2048]{2,1,0:T(8,128)(2,1)S(1)}, bf16[2,64,2048]{2,1,0:T(8,128)(2,1)S(1)}, u32[]{:S(2)}, u32[]{:S(2)}) collective-permute-start(bf16[2,64,2048]{2,1,0:T(8,128)(2,1)S(1)} %collective-permute-done.8.refs_3_.refs_7_), channel_id=1, source_target_pairs={{4,0},{8,12},{5,1},{9,13},{6,2},{10,14},{7,3},{11,15},{20,16},{24,... | collective-permute-start | bytes 1572872 | tf_op jit(solution)/shard_map/ppermute | solution.py:213
  43.6 4.0 %collective-permute-done.9.refs_4_.refs_11_ = bf16[2,64,2048]{2,1,0:T(8,128)(2,1)S(1)} collective-permute-done((bf16[2,64,2048]{2,1,0:T(8,128)(2,1)S(1)}, bf16[2,64,2048]{2,1,0:T(8,128)(2,1)S(1)}, u32[]{:S(2)}, u32[]{:S(2)}) %collective-permute-start.9) | collective-permute-done | bytes 524320 | tf_op jit(solution)/shard_map/ppermute | solution.py:213
  47.6 1.1 %sum_4.1.refs_5_ = f32[2,128,64]{2,1,0:T(8,128)S(1)} custom-call(s32[33]{0:T(128)S(1)} %get-tuple-element.20.scalar_ref, bf16[256,2048]{1,0:T(8,128)(2,1)S(1)} %get-tuple-element.21.refs_0_, bf16[256,2048]{1,0:T(8,128)(2,1)S(1)} %collective-permute-done.refs_1_, bf16[256,2048]{1,0:T(8,128)(2,1)S(1)} %collective-permute-done.1.refs_2_, ...), custom_call_target="tpu_custom_call" | custom-call | tf_op jit(solution)/shard_map/sum_4/pallas_call | solution.py:163
  48.7 1.3 %collective-permute-start.10 = (bf16[2,64,2048]{2,1,0:T(8,128)(2,1)S(1)}, bf16[2,64,2048]{2,1,0:T(8,128)(2,1)S(1)}, u32[]{:S(2)}, u32[]{:S(2)}) collective-permute-start(bf16[2,64,2048]{2,1,0:T(8,128)(2,1)S(1)} %collective-permute-done.7.refs_3_.refs_8_), channel_id=1, source_target_pairs={{4,0},{8,12},{5,1},{9,13},{6,2},{10,14},{7,3},{11,15},{20,16},{24,... | collective-permute-start | bytes 1572872 | tf_op jit(solution)/shard_map/ppermute | solution.py:213
  50.0 9.3 %collective-permute-done.12.refs_4_.refs_12_ = bf16[2,64,2048]{2,1,0:T(8,128)(2,1)S(1)} collective-permute-done((bf16[2,64,2048]{2,1,0:T(8,128)(2,1)S(1)}, bf16[2,64,2048]{2,1,0:T(8,128)(2,1)S(1)}, u32[]{:S(2)}, u32[]{:S(2)}) %collective-permute-start.12) | collective-permute-done | bytes 524320 | tf_op jit(solution)/shard_map/ppermute | solution.py:213
  59.3 1.1 %sum_5.1.refs_14_ = f32[2,128,64]{2,1,0:T(8,128)S(1)} custom-call(s32[33]{0:T(128)S(1)} %get-tuple-element.20.scalar_ref, bf16[256,2048]{1,0:T(8,128)(2,1)S(1)} %get-tuple-element.21.refs_0_, bf16[256,2048]{1,0:T(8,128)(2,1)S(1)} %collective-permute-done.refs_1_, bf16[256,2048]{1,0:T(8,128)(2,1)S(1)} %collective-permute-done.1.refs_2_, ...), custom_call_target="tpu_custom_call" | custom-call | tf_op jit(solution)/shard_map/sum_5/pallas_call | solution.py:163
  60.3 4.5 %collective-permute-done.6.refs_3_ = bf16[256,2048]{1,0:T(8,128)(2,1)S(1)} collective-permute-done((bf16[256,2048]{1,0:T(8,128)(2,1)S(1)}, bf16[256,2048]{1,0:T(8,128)(2,1)S(1)}, u32[]{:S(2)}, u32[]{:S(2)}) %collective-permute-start.6) | collective-permute-done | bytes 1048608 | tf_op jit(solution)/shard_map/ppermute | solution.py:228
  64.8 2.9 %sum_6.1.refs_5_ = f32[2,128,64]{2,1,0:T(8,128)S(1)} custom-call(s32[33]{0:T(128)S(1)} %get-tuple-element.20.scalar_ref, bf16[256,2048]{1,0:T(8,128)(2,1)S(1)} %get-tuple-element.21.refs_0_, bf16[256,2048]{1,0:T(8,128)(2,1)S(1)} %collective-permute-done.refs_1_, bf16[256,2048]{1,0:T(8,128)(2,1)S(1)} %collective-permute-done.1.refs_2_, ...), custom_call_target="tpu_custom_call" | custom-call | tf_op jit(solution)/shard_map/sum_6/pallas_call | solution.py:163
  67.7 2.8 %collective-permute-done.11.refs_4_ = bf16[2,64,2048]{2,1,0:T(8,128)(2,1)S(1)} collective-permute-done((bf16[2,64,2048]{2,1,0:T(8,128)(2,1)S(1)}, bf16[2,64,2048]{2,1,0:T(8,128)(2,1)S(1)}, u32[]{:S(2)}, u32[]{:S(2)}) %collective-permute-start.11) | collective-permute-done | bytes 524320 | tf_op jit(solution)/shard_map/ppermute | solution.py:213
  70.5 1.1 %sum_7.1.refs_5_ = f32[2,128,64]{2,1,0:T(8,128)S(1)} custom-call(s32[33]{0:T(128)S(1)} %get-tuple-element.20.scalar_ref, bf16[256,2048]{1,0:T(8,128)(2,1)S(1)} %get-tuple-element.21.refs_0_, bf16[256,2048]{1,0:T(8,128)(2,1)S(1)} %collective-permute-done.refs_1_, bf16[256,2048]{1,0:T(8,128)(2,1)S(1)} %collective-permute-done.1.refs_2_, ...), custom_call_target="tpu_custom_call" | custom-call | tf_op jit(solution)/shard_map/sum_7/pallas_call | solution.py:163
  71.6 9.9 %collective-permute-done.10.refs_4_ = bf16[2,64,2048]{2,1,0:T(8,128)(2,1)S(1)} collective-permute-done((bf16[2,64,2048]{2,1,0:T(8,128)(2,1)S(1)}, bf16[2,64,2048]{2,1,0:T(8,128)(2,1)S(1)}, u32[]{:S(2)}, u32[]{:S(2)}) %collective-permute-start.10) | collective-permute-done | bytes 524320 | tf_op jit(solution)/shard_map/ppermute | solution.py:213
  81.5 1.2 %sum_8.1 = (f32[32,128]{1,0:T(8,128)S(1)}, f32[32,128]{1,0:T(8,128)S(1)}, f32[32,128]{1,0:T(8,128)S(1)}, f32[32,128]{1,0:T(8,128)S(1)}) custom-call(s32[33]{0:T(128)S(1)} %get-tuple-element.20.scalar_ref, bf16[256,2048]{1,0:T(8,128)(2,1)S(1)} %get-tuple-element.21.refs_0_, bf16[256,2048]{1,0:T(8,128)(2,1)S(1)} %collective-permute-done.refs_1_, ...), custom_call_target="tpu_custom_call" | custom-call | tf_op jit(solution)/shard_map/sum_8/pallas_call | solution.py:163
  83.5 1.2 %collective-permute-start.15 = (f32[32,128]{1,0:T(8,128)S(1)}, f32[32,128]{1,0:T(8,128)S(1)}, u32[]{:S(2)}, u32[]{:S(2)}) collective-permute-start(f32[32,128]{1,0:T(8,128)S(1)} %get-tuple-element.34), channel_id=1, source_target_pairs={{0,3},{1,2},{2,1},{3,0},{4,7},{5,6},{6,5},{7,4},{8,11},{9,10},{10,... | collective-permute-start | bytes 49160 | tf_op jit(solution)/shard_map/ppermute | solution.py:238
  84.7 2.0 %collective-permute-done.14 = f32[32,128]{1,0:T(8,128)S(1)} collective-permute-done((f32[32,128]{1,0:T(8,128)S(1)}, f32[32,128]{1,0:T(8,128)S(1)}, u32[]{:S(2)}, u32[]{:S(2)}) %collective-permute-start.14) | collective-permute-done | bytes 16416 | tf_op jit(solution)/shard_map/ppermute | solution.py:238
  (26 shorter events, 7.7 us)
Async XLA Ops:
  5.0 8.9 %collective-permute-start = (bf16[256,2048]{1,0:T(8,128)(2,1)S(1)}, bf16[256,2048]{1,0:T(8,128)(2,1)S(1)}, u32[]{:S(2)}, u32[]{:S(2)}) collective-permute-start(bf16[256,2048]{1,0:T(8,128)(2,1)S(1)} %get-tuple-element.26), channel_id=1, source_target_pairs={{0,1},{1,0},{2,3},{3,2},{4,5},{5,4},{6,7},{7,6},{8,9},{9,8},{10,11... | collective-permute-start | bytes 3145736 | tf_op jit(solution)/shard_map/ppermute | solution.py:197
  5.5 32.7 %collective-permute-start.1 = (bf16[256,2048]{1,0:T(8,128)(2,1)S(1)}, bf16[256,2048]{1,0:T(8,128)(2,1)S(1)}, u32[]{:S(2)}, u32[]{:S(2)}) collective-permute-start(bf16[256,2048]{1,0:T(8,128)(2,1)S(1)} %get-tuple-element.21.refs_0_), channel_id=1, source_target_pairs={{0,2},{1,3},{2,0},{3,1},{4,6},{5,7},{6,4},{7,5},{8,10},{9,11},{10,... | collective-permute-start | bytes 3145736 | tf_op jit(solution)/shard_map/ppermute | solution.py:217
  8.0 18.6 %collective-permute-start.2 = (bf16[2,64,2048]{2,1,0:T(8,128)(2,1)S(1)}, bf16[2,64,2048]{2,1,0:T(8,128)(2,1)S(1)}, u32[]{:S(2)}, u32[]{:S(2)}) collective-permute-start(bf16[2,64,2048]{2,1,0:T(8,128)(2,1)S(1)} %get-tuple-element.23.refs_2_.refs_3_.refs_4_), channel_id=1, source_target_pairs={{4,8},{8,4},{5,9},{9,5},{6,10},{10,6},{7,11},{11,7},{20,24},{24,20... | collective-permute-start | bytes 1572872 | tf_op jit(solution)/shard_map/ppermute | solution.py:213
  8.7 17.2 %collective-permute-start.4 = (bf16[2,64,2048]{2,1,0:T(8,128)(2,1)S(1)}, bf16[2,64,2048]{2,1,0:T(8,128)(2,1)S(1)}, u32[]{:S(2)}, u32[]{:S(2)}) collective-permute-start(bf16[2,64,2048]{2,1,0:T(8,128)(2,1)S(1)} %get-tuple-element.23.refs_2_.refs_3_.refs_4_), channel_id=1, source_target_pairs={{0,4},{4,0},{8,12},{12,8},{1,5},{5,1},{9,13},{13,9},{2,6},{6,2},{1... | collective-permute-start | bytes 1572872 | tf_op jit(solution)/shard_map/ppermute | solution.py:213
  13.2 15.7 %collective-permute-start.3 = (bf16[2,64,2048]{2,1,0:T(8,128)(2,1)S(1)}, bf16[2,64,2048]{2,1,0:T(8,128)(2,1)S(1)}, u32[]{:S(2)}, u32[]{:S(2)}) collective-permute-start(bf16[2,64,2048]{2,1,0:T(8,128)(2,1)S(1)} %get-tuple-element.25.refs_3_.refs_8_.refs_13_), channel_id=1, source_target_pairs={{4,8},{8,4},{5,9},{9,5},{6,10},{10,6},{7,11},{11,7},{20,24},{24,20... | collective-permute-start | bytes 1572872 | tf_op jit(solution)/shard_map/ppermute | solution.py:213
  15.3 21.9 %collective-permute-start.5 = (bf16[2,64,2048]{2,1,0:T(8,128)(2,1)S(1)}, bf16[2,64,2048]{2,1,0:T(8,128)(2,1)S(1)}, u32[]{:S(2)}, u32[]{:S(2)}) collective-permute-start(bf16[2,64,2048]{2,1,0:T(8,128)(2,1)S(1)} %get-tuple-element.25.refs_3_.refs_8_.refs_13_), channel_id=1, source_target_pairs={{0,4},{4,0},{8,12},{12,8},{1,5},{5,1},{9,13},{13,9},{2,6},{6,2},{1... | collective-permute-start | bytes 1572872 | tf_op jit(solution)/shard_map/ppermute | solution.py:213
  25.9 16.4 %collective-permute-start.8 = (bf16[2,64,2048]{2,1,0:T(8,128)(2,1)S(1)}, bf16[2,64,2048]{2,1,0:T(8,128)(2,1)S(1)}, u32[]{:S(2)}, u32[]{:S(2)}) collective-permute-start(bf16[2,64,2048]{2,1,0:T(8,128)(2,1)S(1)} %collective-permute-done.4.refs_3_.refs_6_.refs_9_), channel_id=1, source_target_pairs={{4,8},{8,4},{5,9},{9,5},{6,10},{10,6},{7,11},{11,7},{20,24},{24,20... | collective-permute-start | bytes 1572872 | tf_op jit(solution)/shard_map/ppermute | solution.py:213
  26.6 21.0 %collective-permute-start.9 = (bf16[2,64,2048]{2,1,0:T(8,128)(2,1)S(1)}, bf16[2,64,2048]{2,1,0:T(8,128)(2,1)S(1)}, u32[]{:S(2)}, u32[]{:S(2)}) collective-permute-start(bf16[2,64,2048]{2,1,0:T(8,128)(2,1)S(1)} %collective-permute-done.2.refs_2_.refs_4_.refs_5_), channel_id=1, source_target_pairs={{4,0},{8,12},{5,1},{9,13},{6,2},{10,14},{7,3},{11,15},{20,16},{24,... | collective-permute-start | bytes 1572872 | tf_op jit(solution)/shard_map/ppermute | solution.py:213
  40.2 24.6 %collective-permute-start.6 = (bf16[256,2048]{1,0:T(8,128)(2,1)S(1)}, bf16[256,2048]{1,0:T(8,128)(2,1)S(1)}, u32[]{:S(2)}, u32[]{:S(2)}) collective-permute-start(bf16[256,2048]{1,0:T(8,128)(2,1)S(1)} %get-tuple-element.26), channel_id=1, source_target_pairs={{0,3},{1,2},{2,1},{3,0},{4,7},{5,6},{6,5},{7,4},{8,11},{9,10},{10,... | collective-permute-start | bytes 3145736 | tf_op jit(solution)/shard_map/ppermute | solution.py:228
  40.3 8.4 %collective-permute-start.7 = (bf16[2,64,2048]{2,1,0:T(8,128)(2,1)S(1)}, bf16[2,64,2048]{2,1,0:T(8,128)(2,1)S(1)}, u32[]{:S(2)}, u32[]{:S(2)}) collective-permute-start(bf16[2,64,2048]{2,1,0:T(8,128)(2,1)S(1)} %collective-permute-done.5.refs_3_.refs_7_.refs_10_), channel_id=1, source_target_pairs={{4,8},{8,4},{5,9},{9,5},{6,10},{10,6},{7,11},{11,7},{20,24},{24,20... | collective-permute-start | bytes 1572872 | tf_op jit(solution)/shard_map/ppermute | solution.py:213
  41.0 18.3 %collective-permute-start.12 = (bf16[2,64,2048]{2,1,0:T(8,128)(2,1)S(1)}, bf16[2,64,2048]{2,1,0:T(8,128)(2,1)S(1)}, u32[]{:S(2)}, u32[]{:S(2)}) collective-permute-start(bf16[2,64,2048]{2,1,0:T(8,128)(2,1)S(1)} %collective-permute-done.3.refs_2_.refs_5_.refs_6_), channel_id=1, source_target_pairs={{4,0},{8,12},{5,1},{9,13},{6,2},{10,14},{7,3},{11,15},{20,16},{24,... | collective-permute-start | bytes 1572872 | tf_op jit(solution)/shard_map/ppermute | solution.py:213
  42.3 28.2 %collective-permute-start.11 = (bf16[2,64,2048]{2,1,0:T(8,128)(2,1)S(1)}, bf16[2,64,2048]{2,1,0:T(8,128)(2,1)S(1)}, u32[]{:S(2)}, u32[]{:S(2)}) collective-permute-start(bf16[2,64,2048]{2,1,0:T(8,128)(2,1)S(1)} %collective-permute-done.8.refs_3_.refs_7_), channel_id=1, source_target_pairs={{4,0},{8,12},{5,1},{9,13},{6,2},{10,14},{7,3},{11,15},{20,16},{24,... | collective-permute-start | bytes 1572872 | tf_op jit(solution)/shard_map/ppermute | solution.py:213
  48.7 32.8 %collective-permute-start.10 = (bf16[2,64,2048]{2,1,0:T(8,128)(2,1)S(1)}, bf16[2,64,2048]{2,1,0:T(8,128)(2,1)S(1)}, u32[]{:S(2)}, u32[]{:S(2)}) collective-permute-start(bf16[2,64,2048]{2,1,0:T(8,128)(2,1)S(1)} %collective-permute-done.7.refs_3_.refs_8_), channel_id=1, source_target_pairs={{4,0},{8,12},{5,1},{9,13},{6,2},{10,14},{7,3},{11,15},{20,16},{24,... | collective-permute-start | bytes 1572872 | tf_op jit(solution)/shard_map/ppermute | solution.py:213
  67.7 17.0 %copy-start = (s32[32]{0:T(128)S(1)}, s32[32]{0:T(128)}, u32[]{:S(2)}) copy-start(s32[32]{0:T(128)} %param.7) | copy-start | bytes 388
  82.7 2.0 %collective-permute-start.13 = (f32[32,128]{1,0:T(8,128)S(1)}, f32[32,128]{1,0:T(8,128)S(1)}, u32[]{:S(2)}, u32[]{:S(2)}) collective-permute-start(f32[32,128]{1,0:T(8,128)S(1)} %get-tuple-element.32), channel_id=1, source_target_pairs={{0,1},{1,0},{2,3},{3,2},{4,5},{5,4},{6,7},{7,6},{8,9},{9,8},{10,11... | collective-permute-start | bytes 49160 | tf_op jit(solution)/shard_map/ppermute | solution.py:237
  82.8 3.9 %collective-permute-start.14 = (f32[32,128]{1,0:T(8,128)S(1)}, f32[32,128]{1,0:T(8,128)S(1)}, u32[]{:S(2)}, u32[]{:S(2)}) collective-permute-start(f32[32,128]{1,0:T(8,128)S(1)} %get-tuple-element.33), channel_id=1, source_target_pairs={{0,2},{1,3},{2,0},{3,1},{4,6},{5,7},{6,4},{7,5},{8,10},{9,11},{10,... | collective-permute-start | bytes 49160 | tf_op jit(solution)/shard_map/ppermute | solution.py:238
  83.5 3.3 %collective-permute-start.15 = (f32[32,128]{1,0:T(8,128)S(1)}, f32[32,128]{1,0:T(8,128)S(1)}, u32[]{:S(2)}, u32[]{:S(2)}) collective-permute-start(f32[32,128]{1,0:T(8,128)S(1)} %get-tuple-element.34), channel_id=1, source_target_pairs={{0,3},{1,2},{2,1},{3,0},{4,7},{5,6},{6,5},{7,4},{8,11},{9,10},{10,... | collective-permute-start | bytes 49160 | tf_op jit(solution)/shard_map/ppermute | solution.py:238

commit v3 on v2

v3 whole, which is shorter than its diff:
```python
import functools

import jax
import jax.numpy as jnp
from jax import lax
from jax.experimental import pallas as pl
from jax.experimental.pallas import tpu as pltpu
from jax.sharding import PartitionSpec as P

VMEM_LIMIT = 12 * 1024 * 1024
PREPARE_VMEM = 50 * 1024 * 1024
NT = (((1,), (1,)), ((), ()))
SWAP = [(0, 1), (1, 0)]
NEAR = [(0, 1), (1, 0), (2, 3), (3, 2)]
MIDDLE = [(1, 2), (2, 1)]
OUTWARD = [(1, 0), (2, 3)]
INWARD = [(0, 1), (3, 2)]


def plain(amplitudes, integrals, pair_irrep, slot_irrep, owner_slot_map):
    row_count, slot_count, tile_size = amplitudes.shape
    slot_position_index = jnp.arange(slot_count, dtype=jnp.int32)
    picked = owner_slot_map[:, None] == slot_position_index[None, :]
    owner_irrep = jnp.sum(jnp.where(picked, slot_irrep[None, :], 0), axis=1)
    sorted_slots = jnp.take(amplitudes, owner_slot_map, axis=1)
    live_tiles = pair_irrep[:, None] == owner_irrep[None, :]
    sorted_slots = jnp.where(live_tiles[:, :, None], sorted_slots, jnp.zeros((), jnp.bfloat16))
    flattened = sorted_slots.reshape(row_count, slot_count * tile_size)
    columns = lax.all_to_all(flattened, "pair", split_axis=1, concat_axis=0, tiled=True)
    partial_sums = lax.dot_general(
        columns,
        lax.all_gather(integrals, "ints", axis=0, tiled=True),
        NT,
        preferred_element_type=jnp.float32,
    )
    return lax.psum_scatter(partial_sums, "pair", scatter_dimension=0, tiled=True)


def prepare_kernel(rows, slots, scalar_ref, x_ref, integrals_ref, other_ref, mine_ref, own_ref, first_ref, second_ref, table_ref, held_ref, pick_ref, copied, loaded):
    steps, _, width = held_ref.shape
    half = first_ref.shape[2]
    core = scalar_ref[1]
    moves, loads = [], []
    held = own_ref.shape[0]
    for p in range(held):
        start = pl.multiple_of((2 * p + core) * half, half)
        source = integrals_ref.at[:, pl.ds(start, half)]
        moves.append(pltpu.make_async_copy(source, own_ref.at[p], copied.at[p]))
    for i in range(steps):
        half_here = core if i < steps // 2 else 1 - core
        start = pl.multiple_of(half_here * half + i % (steps // 2) * width, width)
        loads.append(pltpu.make_async_copy(x_ref.at[:, pl.ds(start, width)], held_ref.at[i], loaded.at[i]))
    for move in moves + loads:
        move.start()

    groups, picked, per_group = pick_ref.shape
    group = per_group // slots
    lane = lax.broadcasted_iota(jnp.int32, (1, per_group), 1)
    slot_lane, row_lane = lane % slots, lane // slots
    counts = [jnp.int32(0), jnp.int32(0)]
    lane_rank = jnp.zeros_like(lane)
    lane_irrep = jnp.zeros_like(lane)
    begin = jnp.where(scalar_ref[0] < 2, slots - held, 0) + held // 2
    for q in range(slots):
        position = lax.rem(begin + q, slots)
        slot = scalar_ref[2 + slots + position]
        irrep = scalar_ref[2 + slot]
        odd = irrep == 1
        rank = jnp.where(odd, counts[1], counts[0])
        counts = [jnp.where(odd, counts[0], counts[0] + 1), jnp.where(odd, counts[1] + 1, counts[1])]
        table_ref[position] = rank
        table_ref[slots + position] = irrep
        here = slot_lane == slot
        lane_rank = jnp.where(here, rank, lane_rank)
        lane_irrep = jnp.where(here, irrep, lane_irrep)
    table_ref[2 * slots] = scalar_ref[0]
    row = lax.broadcasted_iota(jnp.int32, (picked, per_group), 0)
    for g in range(groups):
        row_irrep = jnp.zeros_like(lane)
        for o in range(group):
            row_irrep = jnp.where(row_lane == o, scalar_ref[2 + 2 * slots + g * group + o], row_irrep)
        target = jnp.where(lane_irrep == row_irrep, lane_rank * group + row_lane, -1)
        pick_ref[g] = jnp.where(row == target, 1.0, 0.0).astype(pick_ref.dtype)

    for i in range(steps):
        loads[i].wait()
        into = mine_ref if i < steps // 2 else other_ref
        at = i % (steps // 2) * width
        for g in range(groups):
            source = held_ref[i, g * per_group : (g + 1) * per_group]
            packed = jnp.dot(pick_ref[g], source, preferred_element_type=jnp.float32).astype(held_ref.dtype)
            for j in range(picked // group):
                to = j * rows + g * group
                into[to : to + group, at : at + width] = packed[j * group : (j + 1) * group]
    for p, move in enumerate(moves):
        move.wait()
        chunk_ref = first_ref if p < held // 2 else second_ref
        chunk_ref[p % (held // 2)] = own_ref[p]


def prepare(scalars, amplitudes, integrals, steps=8):
    rows, slots, tile = amplitudes.shape
    live, half = slots // 2, tile // 2
    ab, columns = integrals.shape
    held = columns // tile
    packed = jax.ShapeDtypeStruct((live * rows, half), amplitudes.dtype)
    whole = jax.ShapeDtypeStruct((held, ab, half), integrals.dtype)
    chunk = jax.ShapeDtypeStruct((held // 2, ab, half), integrals.dtype)
    hbm = pl.BlockSpec(memory_space=pltpu.HBM)
    vmem = pl.BlockSpec(memory_space=pltpu.VMEM)
    smem = pl.BlockSpec(memory_space=pltpu.SMEM)
    return pl.pallas_call(
        functools.partial(prepare_kernel, rows, slots),
        in_specs=[smem, hbm, hbm],
        out_specs=[vmem, vmem, vmem, vmem, vmem, smem],
        out_shape=[packed, packed, whole, chunk, chunk, jax.ShapeDtypeStruct((2 * slots + 1,), jnp.int32)],
        scratch_shapes=[
            pltpu.VMEM((steps, rows * slots, tile // steps), amplitudes.dtype),
            pltpu.VMEM((rows // 16, live * 16, 16 * slots), amplitudes.dtype),
            pltpu.SemaphoreType.DMA((held,)),
            pltpu.SemaphoreType.DMA((steps,)),
        ],
        compiler_params=pltpu.CompilerParams(vmem_limit_bytes=PREPARE_VMEM),
        cost_estimate=pl.CostEstimate(
            flops=2 * live * rows * rows * slots * tile, bytes_accessed=3 * rows * slots * tile, transcendentals=0
        ),
        name="prepare",
    )(scalars, amplitudes.reshape(rows * slots, tile), integrals)


def sum_kernel(rows, slots, tiles, work, table, ends, extra, scalar_ref, *refs):
    arrays, refs = refs[: tiles[-1][0] + 1], refs[tiles[-1][0] + 1 :]
    chunks, refs = refs[: len(table)], refs[len(table) :]
    total_ref = refs[-1]
    total_ref[...] = refs[0][...] if extra else jnp.zeros_like(total_ref)
    place = scalar_ref[2 * slots]
    for (low, high), used in work:
        for c in used:
            for i in range(chunks[c].shape[0]):
                position = jnp.int32(table[c][0][i])
                for z in range(1, len(table[c])):
                    position = jnp.where(place == z, table[c][z][i], position)

                @pl.when(position >= 0)
                def _():
                    at = jnp.maximum(position, 0)
                    start = scalar_ref[at] * rows
                    here = jnp.concatenate(
                        [arrays[t][pl.ds(pl.multiple_of(start + base, rows), rows), :] for t, base in tiles[low:high]], axis=0
                    )
                    term = lax.dot_general(here, chunks[c][i], NT, preferred_element_type=jnp.float32)
                    total_ref[scalar_ref[slots + at], low * rows : high * rows] += term

    if ends:
        blocks = refs[-1 - ends : -1]
        for t, out_ref in enumerate(blocks):
            size = total_ref.shape[1] // ends
            at = slice(t * size, (t + 1) * size)
            out = jnp.concatenate([total_ref[0, at], total_ref[1, at]], axis=1)
            if extra > 1 and (t + 1) * size <= refs[1].shape[0]:
                out = out + refs[1][at]
            out_ref[...] = out


def add_positions(scalars, arrays, tiles, rows, blocks, chunks, table, work, extra=(), ends=0, name="sum"):
    slots = scalars.shape[0] // 2
    ab = chunks[0].shape[1]
    vmem = pl.BlockSpec(memory_space=pltpu.VMEM)
    smem = pl.BlockSpec(memory_space=pltpu.SMEM)
    total = (2, blocks * rows, ab)
    end = jax.ShapeDtypeStruct((blocks * rows // max(ends, 1), 2 * ab), jnp.float32)
    return pl.pallas_call(
        functools.partial(sum_kernel, rows, slots, tuple(tiles), work, table, ends, len(extra)),
        in_specs=[smem] + [vmem] * (len(arrays) + len(chunks) + len(extra)),
        out_specs=[vmem] * ends if ends else vmem,
        out_shape=[end] * ends if ends else jax.ShapeDtypeStruct(total, jnp.float32),
        scratch_shapes=[pltpu.VMEM(total, jnp.float32)] if ends else [],
        compiler_params=pltpu.CompilerParams(vmem_limit_bytes=VMEM_LIMIT),
        name=name,
    )(scalars, *arrays, *chunks, *extra)


def after(array, *earlier):
    return lax.optimization_barrier((array, *earlier))[0] if earlier else array


def on_line(amplitudes, integrals, pair_irrep, slot_irrep, owner_slot_map):
    rows, slots, tile = amplitudes.shape
    place, side, core = lax.axis_index("pair"), lax.axis_index("ints"), lax.axis_index("rep")
    scalars = jnp.concatenate([jnp.stack([place, core]).astype(jnp.int32), slot_irrep, owner_slot_map, pair_irrep])
    across = [(i, 3 - i) for i in range(4)]
    beside = [(i, i ^ 2) for i in range(4)]

    other, mine, own, first, second, scalars = prepare(scalars, amplitudes, integrals)
    held = slots // 4
    per = held // 2

    def held_at(places, low=0, high=held):
        return tuple((-1,) * (high - low) if z is None else tuple(range(z * held + low, z * held + high)) for z in places)

    home, near = (0, 1, 2, 3), (1, 0, 3, 2)
    middle, beyond = (None, 2, 1, None), (None, 3, 0, None)
    outer, outermost = (2, None, None, 1), (3, None, None, 0)
    chunks = {"own": (own, held_at(home)), "own1": (first, ()), "own2": (second, ())}
    tiles = [mine, lax.ppermute(other, "rep", SWAP)]

    def add(name, *step, arrays=None, at=None, blocks=4, extra=(), ends=0):
        names = []
        for *_, used in step:
            names += [n for n in used if n not in names]
        if arrays is None:
            arrays = tiles[: max(high for _, high, _ in step)]
            at = [(t, 0) for t in range(len(arrays))]
        return add_positions(
            scalars,
            arrays,
            at,
            rows,
            blocks,
            tuple(chunks[n][0] for n in names),
            tuple(chunks[n][1] for n in names),
            tuple(((low, high), tuple(names.index(n) for n in used)) for low, high, used in step),
            extra=extra,
            ends=ends,
            name=name,
        )

    def send(name, source, pairs, positions, *earlier):
        chunks[name] = (lax.ppermute(after(chunks[source][0], *earlier), "pair", pairs), positions)

    send("near1", "own1", NEAR, held_at(near, 0, per))
    send("mid", "own", MIDDLE, held_at(middle))
    send("near2", "own2", NEAR, held_at(near, per))
    tiles.append(lax.ppermute(mine, ("ints", "rep"), beside))
    sums = add("sum_home", (0, 2, ("own",)))
    tiles.append(lax.ppermute(after(other, sums), ("ints", "rep"), across))
    send("mid3", "near1", MIDDLE, held_at(beyond, 0, per))
    send("out", "mid", OUTWARD, held_at(outer))
    send("mid4", "near2", MIDDLE, held_at(beyond, per))
    sums = add("sum_near", (0, 2, ("near1", "near2", "mid")), extra=(sums,))
    sums = add("sum_side", (2, 3, ("own", "near1", "near2", "mid")), extra=(sums,))
    heads = lax.ppermute(after(jnp.concatenate([t[: per * rows] for t in tiles[:3]]), sums), "pair", INWARD)
    send("out3", "mid3", OUTWARD, held_at(outermost, 0, per))
    sums = add("sum_beyond", (0, 3, ("mid3", "mid4")), extra=(sums,))
    away = add("sum_away", (0, 3, ("mid4",)), arrays=[after(heads, sums)], at=[(0, t * per * rows) for t in range(3)], blocks=3, ends=1)
    back = lax.ppermute(away[0], "pair", OUTWARD)
    last_heads = lax.ppermute(tiles[3][: per * rows], "pair", INWARD)
    sums = add("sum_outer", (0, 3, ("out",)), extra=(sums,))
    everything = ("own", "near1", "near2", "mid", "mid3", "mid4", "out")
    sums = add("sum_across", (3, 4, everything), extra=(sums,))
    away = add("sum_away_across", (0, 1, ("mid4",)), arrays=[last_heads], at=[(0, 0)], blocks=1, ends=1)
    home_pairs = [(4 * a + i, 4 * b + 3 - i) for a, b in OUTWARD for i in range(4)]
    back_across = lax.ppermute(away[0], ("pair", "ints", "rep"), home_pairs)
    sums = add("sum_last", (0, 4, ("out3",)), extra=(after(sums, away[0]), back), ends=4)

    own = sums[0] + lax.ppermute(sums[1], "rep", SWAP)
    theirs = lax.ppermute(sums[2], ("ints", "rep"), beside) + lax.ppermute(sums[3], ("ints", "rep"), across)
    theirs = theirs + back_across
    ab = integrals.shape[0]
    odd = (pair_irrep == 1)[:, None]
    own = jnp.where(odd, own[:, ab:], own[:, :ab])
    theirs = jnp.where(odd, theirs[:, ab:], theirs[:, :ab])
    return jnp.where(side == 0, jnp.concatenate([own, theirs], axis=1), jnp.concatenate([theirs, own], axis=1))


def solution(mesh):
    placed = (
        P(("groups", "pair", "ints", "rep"), None, None),
        P(("groups", "ints"), "pair"),
        P(("groups", "pair", "ints", "rep")),
        P("groups"),
        P("groups"),
    )
    line = mesh.shape["pair"] == 4 and mesh.shape["ints"] == 2 and mesh.shape["rep"] == 2
    return jax.shard_map(
        on_line if line else plain,
        mesh=mesh,
        in_specs=placed,
        out_specs=P(("groups", "pair", "ints", "rep"), None),
        check_vma=False,
    )
```

time: 87.8 us -> 79.8 us (0.909)
  waiting for transfers between devices: 49.7 us -> 31.1 us
  starting transfers between devices: 19.2 us -> 28.3 us
  local copies, waits for them, and re-layouts: 0.77 us -> 2.07 us
    ppermute x10 -> x7, waiting for transfers between devices: 43.1 us -> 20.5 us  [send(): lax.ppermute(after(chunks[source][0], *earlier), 'pair', pairs)]
    ppermute x0 -> x4, starting transfers between devices: none -> 13.7 us  [the longest x1 5.69 us: on_line(): last_heads = lax.ppermute(tiles[3][:per * rows], 'pair', INWARD)]
    ppermute x10 -> x7, starting transfers between devices: 14.1 us -> 9.18 us  [send(): lax.ppermute(after(chunks[source][0], *earlier), 'pair', pairs)]
    ppermute x1, waiting for transfers between devices: 4.47 us -> 7.57 us  [on_line(): tiles.append(lax.ppermute(after(other, sums), ('ints', 'rep'), across))]
    ppermute x1, waiting for transfers between devices: 2.04 us -> 0.75 us  [on_line(): lax.ppermute(sums[2], ('ints', 'rep'), beside)]
    unnamed x2 -> x6, local copies, waits for them, and re-layouts: 0.01 us -> 1.23 us
    ppermute x1, starting transfers between devices: 1.17 us -> 0.01 us  [on_line(): lax.ppermute(sums[3], ('ints', 'rep'), across)]
  transfers between devices with their start and end apart: 16 -> 17, of which waited for: 9 -> 9; matrix products, arithmetic and copies ran while one was open for 0% -> 0% of each run, Pallas kernels for 13% -> 15%
where the time goes in v3:
time: 79.8 us; the launch traced here: 79.5 us
  waiting for transfers between devices  31.1 us (39%)
  starting transfers between devices  28.3 us (35%)
  Pallas kernels  16.9 us (21%)
  local copies, waits for them, and re-layouts  2.07 us (3%)
  other arithmetic  0.86 us (1%)
    ppermute x7, waiting for transfers between devices, send(): lax.ppermute(after(chunks[source][0], *earlier), 'pair', pairs)  20.5 us
    pallas_call x9, Pallas kernels, add_positions(): pl.pallas_call(functools.partial(sum_kernel, rows, slots, tuple(tiles), w...  12.2 us
    ppermute x7, starting transfers between devices, send(): lax.ppermute(after(chunks[source][0], *earlier), 'pair', pairs)  9.18 us
    ppermute x1, waiting for transfers between devices, on_line(): tiles.append(lax.ppermute(after(other, sums), ('ints', 'rep'), across))  7.57 us
    ppermute x1, starting transfers between devices, on_line(): last_heads = lax.ppermute(tiles[3][:per * rows], 'pair', INWARD)  5.69 us
    ppermute x1, starting transfers between devices, on_line(): lax.ppermute(after(jnp.concatenate([t[:per * rows] for t in tiles[:3]]),...  5.33 us
    pallas_call x1, Pallas kernels, prepare(): pl.pallas_call(functools.partial(prepare_kernel, rows, slots), in_specs=[...  4.65 us
    ppermute x1, starting transfers between devices, on_line(): tiles.append(lax.ppermute(mine, ('ints', 'rep'), beside))  2.58 us
  transfers between devices with their start and end apart: 17, of which 9 were waited for; matrix products, arithmetic and copies ran while one was open for 0% of the time, Pallas kernels for 15%

profile of v3, /device:TPU:0, one launch (start us, length us, event | category | flops | bytes accessed | tf_op | source)
XLA Modules:
  0.0 79.5 jit_solution(14358720746755339819)
XLA Ops:
  0.0 0.8 concatenate.12.scalar_ref
  0.8 4.6 %prepare.1 = (bf16[256,2048]{1,0:T(8,128)(2,1)S(1)}, bf16[256,2048]{1,0:T(8,128)(2,1)S(1)}, bf16[4,64,2048]{2,1,0:T(8,128)(2,1)}, bf16[2,64,2048]{2,1,0:T(8,128)...) custom-call(s32[66]{0:T(128)S(1)} %concatenate.12.scalar_ref, bf16[512,4096]{1,0:T(8,128)(2,1)} %bitcast.3, ...), custom_call_target="tpu_custom_call" | custom-call | flops 1073741824 | bytes 6291456 | tf_op jit(solution)/shard_map/prepare/pallas_call | solution.py:112
  6.7 2.6 %collective-permute-start.1 = (bf16[256,2048]{1,0:T(8,128)(2,1)S(1)}, bf16[256,2048]{1,0:T(8,128)(2,1)S(1)}, u32[]{:S(2)}, u32[]{:S(2)}) collective-permute-start(bf16[256,2048]{1,0:T(8,128)(2,1)S(1)} %get-tuple-element.20.refs_0_), channel_id=1, source_target_pairs={{0,2},{1,3},{2,0},{3,1},{4,6},{5,7},{6,4},{7,5},{8,10},{9,11},{10,... | collective-permute-start | bytes 3145736 | tf_op jit(solution)/shard_map/ppermute | solution.py:234
  9.2 4.3 %collective-permute-start.3 = (bf16[2,64,2048]{2,1,0:T(8,128)(2,1)S(1)}, bf16[2,64,2048]{2,1,0:T(8,128)(2,1)S(1)}, u32[]{:S(2)}, u32[]{:S(2)}) collective-permute-start(bf16[2,64,2048]{2,1,0:T(8,128)(2,1)S(1)} %get-tuple-element.24), channel_id=1, source_target_pairs={{0,4},{4,0},{8,12},{12,8},{1,5},{5,1},{9,13},{13,9},{2,6},{6,2},{1... | collective-permute-start | bytes 1572872 | tf_op jit(solution)/shard_map/ppermute | solution.py:229
  13.6 1.2 %copy-done = bf16[4,64,2048]{2,1,0:T(8,128)(2,1)S(1)} copy-done((bf16[4,64,2048]{2,1,0:T(8,128)(2,1)S(1)}, bf16[4,64,2048]{2,1,0:T(8,128)(2,1)}, u32[]{:S(2)}) %copy-start) | copy-done | bytes 1048600
  14.8 1.4 %sum_home.1.refs_5_ = f32[2,128,64]{2,1,0:T(8,128)S(1)} custom-call(s32[33]{0:T(128)S(1)} %get-tuple-element.19.scalar_ref, bf16[256,2048]{1,0:T(8,128)(2,1)S(1)} %get-tuple-element.20.refs_0_, bf16[256,2048]{1,0:T(8,128)(2,1)S(1)} %collective-permute-done.refs_1_, bf16[4,64,2048]{2,1,0:T(8,128)(2,1)S(1)} %copy-done), custom_call_target="tpu_custom_call" | custom-call | tf_op jit(solution)/shard_map/sum_home/pallas_call | solution.py:172
  16.3 10.0 %collective-permute-done.3.refs_2_.refs_4_.refs_5_ = bf16[2,64,2048]{2,1,0:T(8,128)(2,1)S(1)} collective-permute-done((bf16[2,64,2048]{2,1,0:T(8,128)(2,1)S(1)}, bf16[2,64,2048]{2,1,0:T(8,128)(2,1)S(1)}, u32[]{:S(2)}, u32[]{:S(2)}) %collective-permute-start.3) | collective-permute-done | bytes 524320 | tf_op jit(solution)/shard_map/ppermute | solution.py:229
  27.1 1.4 %collective-permute-start.9 = (bf16[4,64,2048]{2,1,0:T(8,128)(2,1)S(1)}, bf16[4,64,2048]{2,1,0:T(8,128)(2,1)S(1)}, u32[]{:S(2)}, u32[]{:S(2)}) collective-permute-start(bf16[4,64,2048]{2,1,0:T(8,128)(2,1)S(1)} %collective-permute-done.7.refs_4_.refs_6_.refs_7_), channel_id=1, source_target_pairs={{4,0},{8,12},{5,1},{9,13},{6,2},{10,14},{7,3},{11,15},{20,16},{24,... | collective-permute-start | bytes 3145736 | tf_op jit(solution)/shard_map/ppermute | solution.py:229
  28.5 8.3 %collective-permute-done.6.refs_3_.refs_5_.refs_6_ = bf16[2,64,2048]{2,1,0:T(8,128)(2,1)S(1)} collective-permute-done((bf16[2,64,2048]{2,1,0:T(8,128)(2,1)S(1)}, bf16[2,64,2048]{2,1,0:T(8,128)(2,1)S(1)}, u32[]{:S(2)}, u32[]{:S(2)}) %collective-permute-start.6) | collective-permute-done | bytes 524320 | tf_op jit(solution)/shard_map/ppermute | solution.py:229
  36.8 1.4 %sum_near.1.refs_7_ = f32[2,128,64]{2,1,0:T(8,128)S(1)} custom-call(s32[33]{0:T(128)S(1)} %get-tuple-element.19.scalar_ref, bf16[256,2048]{1,0:T(8,128)(2,1)S(1)} %get-tuple-element.20.refs_0_, bf16[256,2048]{1,0:T(8,128)(2,1)S(1)} %collective-permute-done.refs_1_, bf16[2,64,2048]{2,1,0:T(8,128)(2,1)S(1)} %collective-permute-done.3.refs_2_.refs_4_.refs_5_, ...), custom_call_target="tpu_custom_call" | custom-call | tf_op jit(solution)/shard_map/sum_near/pallas_call | solution.py:172
  38.3 2.0 %sum_side.1.refs_5_ = f32[2,128,64]{2,1,0:T(8,128)S(1)} custom-call(s32[33]{0:T(128)S(1)} %get-tuple-element.19.scalar_ref, bf16[256,2048]{1,0:T(8,128)(2,1)S(1)} %get-tuple-element.20.refs_0_, bf16[256,2048]{1,0:T(8,128)(2,1)S(1)} %collective-permute-done.refs_1_, bf16[256,2048]{1,0:T(8,128)(2,1)S(1)} %collective-permute-done.1.refs_2_, ...), custom_call_target="tpu_custom_call" | custom-call | tf_op jit(solution)/shard_map/sum_side/pallas_call | solution.py:172
  40.4 5.3 %collective-permute-start.11 = (bf16[192,2048]{1,0:T(8,128)(2,1)S(1)}, bf16[192,2048]{1,0:T(8,128)(2,1)S(1)}, u32[]{:S(2)}, u32[]{:S(2)}) collective-permute-start(bf16[192,2048]{1,0:T(8,128)(2,1)S(1)} %pad_maximum_fusion), channel_id=1, source_target_pairs={{0,4},{12,8},{1,5},{13,9},{2,6},{14,10},{3,7},{15,11},{16,20},{28,... | collective-permute-start | bytes 2359304 | tf_op jit(solution)/shard_map/ppermute | solution.py:242
  46.4 1.3 %collective-permute-start.5 = (bf16[2,64,2048]{2,1,0:T(8,128)(2,1)S(1)}, bf16[2,64,2048]{2,1,0:T(8,128)(2,1)S(1)}, u32[]{:S(2)}, u32[]{:S(2)}) collective-permute-start(bf16[2,64,2048]{2,1,0:T(8,128)(2,1)S(1)} %collective-permute-done.4.refs_3_.refs_8_), channel_id=1, source_target_pairs={{4,0},{8,12},{5,1},{9,13},{6,2},{10,14},{7,3},{11,15},{20,16},{24,... | collective-permute-start | bytes 1572872 | tf_op jit(solution)/shard_map/ppermute | solution.py:229
  47.7 7.6 %collective-permute-done.2.refs_3_ = bf16[256,2048]{1,0:T(8,128)(2,1)S(1)} collective-permute-done((bf16[256,2048]{1,0:T(8,128)(2,1)S(1)}, bf16[256,2048]{1,0:T(8,128)(2,1)S(1)}, u32[]{:S(2)}, u32[]{:S(2)}) %collective-permute-start.2) | collective-permute-done | bytes 1048608 | tf_op jit(solution)/shard_map/ppermute | solution.py:236
  55.3 5.7 %collective-permute-start.10 = (bf16[64,2048]{1,0:T(8,128)(2,1)S(1)}, bf16[64,2048]{1,0:T(8,128)(2,1)S(1)}, u32[]{:S(2)}, u32[]{:S(2)}) collective-permute-start(bf16[64,2048]{1,0:T(8,128)(2,1)S(1)} %slice.32), channel_id=1, source_target_pairs={{0,4},{12,8},{1,5},{13,9},{2,6},{14,10},{3,7},{15,11},{16,20},{28,... | collective-permute-start | bytes 786440 | tf_op jit(solution)/shard_map/ppermute | solution.py:247
  62.3 1.3 %collective-permute-start.12 = (f32[96,128]{1,0:T(8,128)S(1)}, f32[96,128]{1,0:T(8,128)S(1)}, u32[]{:S(2)}, u32[]{:S(2)}) collective-permute-start(f32[96,128]{1,0:T(8,128)S(1)} %sum_away.1), channel_id=1, source_target_pairs={{4,0},{8,12},{5,1},{9,13},{6,2},{10,14},{7,3},{11,15},{20,16},{24,... | collective-permute-start | bytes 147464 | tf_op jit(solution)/shard_map/ppermute | solution.py:246
  63.6 1.5 %sum_outer.1.refs_11_ = f32[2,128,64]{2,1,0:T(8,128)S(1)} custom-call(s32[33]{0:T(128)S(1)} %get-tuple-element.19.scalar_ref, bf16[256,2048]{1,0:T(8,128)(2,1)S(1)} %get-tuple-element.20.refs_0_, bf16[256,2048]{1,0:T(8,128)(2,1)S(1)} %collective-permute-done.refs_1_, bf16[256,2048]{1,0:T(8,128)(2,1)S(1)} %collective-permute-done.1.refs_2_, ...), custom_call_target="tpu_custom_call" | custom-call | tf_op jit(solution)/shard_map/sum_outer/pallas_call | solution.py:172
  65.2 2.9 %sum_across.1.refs_5_ = f32[2,128,64]{2,1,0:T(8,128)S(1)} custom-call(s32[33]{0:T(128)S(1)} %get-tuple-element.19.scalar_ref, bf16[256,2048]{1,0:T(8,128)(2,1)S(1)} %get-tuple-element.20.refs_0_, bf16[256,2048]{1,0:T(8,128)(2,1)S(1)} %collective-permute-done.refs_1_, bf16[256,2048]{1,0:T(8,128)(2,1)S(1)} %collective-permute-done.1.refs_2_, ...), custom_call_target="tpu_custom_call" | custom-call | tf_op jit(solution)/shard_map/sum_across/pallas_call | solution.py:172
  68.7 1.4 %collective-permute-start.16 = (f32[32,128]{1,0:T(8,128)S(1)}, f32[32,128]{1,0:T(8,128)S(1)}, u32[]{:S(2)}, u32[]{:S(2)}) collective-permute-start(f32[32,128]{1,0:T(8,128)S(1)} %sum_away_across.1), channel_id=1, source_target_pairs={{4,3},{5,2},{6,1},{7,0},{8,15},{9,14},{10,13},{11,12},{20,19},{21,... | collective-permute-start | bytes 49160 | tf_op jit(solution)/shard_map/ppermute | solution.py:253
  70.1 2.1 %collective-permute-done.5.refs_4_ = bf16[2,64,2048]{2,1,0:T(8,128)(2,1)S(1)} collective-permute-done((bf16[2,64,2048]{2,1,0:T(8,128)(2,1)S(1)}, bf16[2,64,2048]{2,1,0:T(8,128)(2,1)S(1)}, u32[]{:S(2)}, u32[]{:S(2)}) %collective-permute-start.5) | collective-permute-done | bytes 524320 | tf_op jit(solution)/shard_map/ppermute | solution.py:229
  72.8 1.2 %sum_last.1 = (f32[32,128]{1,0:T(8,128)S(1)}, f32[32,128]{1,0:T(8,128)S(1)}, f32[32,128]{1,0:T(8,128)S(1)}, f32[32,128]{1,0:T(8,128)S(1)}) custom-call(s32[33]{0:T(128)S(1)} %get-tuple-element.19.scalar_ref, bf16[256,2048]{1,0:T(8,128)(2,1)S(1)} %get-tuple-element.20.refs_0_, bf16[256,2048]{1,0:T(8,128)(2,1)S(1)} %collective-permute-done.refs_1_, ...), custom_call_target="tpu_custom_call" | custom-call | tf_op jit(solution)/shard_map/sum_last/pallas_call | solution.py:172
  74.0 1.6 %collective-permute-start.14 = (f32[32,128]{1,0:T(8,128)S(1)}, f32[32,128]{1,0:T(8,128)S(1)}, u32[]{:S(2)}, u32[]{:S(2)}) collective-permute-start(f32[32,128]{1,0:T(8,128)S(1)} %get-tuple-element.31), channel_id=1, source_target_pairs={{0,2},{1,3},{2,0},{3,1},{4,6},{5,7},{6,4},{7,5},{8,10},{9,11},{10,... | collective-permute-start | bytes 49160 | tf_op jit(solution)/shard_map/ppermute | solution.py:257
  76.2 0.8 %collective-permute-done.13 = f32[32,128]{1,0:T(8,128)S(1)} collective-permute-done((f32[32,128]{1,0:T(8,128)S(1)}, f32[32,128]{1,0:T(8,128)S(1)}, u32[]{:S(2)}, u32[]{:S(2)}) %collective-permute-start.13) | collective-permute-done | bytes 16416 | tf_op jit(solution)/shard_map/ppermute | solution.py:256
  77.8 0.9 %collective-permute-done.15 = f32[32,128]{1,0:T(8,128)S(1)} collective-permute-done((f32[32,128]{1,0:T(8,128)S(1)}, f32[32,128]{1,0:T(8,128)S(1)}, u32[]{:S(2)}, u32[]{:S(2)}) %collective-permute-start.15) | collective-permute-done | bytes 16416 | tf_op jit(solution)/shard_map/ppermute | solution.py:257
  (37 shorter events, 7.5 us)
Async XLA Ops:
  5.4 8.2 %collective-permute-start = (bf16[256,2048]{1,0:T(8,128)(2,1)S(1)}, bf16[256,2048]{1,0:T(8,128)(2,1)S(1)}, u32[]{:S(2)}, u32[]{:S(2)}) collective-permute-start(bf16[256,2048]{1,0:T(8,128)(2,1)S(1)} %get-tuple-element.23), channel_id=1, source_target_pairs={{0,1},{1,0},{2,3},{3,2},{4,5},{5,4},{6,7},{7,6},{8,9},{9,8},{10,11... | collective-permute-start | bytes 3145736 | tf_op jit(solution)/shard_map/ppermute | solution.py:205
  5.9 21.1 %collective-permute-start.7 = (bf16[4,64,2048]{2,1,0:T(8,128)(2,1)}, bf16[4,64,2048]{2,1,0:T(8,128)(2,1)S(1)}, u32[]{:S(2)}, u32[]{:S(2)}) collective-permute-start(bf16[4,64,2048]{2,1,0:T(8,128)(2,1)} %get-tuple-element.22.refs_2_.refs_3_.refs_4_), channel_id=1, source_target_pairs={{4,8},{8,4},{5,9},{9,5},{6,10},{10,6},{7,11},{11,7},{20,24},{24,20... | collective-permute-start | bytes 3145736 | tf_op jit(solution)/shard_map/ppermute | solution.py:229
  6.7 31.6 %collective-permute-start.1 = (bf16[256,2048]{1,0:T(8,128)(2,1)S(1)}, bf16[256,2048]{1,0:T(8,128)(2,1)S(1)}, u32[]{:S(2)}, u32[]{:S(2)}) collective-permute-start(bf16[256,2048]{1,0:T(8,128)(2,1)S(1)} %get-tuple-element.20.refs_0_), channel_id=1, source_target_pairs={{0,2},{1,3},{2,0},{3,1},{4,6},{5,7},{6,4},{7,5},{8,10},{9,11},{10,... | collective-permute-start | bytes 3145736 | tf_op jit(solution)/shard_map/ppermute | solution.py:234
  9.2 17.1 %collective-permute-start.3 = (bf16[2,64,2048]{2,1,0:T(8,128)(2,1)S(1)}, bf16[2,64,2048]{2,1,0:T(8,128)(2,1)S(1)}, u32[]{:S(2)}, u32[]{:S(2)}) collective-permute-start(bf16[2,64,2048]{2,1,0:T(8,128)(2,1)S(1)} %get-tuple-element.24), channel_id=1, source_target_pairs={{0,4},{4,0},{8,12},{12,8},{1,5},{5,1},{9,13},{13,9},{2,6},{6,2},{1... | collective-permute-start | bytes 1572872 | tf_op jit(solution)/shard_map/ppermute | solution.py:229
  13.6 23.2 %collective-permute-start.6 = (bf16[2,64,2048]{2,1,0:T(8,128)(2,1)S(1)}, bf16[2,64,2048]{2,1,0:T(8,128)(2,1)S(1)}, u32[]{:S(2)}, u32[]{:S(2)}) collective-permute-start(bf16[2,64,2048]{2,1,0:T(8,128)(2,1)S(1)} %get-tuple-element.25), channel_id=1, source_target_pairs={{0,4},{4,0},{8,12},{12,8},{1,5},{5,1},{9,13},{13,9},{2,6},{6,2},{1... | collective-permute-start | bytes 1572872 | tf_op jit(solution)/shard_map/ppermute | solution.py:229
  13.6 1.2 %copy-start = (bf16[4,64,2048]{2,1,0:T(8,128)(2,1)S(1)}, bf16[4,64,2048]{2,1,0:T(8,128)(2,1)}, u32[]{:S(2)}) copy-start(bf16[4,64,2048]{2,1,0:T(8,128)(2,1)} %get-tuple-element.22.refs_2_.refs_3_.refs_4_) | copy-start | bytes 3145732
  16.2 39.1 %collective-permute-start.2 = (bf16[256,2048]{1,0:T(8,128)(2,1)S(1)}, bf16[256,2048]{1,0:T(8,128)(2,1)S(1)}, u32[]{:S(2)}, u32[]{:S(2)}) collective-permute-start(bf16[256,2048]{1,0:T(8,128)(2,1)S(1)} %get-tuple-element.23), channel_id=1, source_target_pairs={{0,3},{1,2},{2,1},{3,0},{4,7},{5,6},{6,5},{7,4},{8,11},{9,10},{10,... | collective-permute-start | bytes 3145736 | tf_op jit(solution)/shard_map/ppermute | solution.py:236
  26.3 20.1 %collective-permute-start.4 = (bf16[2,64,2048]{2,1,0:T(8,128)(2,1)S(1)}, bf16[2,64,2048]{2,1,0:T(8,128)(2,1)S(1)}, u32[]{:S(2)}, u32[]{:S(2)}) collective-permute-start(bf16[2,64,2048]{2,1,0:T(8,128)(2,1)S(1)} %collective-permute-done.3.refs_2_.refs_4_.refs_5_), channel_id=1, source_target_pairs={{4,8},{8,4},{5,9},{9,5},{6,10},{10,6},{7,11},{11,7},{20,24},{24,20... | collective-permute-start | bytes 1572872 | tf_op jit(solution)/shard_map/ppermute | solution.py:229
  27.0 11.2 %copy-start.1 = (bf16[4,64,2048]{2,1,0:T(8,128)(2,1)S(1)}, bf16[4,64,2048]{2,1,0:T(8,128)(2,1)}, u32[]{:S(2)}) copy-start(bf16[4,64,2048]{2,1,0:T(8,128)(2,1)} %get-tuple-element.22.refs_2_.refs_3_.refs_4_) | copy-start | bytes 3145732
  27.1 36.6 %collective-permute-start.9 = (bf16[4,64,2048]{2,1,0:T(8,128)(2,1)S(1)}, bf16[4,64,2048]{2,1,0:T(8,128)(2,1)S(1)}, u32[]{:S(2)}, u32[]{:S(2)}) collective-permute-start(bf16[4,64,2048]{2,1,0:T(8,128)(2,1)S(1)} %collective-permute-done.7.refs_4_.refs_6_.refs_7_), channel_id=1, source_target_pairs={{4,0},{8,12},{5,1},{9,13},{6,2},{10,14},{7,3},{11,15},{20,16},{24,... | collective-permute-start | bytes 3145736 | tf_op jit(solution)/shard_map/ppermute | solution.py:229
  40.4 21.3 %collective-permute-start.11 = (bf16[192,2048]{1,0:T(8,128)(2,1)S(1)}, bf16[192,2048]{1,0:T(8,128)(2,1)S(1)}, u32[]{:S(2)}, u32[]{:S(2)}) collective-permute-start(bf16[192,2048]{1,0:T(8,128)(2,1)S(1)} %pad_maximum_fusion), channel_id=1, source_target_pairs={{0,4},{12,8},{1,5},{13,9},{2,6},{14,10},{3,7},{15,11},{16,20},{28,... | collective-permute-start | bytes 2359304 | tf_op jit(solution)/shard_map/ppermute | solution.py:242
  45.7 15.3 %collective-permute-start.8 = (bf16[2,64,2048]{2,1,0:T(8,128)(2,1)S(1)}, bf16[2,64,2048]{2,1,0:T(8,128)(2,1)S(1)}, u32[]{:S(2)}, u32[]{:S(2)}) collective-permute-start(bf16[2,64,2048]{2,1,0:T(8,128)(2,1)S(1)} %collective-permute-done.6.refs_3_.refs_5_.refs_6_), channel_id=1, source_target_pairs={{4,8},{8,4},{5,9},{9,5},{6,10},{10,6},{7,11},{11,7},{20,24},{24,20... | collective-permute-start | bytes 1572872 | tf_op jit(solution)/shard_map/ppermute | solution.py:229
  46.4 25.8 %collective-permute-start.5 = (bf16[2,64,2048]{2,1,0:T(8,128)(2,1)S(1)}, bf16[2,64,2048]{2,1,0:T(8,128)(2,1)S(1)}, u32[]{:S(2)}, u32[]{:S(2)}) collective-permute-start(bf16[2,64,2048]{2,1,0:T(8,128)(2,1)S(1)} %collective-permute-done.4.refs_3_.refs_8_), channel_id=1, source_target_pairs={{4,0},{8,12},{5,1},{9,13},{6,2},{10,14},{7,3},{11,15},{20,16},{24,... | collective-permute-start | bytes 1572872 | tf_op jit(solution)/shard_map/ppermute | solution.py:229
  55.3 12.7 %collective-permute-start.10 = (bf16[64,2048]{1,0:T(8,128)(2,1)S(1)}, bf16[64,2048]{1,0:T(8,128)(2,1)S(1)}, u32[]{:S(2)}, u32[]{:S(2)}) collective-permute-start(bf16[64,2048]{1,0:T(8,128)(2,1)S(1)} %slice.32), channel_id=1, source_target_pairs={{0,4},{12,8},{1,5},{13,9},{2,6},{14,10},{3,7},{15,11},{16,20},{28,... | collective-permute-start | bytes 786440 | tf_op jit(solution)/shard_map/ppermute | solution.py:247
  62.3 10.4 %collective-permute-start.12 = (f32[96,128]{1,0:T(8,128)S(1)}, f32[96,128]{1,0:T(8,128)S(1)}, u32[]{:S(2)}, u32[]{:S(2)}) collective-permute-start(f32[96,128]{1,0:T(8,128)S(1)} %sum_away.1), channel_id=1, source_target_pairs={{4,0},{8,12},{5,1},{9,13},{6,2},{10,14},{7,3},{11,15},{20,16},{24,... | collective-permute-start | bytes 147464 | tf_op jit(solution)/shard_map/ppermute | solution.py:246
  68.7 7.5 %copy-start.2 = (s32[32]{0:T(128)S(1)}, s32[32]{0:T(128)}, u32[]{:S(2)}) copy-start(s32[32]{0:T(128)} %param.7) | copy-start | bytes 388
  68.7 10.0 %collective-permute-start.16 = (f32[32,128]{1,0:T(8,128)S(1)}, f32[32,128]{1,0:T(8,128)S(1)}, u32[]{:S(2)}, u32[]{:S(2)}) collective-permute-start(f32[32,128]{1,0:T(8,128)S(1)} %sum_away_across.1), channel_id=1, source_target_pairs={{4,3},{5,2},{6,1},{7,0},{8,15},{9,14},{10,13},{11,12},{20,19},{21,... | collective-permute-start | bytes 49160 | tf_op jit(solution)/shard_map/ppermute | solution.py:253
  74.0 3.8 %collective-permute-start.14 = (f32[32,128]{1,0:T(8,128)S(1)}, f32[32,128]{1,0:T(8,128)S(1)}, u32[]{:S(2)}, u32[]{:S(2)}) collective-permute-start(f32[32,128]{1,0:T(8,128)S(1)} %get-tuple-element.31), channel_id=1, source_target_pairs={{0,2},{1,3},{2,0},{3,1},{4,6},{5,7},{6,4},{7,5},{8,10},{9,11},{10,... | collective-permute-start | bytes 49160 | tf_op jit(solution)/shard_map/ppermute | solution.py:257
  75.5 3.2 %collective-permute-start.15 = (f32[32,128]{1,0:T(8,128)S(1)}, f32[32,128]{1,0:T(8,128)S(1)}, u32[]{:S(2)}, u32[]{:S(2)}) collective-permute-start(f32[32,128]{1,0:T(8,128)S(1)} %get-tuple-element.32), channel_id=1, source_target_pairs={{0,3},{1,2},{2,1},{3,0},{4,7},{5,6},{6,5},{7,4},{8,11},{9,10},{10,... | collective-permute-start | bytes 49160 | tf_op jit(solution)/shard_map/ppermute | solution.py:257
  75.5 1.5 %collective-permute-start.13 = (f32[32,128]{1,0:T(8,128)S(1)}, f32[32,128]{1,0:T(8,128)S(1)}, u32[]{:S(2)}, u32[]{:S(2)}) collective-permute-start(f32[32,128]{1,0:T(8,128)S(1)} %get-tuple-element.30), channel_id=1, source_target_pairs={{0,1},{1,0},{2,3},{3,2},{4,5},{5,4},{6,7},{7,6},{8,9},{9,8},{10,11... | collective-permute-start | bytes 49160 | tf_op jit(solution)/shard_map/ppermute | solution.py:256

commit v4 on v3

--- a/solution.py
+++ b/solution.py
@@ -8,7 +8,7 @@
 from jax.sharding import PartitionSpec as P
 
 VMEM_LIMIT = 12 * 1024 * 1024
-PREPARE_VMEM = 50 * 1024 * 1024
+OWN_VMEM = 52 * 1024 * 1024
 NT = (((1,), (1,)), ((), ()))
 SWAP = [(0, 1), (1, 0)]
 NEAR = [(0, 1), (1, 0), (2, 3), (3, 2)]
@@ -36,23 +36,36 @@
     return lax.psum_scatter(partial_sums, "pair", scatter_dimension=0, tiled=True)
 
 
-def prepare_kernel(rows, slots, scalar_ref, x_ref, integrals_ref, other_ref, mine_ref, own_ref, first_ref, second_ref, table_ref, held_ref, pick_ref, copied, loaded):
-    steps, _, width = held_ref.shape
-    half = first_ref.shape[2]
-    core = scalar_ref[1]
-    moves, loads = [], []
-    held = own_ref.shape[0]
+def own_half_kernel(integrals_ref, own_ref, copied):
+    held, _, half = own_ref.shape
+    core = lax.axis_index("rep")
+    moves = []
     for p in range(held):
         start = pl.multiple_of((2 * p + core) * half, half)
-        source = integrals_ref.at[:, pl.ds(start, half)]
-        moves.append(pltpu.make_async_copy(source, own_ref.at[p], copied.at[p]))
-    for i in range(steps):
-        half_here = core if i < steps // 2 else 1 - core
-        start = pl.multiple_of(half_here * half + i % (steps // 2) * width, width)
-        loads.append(pltpu.make_async_copy(x_ref.at[:, pl.ds(start, width)], held_ref.at[i], loaded.at[i]))
-    for move in moves + loads:
+        moves.append(pltpu.make_async_copy(integrals_ref.at[:, pl.ds(start, half)], own_ref.at[p], copied.at[p]))
+    for move in moves:
         move.start()
-
+    for move in moves:
+        move.wait()
+
+
+def own_half(integrals, tile):
+    ab, columns = integrals.shape
+    held, half = columns // tile, tile // 2
+    return pl.pallas_call(
+        own_half_kernel,
+        in_specs=[pl.BlockSpec(memory_space=pltpu.HBM)],
+        out_specs=pl.BlockSpec(memory_space=pltpu.VMEM),
+        out_shape=jax.ShapeDtypeStruct((held, ab, half), integrals.dtype),
+        scratch_shapes=[pltpu.SemaphoreType.DMA((held,))],
+        compiler_params=pltpu.CompilerParams(vmem_limit_bytes=OWN_VMEM),
+        name="own_half",
+    )(integrals)
+
+
+def pack_kernel(rows, slots, held, width, scalar_ref, x_ref, other_ref, mine_ref, table_ref, pick_ref):
+    half = mine_ref.shape[1]
+    core = scalar_ref[1]
     groups, picked, per_group = pick_ref.shape
     group = per_group // slots
     lane = lax.broadcasted_iota(jnp.int32, (1, per_group), 1)
@@ -82,50 +95,33 @@
         target = jnp.where(lane_irrep == row_irrep, lane_rank * group + row_lane, -1)
         pick_ref[g] = jnp.where(row == target, 1.0, 0.0).astype(pick_ref.dtype)
 
-    for i in range(steps):
-        loads[i].wait()
-        into = mine_ref if i < steps // 2 else other_ref
-        at = i % (steps // 2) * width
+    for i in range(2 * half // width):
+        into = mine_ref if i < half // width else other_ref
+        at = i % (half // width) * width
+        start = pl.multiple_of((core if i < half // width else 1 - core) * half + at, width)
         for g in range(groups):
-            source = held_ref[i, g * per_group : (g + 1) * per_group]
-            packed = jnp.dot(pick_ref[g], source, preferred_element_type=jnp.float32).astype(held_ref.dtype)
+            source = x_ref[g * per_group : (g + 1) * per_group, pl.ds(start, width)]
+            packed = jnp.dot(pick_ref[g], source, preferred_element_type=jnp.float32).astype(x_ref.dtype)
             for j in range(picked // group):
                 to = j * rows + g * group
                 into[to : to + group, at : at + width] = packed[j * group : (j + 1) * group]
-    for p, move in enumerate(moves):
-        move.wait()
-        chunk_ref = first_ref if p < held // 2 else second_ref
-        chunk_ref[p % (held // 2)] = own_ref[p]
-
-
-def prepare(scalars, amplitudes, integrals, steps=8):
+
+
+def pack(scalars, amplitudes, held):
     rows, slots, tile = amplitudes.shape
     live, half = slots // 2, tile // 2
-    ab, columns = integrals.shape
-    held = columns // tile
     packed = jax.ShapeDtypeStruct((live * rows, half), amplitudes.dtype)
-    whole = jax.ShapeDtypeStruct((held, ab, half), integrals.dtype)
-    chunk = jax.ShapeDtypeStruct((held // 2, ab, half), integrals.dtype)
-    hbm = pl.BlockSpec(memory_space=pltpu.HBM)
     vmem = pl.BlockSpec(memory_space=pltpu.VMEM)
     smem = pl.BlockSpec(memory_space=pltpu.SMEM)
     return pl.pallas_call(
-        functools.partial(prepare_kernel, rows, slots),
-        in_specs=[smem, hbm, hbm],
-        out_specs=[vmem, vmem, vmem, vmem, vmem, smem],
-        out_shape=[packed, packed, whole, chunk, chunk, jax.ShapeDtypeStruct((2 * slots + 1,), jnp.int32)],
-        scratch_shapes=[
-            pltpu.VMEM((steps, rows * slots, tile // steps), amplitudes.dtype),
-            pltpu.VMEM((rows // 16, live * 16, 16 * slots), amplitudes.dtype),
-            pltpu.SemaphoreType.DMA((held,)),
-            pltpu.SemaphoreType.DMA((steps,)),
-        ],
-        compiler_params=pltpu.CompilerParams(vmem_limit_bytes=PREPARE_VMEM),
-        cost_estimate=pl.CostEstimate(
-            flops=2 * live * rows * rows * slots * tile, bytes_accessed=3 * rows * slots * tile, transcendentals=0
-        ),
-        name="prepare",
-    )(scalars, amplitudes.reshape(rows * slots, tile), integrals)
+        functools.partial(pack_kernel, rows, slots, held, half // 4),
+        in_specs=[smem, vmem],
+        out_specs=[vmem, vmem, smem],
+        out_shape=[packed, packed, jax.ShapeDtypeStruct((2 * slots + 1,), jnp.int32)],
+        scratch_shapes=[pltpu.VMEM((rows // 16, live * 16, 16 * slots), amplitudes.dtype)],
+        compiler_params=pltpu.CompilerParams(vmem_limit_bytes=VMEM_LIMIT),
+        name="pack",
+    )(scalars, amplitudes.reshape(rows * slots, tile))
 
 
 def sum_kernel(rows, slots, tiles, work, table, ends, extra, scalar_ref, *refs):
@@ -191,7 +187,8 @@
     across = [(i, 3 - i) for i in range(4)]
     beside = [(i, i ^ 2) for i in range(4)]
 
-    other, mine, own, first, second, scalars = prepare(scalars, amplitudes, integrals)
+    own = own_half(integrals, tile)
+    other, mine, scalars = pack(after(scalars, own), amplitudes, integrals.shape[1] // tile)
     held = slots // 4
     per = held // 2
 
@@ -201,7 +198,7 @@
     home, near = (0, 1, 2, 3), (1, 0, 3, 2)
     middle, beyond = (None, 2, 1, None), (None, 3, 0, None)
     outer, outermost = (2, None, None, 1), (3, None, None, 0)
-    chunks = {"own": (own, held_at(home)), "own1": (first, ()), "own2": (second, ())}
+    chunks = {"own": (own, held_at(home))}
     tiles = [mine, lax.ppermute(other, "rep", SWAP)]
 
     def add(name, *step, arrays=None, at=None, blocks=4, extra=(), ends=0):
@@ -225,30 +222,31 @@
             name=name,
         )
 
-    def send(name, source, pairs, positions, *earlier):
-        chunks[name] = (lax.ppermute(after(chunks[source][0], *earlier), "pair", pairs), positions)
-
-    send("near1", "own1", NEAR, held_at(near, 0, per))
-    send("mid", "own", MIDDLE, held_at(middle))
-    send("near2", "own2", NEAR, held_at(near, per))
+    def send(name, array, pairs, positions, *earlier):
+        chunks[name] = (lax.ppermute(after(array, *earlier), "pair", pairs), positions)
+        return chunks[name][0]
+
+    low = per * rows
+    near_chunk = send("near", own, NEAR, held_at(near))
+    mid_chunk = send("mid", own, MIDDLE, held_at(middle))
     tiles.append(lax.ppermute(mine, ("ints", "rep"), beside))
-    sums = add("sum_home", (0, 2, ("own",)))
-    tiles.append(lax.ppermute(after(other, sums), ("ints", "rep"), across))
-    send("mid3", "near1", MIDDLE, held_at(beyond, 0, per))
-    send("out", "mid", OUTWARD, held_at(outer))
-    send("mid4", "near2", MIDDLE, held_at(beyond, per))
-    sums = add("sum_near", (0, 2, ("near1", "near2", "mid")), extra=(sums,))
-    sums = add("sum_side", (2, 3, ("own", "near1", "near2", "mid")), extra=(sums,))
-    heads = lax.ppermute(after(jnp.concatenate([t[: per * rows] for t in tiles[:3]]), sums), "pair", INWARD)
-    send("out3", "mid3", OUTWARD, held_at(outermost, 0, per))
-    sums = add("sum_beyond", (0, 3, ("mid3", "mid4")), extra=(sums,))
-    away = add("sum_away", (0, 3, ("mid4",)), arrays=[after(heads, sums)], at=[(0, t * per * rows) for t in range(3)], blocks=3, ends=1)
+    tiles.append(lax.ppermute(other, ("ints", "rep"), across))
+    mid3_chunk = send("mid3", near_chunk[:per], MIDDLE, held_at(beyond, 0, per))
+    send("out", mid_chunk, OUTWARD, held_at(outer))
+    send("mid4", near_chunk[per:], MIDDLE, held_at(beyond, per))
+    first = ("own", "mid", "near")
+    sums = add("sum_near", (0, 1, first))
+    sums = add("sum_side", (1, 3, first), extra=(sums,))
+    heads = jnp.concatenate([t[:low] for t in tiles[:3]])
+    heads = lax.ppermute(after(heads, sums), "pair", INWARD)
+    send("out3", mid3_chunk, OUTWARD, held_at(outermost, 0, per), sums)
+    last_heads = lax.ppermute(tiles[3][:low], "pair", INWARD)
+    sums = add("sum_across", (3, 4, first), extra=(sums,))
+    rows_at = [(0, t * low) for t in range(3)]
+    away = add("sum_away", (0, 3, ("mid4",)), arrays=[after(heads, sums)], at=rows_at, blocks=3, ends=1)
     back = lax.ppermute(away[0], "pair", OUTWARD)
-    last_heads = lax.ppermute(tiles[3][: per * rows], "pair", INWARD)
-    sums = add("sum_outer", (0, 3, ("out",)), extra=(sums,))
-    everything = ("own", "near1", "near2", "mid", "mid3", "mid4", "out")
-    sums = add("sum_across", (3, 4, everything), extra=(sums,))
-    away = add("sum_away_across", (0, 1, ("mid4",)), arrays=[last_heads], at=[(0, 0)], blocks=1, ends=1)
+    sums = add("sum_beyond", (0, 4, ("mid3", "mid4", "out")), extra=(sums,))
+    away = add("sum_last_away", (0, 1, ("mid4",)), arrays=[after(last_heads, sums)], at=[(0, 0)], blocks=1, ends=1)
     home_pairs = [(4 * a + i, 4 * b + 3 - i) for a, b in OUTWARD for i in range(4)]
     back_across = lax.ppermute(away[0], ("pair", "ints", "rep"), home_pairs)
     sums = add("sum_last", (0, 4, ("out3",)), extra=(after(sums, away[0]), back), ends=4)

time: 79.8 us -> 76.6 us (0.960)
  Pallas kernels: 16.9 us -> 13.6 us
    ppermute x1, waiting for transfers between devices: 0.01 us -> 3.65 us  [on_line(): tiles.append(lax.ppermute(mine, ('ints', 'rep'), beside))]
    ppermute x10 -> x9, waiting for transfers between devices: 28.1 us -> 25.3 us  [the longest x6 16.1 us: send(): lax.ppermute(after(array, *earlier), 'pair', pairs)]
    pallas_call x9 -> x7, Pallas kernels: 12.2 us -> 10.6 us  [add_positions(): pl.pallas_call(functools.partial(sum_kernel, rows, slots, tuple(tiles), w...]
    pallas_call x1 -> x2, Pallas kernels: 4.65 us -> 3.02 us  [the longest x1 1.76 us: pack(): pl.pallas_call(functools.partial(pack_kernel, rows, slots, held, half //...]
    ppermute x10 -> x9, starting transfers between devices: 20.3 us -> 21.6 us  [the longest x6 7.78 us: send(): lax.ppermute(after(array, *earlier), 'pair', pairs)]
    ppermute x1, starting transfers between devices: 1.55 us -> 0.4 us  [on_line(): lax.ppermute(sums[2], ('ints', 'rep'), beside)]
    ppermute x1, starting transfers between devices: 2.58 us -> 1.55 us  [on_line(): tiles.append(lax.ppermute(mine, ('ints', 'rep'), beside))]
    ppermute x1, starting transfers between devices: 0.01 us -> 1 us  [on_line(): lax.ppermute(sums[3], ('ints', 'rep'), across)]
  transfers between devices with their start and end apart: 17 -> 16, of which waited for: 9 -> 7; matrix products, arithmetic and copies ran while one was open for 0% -> 0% of each run, Pallas kernels for 15% -> 16%
where the time goes in v4:
time: 76.6 us; the launch traced here: 76.2 us
  waiting for transfers between devices  31.2 us (41%)
  starting transfers between devices  27.9 us (36%)
  Pallas kernels  13.6 us (18%)
  local copies, waits for them, and re-layouts  2.43 us (3%)
  other arithmetic  0.86 us (1%)
    ppermute x6, waiting for transfers between devices, send(): lax.ppermute(after(array, *earlier), 'pair', pairs)  16.1 us
    pallas_call x7, Pallas kernels, add_positions(): pl.pallas_call(functools.partial(sum_kernel, rows, slots, tuple(tiles), w...  10.6 us
    ppermute x1, waiting for transfers between devices, on_line(): tiles.append(lax.ppermute(other, ('ints', 'rep'), across))  8.42 us
    ppermute x6, starting transfers between devices, send(): lax.ppermute(after(array, *earlier), 'pair', pairs)  7.78 us
    ppermute x1, starting transfers between devices, on_line(): heads = lax.ppermute(after(heads, sums), 'pair', INWARD)  7.15 us
    ppermute x1, starting transfers between devices, on_line(): last_heads = lax.ppermute(tiles[3][:low], 'pair', INWARD)  5.97 us
    ppermute x1, waiting for transfers between devices, on_line(): tiles.append(lax.ppermute(mine, ('ints', 'rep'), beside))  3.65 us
    unnamed x8, local copies, waits for them, and re-layouts  2.21 us
  transfers between devices with their start and end apart: 16, of which 7 were waited for; matrix products, arithmetic and copies ran while one was open for 0% of the time, Pallas kernels for 16%

profile of v4, /device:TPU:0, one launch (start us, length us, event | category | flops | bytes accessed | tf_op | source)
XLA Modules:
  0.0 76.2 jit_solution(2522437911764937131)
XLA Ops:
  0.0 1.3 %own_half.1.refs_1_.refs_3_.refs_4_ = bf16[4,64,2048]{2,1,0:T(8,128)(2,1)S(1)} custom-call(bf16[64,16384]{1,0:T(8,128)(2,1)} %integrals_ref.1), custom_call_target="tpu_custom_call" | custom-call | tf_op jit(solution)/shard_map/own_half/pallas_call | solution.py:55
  1.3 3.1 %collective-permute-start.3 = (bf16[4,64,2048]{2,1,0:T(8,128)(2,1)S(1)}, bf16[4,64,2048]{2,1,0:T(8,128)(2,1)S(1)}, u32[]{:S(2)}, u32[]{:S(2)}) collective-permute-start(bf16[4,64,2048]{2,1,0:T(8,128)(2,1)S(1)} %own_half.1.refs_1_.refs_3_.refs_4_), channel_id=1, source_target_pairs={{0,4},{4,0},{8,12},{12,8},{1,5},{5,1},{9,13},{13,9},{2,6},{6,2},{1... | collective-permute-start | bytes 3145736 | tf_op jit(solution)/shard_map/ppermute | solution.py:226
  5.2 2.2 %copy-done = bf16[32,16,4096]{2,1,0:T(8,128)(2,1)S(1)} copy-done((bf16[32,16,4096]{2,1,0:T(8,128)(2,1)S(1)}, bf16[32,16,4096]{2,1,0:T(8,128)(2,1)}, u32[]{:S(2)}) %copy-start) | copy-done | bytes 4194328
  7.4 1.8 %pack.1 = (bf16[256,2048]{1,0:T(8,128)(2,1)S(1)}, bf16[256,2048]{1,0:T(8,128)(2,1)S(1)}, s32[33]{0:T(128)S(1)}) custom-call(s32[66]{0:T(128)S(1)} %concatenate.12.scalar_ref, bf16[512,4096]{1,0:T(8,128)(2,1)S(1)} %bitcast.3), custom_call_target="tpu_custom_call" | custom-call | tf_op jit(solution)/shard_map/pack/pallas_call | solution.py:116
  9.2 1.6 %collective-permute-start.1 = (bf16[256,2048]{1,0:T(8,128)(2,1)S(1)}, bf16[256,2048]{1,0:T(8,128)(2,1)S(1)}, u32[]{:S(2)}, u32[]{:S(2)}) collective-permute-start(bf16[256,2048]{1,0:T(8,128)(2,1)S(1)} %get-tuple-element.20.refs_0_), channel_id=1, source_target_pairs={{0,2},{1,3},{2,0},{3,1},{4,6},{5,7},{6,4},{7,5},{8,10},{9,11},{10,... | collective-permute-start | bytes 3145736 | tf_op jit(solution)/shard_map/ppermute | solution.py:232
  11.4 16.1 %collective-permute-done.3.refs_3_.refs_5_.refs_6_ = bf16[4,64,2048]{2,1,0:T(8,128)(2,1)S(1)} collective-permute-done((bf16[4,64,2048]{2,1,0:T(8,128)(2,1)S(1)}, bf16[4,64,2048]{2,1,0:T(8,128)(2,1)S(1)}, u32[]{:S(2)}, u32[]{:S(2)}) %collective-permute-start.3) | collective-permute-done | bytes 1048608 | tf_op jit(solution)/shard_map/ppermute | solution.py:226
  28.3 1.3 %collective-permute-start.8 = (bf16[4,64,2048]{2,1,0:T(8,128)(2,1)S(1)}, bf16[4,64,2048]{2,1,0:T(8,128)(2,1)S(1)}, u32[]{:S(2)}, u32[]{:S(2)}) collective-permute-start(bf16[4,64,2048]{2,1,0:T(8,128)(2,1)S(1)} %collective-permute-done.5.refs_2_.refs_4_.refs_5_), channel_id=1, source_target_pairs={{4,0},{8,12},{5,1},{9,13},{6,2},{10,14},{7,3},{11,15},{20,16},{24,... | collective-permute-start | bytes 3145736 | tf_op jit(solution)/shard_map/ppermute | solution.py:226
  29.6 2.1 %sum_near.1.refs_6_ = f32[2,128,64]{2,1,0:T(8,128)S(1)} custom-call(s32[33]{0:T(128)S(1)} %get-tuple-element.19.scalar_ref, bf16[256,2048]{1,0:T(8,128)(2,1)S(1)} %get-tuple-element.20.refs_0_, bf16[4,64,2048]{2,1,0:T(8,128)(2,1)S(1)} %own_half.1.refs_1_.refs_3_.refs_4_, bf16[4,64,2048]{2,1,0:T(8,128)(2,1)S(1)} %collective-permute-done.5.refs_2_.refs_4_.refs_5_, ...), custom_call_target="tpu_custom_call" | custom-call | tf_op jit(solution)/shard_map/sum_near/pallas_call | solution.py:168
  31.7 3.6 %collective-permute-done.1.refs_2_ = bf16[256,2048]{1,0:T(8,128)(2,1)S(1)} collective-permute-done((bf16[256,2048]{1,0:T(8,128)(2,1)S(1)}, bf16[256,2048]{1,0:T(8,128)(2,1)S(1)}, u32[]{:S(2)}, u32[]{:S(2)}) %collective-permute-start.1) | collective-permute-done | bytes 1048608 | tf_op jit(solution)/shard_map/ppermute | solution.py:232
  35.4 2.3 %sum_side.1.refs_7_ = f32[2,128,64]{2,1,0:T(8,128)S(1)} custom-call(s32[33]{0:T(128)S(1)} %get-tuple-element.19.scalar_ref, bf16[256,2048]{1,0:T(8,128)(2,1)S(1)} %get-tuple-element.20.refs_0_, bf16[256,2048]{1,0:T(8,128)(2,1)S(1)} %collective-permute-done.refs_1_, bf16[256,2048]{1,0:T(8,128)(2,1)S(1)} %collective-permute-done.1.refs_2_, ...), custom_call_target="tpu_custom_call" | custom-call | tf_op jit(solution)/shard_map/sum_side/pallas_call | solution.py:168
  37.7 7.2 %collective-permute-start.10 = (bf16[192,2048]{1,0:T(8,128)(2,1)S(1)}, bf16[192,2048]{1,0:T(8,128)(2,1)S(1)}, u32[]{:S(2)}, u32[]{:S(2)}) collective-permute-start(bf16[192,2048]{1,0:T(8,128)(2,1)S(1)} %pad_maximum_fusion), channel_id=1, source_target_pairs={{0,4},{12,8},{1,5},{13,9},{2,6},{14,10},{3,7},{15,11},{16,20},{28,... | collective-permute-start | bytes 2359304 | tf_op jit(solution)/shard_map/ppermute | solution.py:241
  45.6 1.3 %collective-permute-start.6 = (bf16[2,64,2048]{2,1,0:T(8,128)(2,1)S(1)}, bf16[2,64,2048]{2,1,0:T(8,128)(2,1)S(1)}, u32[]{:S(2)}, u32[]{:S(2)}) collective-permute-start(bf16[2,64,2048]{2,1,0:T(8,128)(2,1)S(1)} %collective-permute-done.4.refs_4_), channel_id=1, source_target_pairs={{4,0},{8,12},{5,1},{9,13},{6,2},{10,14},{7,3},{11,15},{20,16},{24,... | collective-permute-start | bytes 1572872 | tf_op jit(solution)/shard_map/ppermute | solution.py:226
  46.9 8.4 %collective-permute-done.2.refs_3_ = bf16[256,2048]{1,0:T(8,128)(2,1)S(1)} collective-permute-done((bf16[256,2048]{1,0:T(8,128)(2,1)S(1)}, bf16[256,2048]{1,0:T(8,128)(2,1)S(1)}, u32[]{:S(2)}, u32[]{:S(2)}) %collective-permute-start.2) | collective-permute-done | bytes 1048608 | tf_op jit(solution)/shard_map/ppermute | solution.py:233
  55.4 6.0 %collective-permute-start.9 = (bf16[64,2048]{1,0:T(8,128)(2,1)S(1)}, bf16[64,2048]{1,0:T(8,128)(2,1)S(1)}, u32[]{:S(2)}, u32[]{:S(2)}) collective-permute-start(bf16[64,2048]{1,0:T(8,128)(2,1)S(1)} %slice.42), channel_id=1, source_target_pairs={{0,4},{12,8},{1,5},{13,9},{2,6},{14,10},{3,7},{15,11},{16,20},{28,... | collective-permute-start | bytes 786440 | tf_op jit(solution)/shard_map/ppermute | solution.py:243
  61.3 2.1 %sum_across.1.refs_7_ = f32[2,128,64]{2,1,0:T(8,128)S(1)} custom-call(s32[33]{0:T(128)S(1)} %get-tuple-element.19.scalar_ref, bf16[256,2048]{1,0:T(8,128)(2,1)S(1)} %get-tuple-element.20.refs_0_, bf16[256,2048]{1,0:T(8,128)(2,1)S(1)} %collective-permute-done.refs_1_, bf16[256,2048]{1,0:T(8,128)(2,1)S(1)} %collective-permute-done.1.refs_2_, ...), custom_call_target="tpu_custom_call" | custom-call | tf_op jit(solution)/shard_map/sum_across/pallas_call | solution.py:168
  64.1 1.3 %collective-permute-start.11 = (f32[96,128]{1,0:T(8,128)S(1)}, f32[96,128]{1,0:T(8,128)S(1)}, u32[]{:S(2)}, u32[]{:S(2)}) collective-permute-start(f32[96,128]{1,0:T(8,128)S(1)} %sum_away.1), channel_id=1, source_target_pairs={{4,0},{8,12},{5,1},{9,13},{6,2},{10,14},{7,3},{11,15},{20,16},{24,... | collective-permute-start | bytes 147464 | tf_op jit(solution)/shard_map/ppermute | solution.py:247
  65.4 1.7 %sum_beyond.1.refs_5_ = f32[2,128,64]{2,1,0:T(8,128)S(1)} custom-call(s32[33]{0:T(128)S(1)} %get-tuple-element.19.scalar_ref, bf16[256,2048]{1,0:T(8,128)(2,1)S(1)} %get-tuple-element.20.refs_0_, bf16[256,2048]{1,0:T(8,128)(2,1)S(1)} %collective-permute-done.refs_1_, bf16[256,2048]{1,0:T(8,128)(2,1)S(1)} %collective-permute-done.1.refs_2_, ...), custom_call_target="tpu_custom_call" | custom-call | tf_op jit(solution)/shard_map/sum_beyond/pallas_call | solution.py:168
  67.1 0.8 %collective-permute-done.9.refs_0_ = bf16[64,2048]{1,0:T(8,128)(2,1)S(1)} collective-permute-done((bf16[64,2048]{1,0:T(8,128)(2,1)S(1)}, bf16[64,2048]{1,0:T(8,128)(2,1)S(1)}, u32[]{:S(2)}, u32[]{:S(2)}) %collective-permute-start.9) | collective-permute-done | bytes 262176 | tf_op jit(solution)/shard_map/ppermute | solution.py:243
  68.5 1.3 %collective-permute-start.15 = (f32[32,128]{1,0:T(8,128)S(1)}, f32[32,128]{1,0:T(8,128)S(1)}, u32[]{:S(2)}, u32[]{:S(2)}) collective-permute-start(f32[32,128]{1,0:T(8,128)S(1)} %sum_last_away.1), channel_id=1, source_target_pairs={{4,3},{5,2},{6,1},{7,0},{8,15},{9,14},{10,13},{11,12},{20,19},{21,... | collective-permute-start | bytes 49160 | tf_op jit(solution)/shard_map/ppermute | solution.py:251
  70.4 1.2 %sum_last.1 = (f32[32,128]{1,0:T(8,128)S(1)}, f32[32,128]{1,0:T(8,128)S(1)}, f32[32,128]{1,0:T(8,128)S(1)}, f32[32,128]{1,0:T(8,128)S(1)}) custom-call(s32[33]{0:T(128)S(1)} %get-tuple-element.19.scalar_ref, bf16[256,2048]{1,0:T(8,128)(2,1)S(1)} %get-tuple-element.20.refs_0_, bf16[256,2048]{1,0:T(8,128)(2,1)S(1)} %collective-permute-done.refs_1_, ...), custom_call_target="tpu_custom_call" | custom-call | tf_op jit(solution)/shard_map/sum_last/pallas_call | solution.py:168
  72.0 1.0 %collective-permute-start.14 = (f32[32,128]{1,0:T(8,128)S(1)}, f32[32,128]{1,0:T(8,128)S(1)}, u32[]{:S(2)}, u32[]{:S(2)}) collective-permute-start(f32[32,128]{1,0:T(8,128)S(1)} %get-tuple-element.30), channel_id=1, source_target_pairs={{0,3},{1,2},{2,1},{3,0},{4,7},{5,6},{6,5},{7,4},{8,11},{9,10},{10,... | collective-permute-start | bytes 49160 | tf_op jit(solution)/shard_map/ppermute | solution.py:255
  73.0 0.8 %collective-permute-start.12 = (f32[32,128]{1,0:T(8,128)S(1)}, f32[32,128]{1,0:T(8,128)S(1)}, u32[]{:S(2)}, u32[]{:S(2)}) collective-permute-start(f32[32,128]{1,0:T(8,128)S(1)} %get-tuple-element.28), channel_id=1, source_target_pairs={{0,1},{1,0},{2,3},{3,2},{4,5},{5,4},{6,7},{7,6},{8,9},{9,8},{10,11... | collective-permute-start | bytes 49160 | tf_op jit(solution)/shard_map/ppermute | solution.py:254
  73.9 0.8 %collective-permute-done.12 = f32[32,128]{1,0:T(8,128)S(1)} collective-permute-done((f32[32,128]{1,0:T(8,128)S(1)}, f32[32,128]{1,0:T(8,128)S(1)}, u32[]{:S(2)}, u32[]{:S(2)}) %collective-permute-start.12) | collective-permute-done | bytes 16416 | tf_op jit(solution)/shard_map/ppermute | solution.py:254
  74.7 0.8 collective-permute-done.13
  (37 shorter events, 6.2 us)
Async XLA Ops:
  0.0 5.1 %copy-start.3 = (s32[32]{0:T(128)S(1)}, s32[32]{0:T(128)}, u32[]{:S(2)}) copy-start(s32[32]{0:T(128)} %param.7) | copy-start | bytes 388
  0.0 5.1 %copy-start.1 = (s32[16]{0:T(128)S(1)}, s32[16]{0:T(128)}, u32[]{:S(2)}) copy-start(s32[16]{0:T(128)} %param.8) | copy-start | bytes 196
  0.0 5.1 %copy-start.2 = (s32[16]{0:T(128)S(1)}, s32[16]{0:T(128)}, u32[]{:S(2)}) copy-start(s32[16]{0:T(128)} %param.9) | copy-start | bytes 196
  1.3 26.2 %collective-permute-start.3 = (bf16[4,64,2048]{2,1,0:T(8,128)(2,1)S(1)}, bf16[4,64,2048]{2,1,0:T(8,128)(2,1)S(1)}, u32[]{:S(2)}, u32[]{:S(2)}) collective-permute-start(bf16[4,64,2048]{2,1,0:T(8,128)(2,1)S(1)} %own_half.1.refs_1_.refs_3_.refs_4_), channel_id=1, source_target_pairs={{0,4},{4,0},{8,12},{12,8},{1,5},{5,1},{9,13},{13,9},{2,6},{6,2},{1... | collective-permute-start | bytes 3145736 | tf_op jit(solution)/shard_map/ppermute | solution.py:226
  4.4 23.9 %collective-permute-start.5 = (bf16[4,64,2048]{2,1,0:T(8,128)(2,1)S(1)}, bf16[4,64,2048]{2,1,0:T(8,128)(2,1)S(1)}, u32[]{:S(2)}, u32[]{:S(2)}) collective-permute-start(bf16[4,64,2048]{2,1,0:T(8,128)(2,1)S(1)} %own_half.1.refs_1_.refs_3_.refs_4_), channel_id=1, source_target_pairs={{4,8},{8,4},{5,9},{9,5},{6,10},{10,6},{7,11},{11,7},{20,24},{24,20... | collective-permute-start | bytes 3145736 | tf_op jit(solution)/shard_map/ppermute | solution.py:226
  5.2 2.2 %copy-start = (bf16[32,16,4096]{2,1,0:T(8,128)(2,1)S(1)}, bf16[32,16,4096]{2,1,0:T(8,128)(2,1)}, u32[]{:S(2)}) copy-start(bf16[32,16,4096]{2,1,0:T(8,128)(2,1)} %param.5) | copy-start | bytes 12582916
  9.2 26.1 %collective-permute-start.1 = (bf16[256,2048]{1,0:T(8,128)(2,1)S(1)}, bf16[256,2048]{1,0:T(8,128)(2,1)S(1)}, u32[]{:S(2)}, u32[]{:S(2)}) collective-permute-start(bf16[256,2048]{1,0:T(8,128)(2,1)S(1)} %get-tuple-element.20.refs_0_), channel_id=1, source_target_pairs={{0,2},{1,3},{2,0},{3,1},{4,6},{5,7},{6,4},{7,5},{8,10},{9,11},{10,... | collective-permute-start | bytes 3145736 | tf_op jit(solution)/shard_map/ppermute | solution.py:232
  10.7 24.6 %collective-permute-start = (bf16[256,2048]{1,0:T(8,128)(2,1)S(1)}, bf16[256,2048]{1,0:T(8,128)(2,1)S(1)}, u32[]{:S(2)}, u32[]{:S(2)}) collective-permute-start(bf16[256,2048]{1,0:T(8,128)(2,1)S(1)} %get-tuple-element.21), channel_id=1, source_target_pairs={{0,1},{1,0},{2,3},{3,2},{4,5},{5,4},{6,7},{7,6},{8,9},{9,8},{10,11... | collective-permute-start | bytes 3145736 | tf_op jit(solution)/shard_map/ppermute | solution.py:202
  10.7 44.6 %collective-permute-start.2 = (bf16[256,2048]{1,0:T(8,128)(2,1)S(1)}, bf16[256,2048]{1,0:T(8,128)(2,1)S(1)}, u32[]{:S(2)}, u32[]{:S(2)}) collective-permute-start(bf16[256,2048]{1,0:T(8,128)(2,1)S(1)} %get-tuple-element.21), channel_id=1, source_target_pairs={{0,3},{1,2},{2,1},{3,0},{4,7},{5,6},{6,5},{7,4},{8,11},{9,10},{10,... | collective-permute-start | bytes 3145736 | tf_op jit(solution)/shard_map/ppermute | solution.py:233
  27.6 18.0 %collective-permute-start.4 = (bf16[2,64,2048]{2,1,0:T(8,128)(2,1)S(1)}, bf16[2,64,2048]{2,1,0:T(8,128)(2,1)S(1)}, u32[]{:S(2)}, u32[]{:S(2)}) collective-permute-start(bf16[2,64,2048]{2,1,0:T(8,128)(2,1)S(1)} %get-tuple-element.32), channel_id=1, source_target_pairs={{4,8},{8,4},{5,9},{9,5},{6,10},{10,6},{7,11},{11,7},{20,24},{24,20... | collective-permute-start | bytes 1572872 | tf_op jit(solution)/shard_map/ppermute | solution.py:226
  28.3 37.1 %collective-permute-start.8 = (bf16[4,64,2048]{2,1,0:T(8,128)(2,1)S(1)}, bf16[4,64,2048]{2,1,0:T(8,128)(2,1)S(1)}, u32[]{:S(2)}, u32[]{:S(2)}) collective-permute-start(bf16[4,64,2048]{2,1,0:T(8,128)(2,1)S(1)} %collective-permute-done.5.refs_2_.refs_4_.refs_5_), channel_id=1, source_target_pairs={{4,0},{8,12},{5,1},{9,13},{6,2},{10,14},{7,3},{11,15},{20,16},{24,... | collective-permute-start | bytes 3145736 | tf_op jit(solution)/shard_map/ppermute | solution.py:226
  37.7 25.7 %collective-permute-start.10 = (bf16[192,2048]{1,0:T(8,128)(2,1)S(1)}, bf16[192,2048]{1,0:T(8,128)(2,1)S(1)}, u32[]{:S(2)}, u32[]{:S(2)}) collective-permute-start(bf16[192,2048]{1,0:T(8,128)(2,1)S(1)} %pad_maximum_fusion), channel_id=1, source_target_pairs={{0,4},{12,8},{1,5},{13,9},{2,6},{14,10},{3,7},{15,11},{16,20},{28,... | collective-permute-start | bytes 2359304 | tf_op jit(solution)/shard_map/ppermute | solution.py:241
  44.9 18.5 %collective-permute-start.7 = (bf16[2,64,2048]{2,1,0:T(8,128)(2,1)S(1)}, bf16[2,64,2048]{2,1,0:T(8,128)(2,1)S(1)}, u32[]{:S(2)}, u32[]{:S(2)}) collective-permute-start(bf16[2,64,2048]{2,1,0:T(8,128)(2,1)S(1)} %get-tuple-element.31), channel_id=1, source_target_pairs={{4,8},{8,4},{5,9},{9,5},{6,10},{10,6},{7,11},{11,7},{20,24},{24,20... | collective-permute-start | bytes 1572872 | tf_op jit(solution)/shard_map/ppermute | solution.py:226
  45.6 24.8 %collective-permute-start.6 = (bf16[2,64,2048]{2,1,0:T(8,128)(2,1)S(1)}, bf16[2,64,2048]{2,1,0:T(8,128)(2,1)S(1)}, u32[]{:S(2)}, u32[]{:S(2)}) collective-permute-start(bf16[2,64,2048]{2,1,0:T(8,128)(2,1)S(1)} %collective-permute-done.4.refs_4_), channel_id=1, source_target_pairs={{4,0},{8,12},{5,1},{9,13},{6,2},{10,14},{7,3},{11,15},{20,16},{24,... | collective-permute-start | bytes 1572872 | tf_op jit(solution)/shard_map/ppermute | solution.py:226
  55.4 12.5 %collective-permute-start.9 = (bf16[64,2048]{1,0:T(8,128)(2,1)S(1)}, bf16[64,2048]{1,0:T(8,128)(2,1)S(1)}, u32[]{:S(2)}, u32[]{:S(2)}) collective-permute-start(bf16[64,2048]{1,0:T(8,128)(2,1)S(1)} %slice.42), channel_id=1, source_target_pairs={{0,4},{12,8},{1,5},{13,9},{2,6},{14,10},{3,7},{15,11},{16,20},{28,... | collective-permute-start | bytes 786440 | tf_op jit(solution)/shard_map/ppermute | solution.py:243
  64.1 6.4 %collective-permute-start.11 = (f32[96,128]{1,0:T(8,128)S(1)}, f32[96,128]{1,0:T(8,128)S(1)}, u32[]{:S(2)}, u32[]{:S(2)}) collective-permute-start(f32[96,128]{1,0:T(8,128)S(1)} %sum_away.1), channel_id=1, source_target_pairs={{4,0},{8,12},{5,1},{9,13},{6,2},{10,14},{7,3},{11,15},{20,16},{24,... | collective-permute-start | bytes 147464 | tf_op jit(solution)/shard_map/ppermute | solution.py:247
  68.5 7.0 %collective-permute-start.15 = (f32[32,128]{1,0:T(8,128)S(1)}, f32[32,128]{1,0:T(8,128)S(1)}, u32[]{:S(2)}, u32[]{:S(2)}) collective-permute-start(f32[32,128]{1,0:T(8,128)S(1)} %sum_last_away.1), channel_id=1, source_target_pairs={{4,3},{5,2},{6,1},{7,0},{8,15},{9,14},{10,13},{11,12},{20,19},{21,... | collective-permute-start | bytes 49160 | tf_op jit(solution)/shard_map/ppermute | solution.py:251
  71.6 3.8 %collective-permute-start.13 = (f32[32,128]{1,0:T(8,128)S(1)}, f32[32,128]{1,0:T(8,128)S(1)}, u32[]{:S(2)}, u32[]{:S(2)}) collective-permute-start(f32[32,128]{1,0:T(8,128)S(1)} %get-tuple-element.29), channel_id=1, source_target_pairs={{0,2},{1,3},{2,0},{3,1},{4,6},{5,7},{6,4},{7,5},{8,10},{9,11},{10,... | collective-permute-start | bytes 49160 | tf_op jit(solution)/shard_map/ppermute | solution.py:255
  72.0 3.4 %collective-permute-start.14 = (f32[32,128]{1,0:T(8,128)S(1)}, f32[32,128]{1,0:T(8,128)S(1)}, u32[]{:S(2)}, u32[]{:S(2)}) collective-permute-start(f32[32,128]{1,0:T(8,128)S(1)} %get-tuple-element.30), channel_id=1, source_target_pairs={{0,3},{1,2},{2,1},{3,0},{4,7},{5,6},{6,5},{7,4},{8,11},{9,10},{10,... | collective-permute-start | bytes 49160 | tf_op jit(solution)/shard_map/ppermute | solution.py:255
  73.0 1.6 %collective-permute-start.12 = (f32[32,128]{1,0:T(8,128)S(1)}, f32[32,128]{1,0:T(8,128)S(1)}, u32[]{:S(2)}, u32[]{:S(2)}) collective-permute-start(f32[32,128]{1,0:T(8,128)S(1)} %get-tuple-element.28), channel_id=1, source_target_pairs={{0,1},{1,0},{2,3},{3,2},{4,5},{5,4},{6,7},{7,6},{8,9},{9,8},{10,11... | collective-permute-start | bytes 49160 | tf_op jit(solution)/shard_map/ppermute | solution.py:254

commit v5 on v4

--- a/solution.py
+++ b/solution.py
@@ -172,6 +172,7 @@
         out_shape=[end] * ends if ends else jax.ShapeDtypeStruct(total, jnp.float32),
         scratch_shapes=[pltpu.VMEM(total, jnp.float32)] if ends else [],
         compiler_params=pltpu.CompilerParams(vmem_limit_bytes=VMEM_LIMIT),
+        cost_estimate=pl.CostEstimate(flops=0, bytes_accessed=1 << 22, transcendentals=0),
         name=name,
     )(scalars, *arrays, *chunks, *extra)
 
@@ -241,11 +242,10 @@
     heads = lax.ppermute(after(heads, sums), "pair", INWARD)
     send("out3", mid3_chunk, OUTWARD, held_at(outermost, 0, per), sums)
     last_heads = lax.ppermute(tiles[3][:low], "pair", INWARD)
-    sums = add("sum_across", (3, 4, first), extra=(sums,))
     rows_at = [(0, t * low) for t in range(3)]
     away = add("sum_away", (0, 3, ("mid4",)), arrays=[after(heads, sums)], at=rows_at, blocks=3, ends=1)
     back = lax.ppermute(away[0], "pair", OUTWARD)
-    sums = add("sum_beyond", (0, 4, ("mid3", "mid4", "out")), extra=(sums,))
+    sums = add("sum_most", (3, 4, first), (0, 4, ("mid3", "mid4", "out")), extra=(after(sums, away[0]),))
     away = add("sum_last_away", (0, 1, ("mid4",)), arrays=[after(last_heads, sums)], at=[(0, 0)], blocks=1, ends=1)
     home_pairs = [(4 * a + i, 4 * b + 3 - i) for a, b in OUTWARD for i in range(4)]
     back_across = lax.ppermute(away[0], ("pair", "ints", "rep"), home_pairs)

time: 76.6 us -> 76.2 us (level)
    pallas_call x7 -> x6, Pallas kernels: 10.6 us -> 10 us  [add_positions(): pl.pallas_call(functools.partial(sum_kernel, rows, slots, tuple(tiles), w...]
  transfers between devices with their start and end apart: 16 -> 16, of which waited for: 7 -> 6; matrix products, arithmetic and copies ran while one was open for 0% -> 0% of each run, Pallas kernels for 16% -> 15%
where the time goes in v5:
time: 76.2 us; the launch traced here: 75.9 us
  waiting for transfers between devices  31.4 us (41%)
  starting transfers between devices  27.9 us (37%)
  Pallas kernels  13 us (17%)
  local copies, waits for them, and re-layouts  2.43 us (3%)
  other arithmetic  0.84 us (1%)
    ppermute x6, waiting for transfers between devices, send(): lax.ppermute(after(array, *earlier), 'pair', pairs)  16.1 us
    pallas_call x6, Pallas kernels, add_positions(): pl.pallas_call(functools.partial(sum_kernel, rows, slots, tuple(tiles), w...  10 us
    ppermute x1, waiting for transfers between devices, on_line(): tiles.append(lax.ppermute(other, ('ints', 'rep'), across))  8.44 us
    ppermute x6, starting transfers between devices, send(): lax.ppermute(after(array, *earlier), 'pair', pairs)  7.78 us
    ppermute x1, starting transfers between devices, on_line(): heads = lax.ppermute(after(heads, sums), 'pair', INWARD)  7.15 us
    ppermute x1, starting transfers between devices, on_line(): last_heads = lax.ppermute(tiles[3][:low], 'pair', INWARD)  5.97 us
    ppermute x1, waiting for transfers between devices, on_line(): tiles.append(lax.ppermute(mine, ('ints', 'rep'), beside))  3.65 us
    unnamed x8, local copies, waits for them, and re-layouts  2.21 us
  transfers between devices with their start and end apart: 16, of which 6 were waited for; matrix products, arithmetic and copies ran while one was open for 0% of the time, Pallas kernels for 15%

profile of v5, /device:TPU:0, one launch (start us, length us, event | category | flops | bytes accessed | tf_op | source)
XLA Modules:
  0.0 75.9 jit_solution(16358732957463102450)
XLA Ops:
  0.0 1.3 %own_half.1.refs_1_.refs_3_.refs_4_ = bf16[4,64,2048]{2,1,0:T(8,128)(2,1)S(1)} custom-call(bf16[64,16384]{1,0:T(8,128)(2,1)} %integrals_ref.1), custom_call_target="tpu_custom_call" | custom-call | tf_op jit(solution)/shard_map/own_half/pallas_call | solution.py:55
  1.3 3.1 %collective-permute-start.3 = (bf16[4,64,2048]{2,1,0:T(8,128)(2,1)S(1)}, bf16[4,64,2048]{2,1,0:T(8,128)(2,1)S(1)}, u32[]{:S(2)}, u32[]{:S(2)}) collective-permute-start(bf16[4,64,2048]{2,1,0:T(8,128)(2,1)S(1)} %own_half.1.refs_1_.refs_3_.refs_4_), channel_id=1, source_target_pairs={{0,4},{4,0},{8,12},{12,8},{1,5},{5,1},{9,13},{13,9},{2,6},{6,2},{1... | collective-permute-start | bytes 3145736 | tf_op jit(solution)/shard_map/ppermute | solution.py:227
  4.4 0.7 collective-permute-start.5
  5.2 2.2 %copy-done = bf16[32,16,4096]{2,1,0:T(8,128)(2,1)S(1)} copy-done((bf16[32,16,4096]{2,1,0:T(8,128)(2,1)S(1)}, bf16[32,16,4096]{2,1,0:T(8,128)(2,1)}, u32[]{:S(2)}) %copy-start) | copy-done | bytes 4194328
  7.4 1.8 %pack.1 = (bf16[256,2048]{1,0:T(8,128)(2,1)S(1)}, bf16[256,2048]{1,0:T(8,128)(2,1)S(1)}, s32[33]{0:T(128)S(1)}) custom-call(s32[66]{0:T(128)S(1)} %concatenate.12.scalar_ref, bf16[512,4096]{1,0:T(8,128)(2,1)S(1)} %bitcast.3), custom_call_target="tpu_custom_call" | custom-call | tf_op jit(solution)/shard_map/pack/pallas_call | solution.py:116
  9.2 1.6 %collective-permute-start.1 = (bf16[256,2048]{1,0:T(8,128)(2,1)S(1)}, bf16[256,2048]{1,0:T(8,128)(2,1)S(1)}, u32[]{:S(2)}, u32[]{:S(2)}) collective-permute-start(bf16[256,2048]{1,0:T(8,128)(2,1)S(1)} %get-tuple-element.21.refs_0_), channel_id=1, source_target_pairs={{0,2},{1,3},{2,0},{3,1},{4,6},{5,7},{6,4},{7,5},{8,10},{9,11},{10,... | collective-permute-start | bytes 3145736 | tf_op jit(solution)/shard_map/ppermute | solution.py:233
  11.4 16.1 %collective-permute-done.3.refs_3_.refs_5_.refs_6_ = bf16[4,64,2048]{2,1,0:T(8,128)(2,1)S(1)} collective-permute-done((bf16[4,64,2048]{2,1,0:T(8,128)(2,1)S(1)}, bf16[4,64,2048]{2,1,0:T(8,128)(2,1)S(1)}, u32[]{:S(2)}, u32[]{:S(2)}) %collective-permute-start.3) | collective-permute-done | bytes 1048608 | tf_op jit(solution)/shard_map/ppermute | solution.py:227
  27.6 0.7 collective-permute-start.4
  28.3 1.3 %collective-permute-start.8 = (bf16[4,64,2048]{2,1,0:T(8,128)(2,1)S(1)}, bf16[4,64,2048]{2,1,0:T(8,128)(2,1)S(1)}, u32[]{:S(2)}, u32[]{:S(2)}) collective-permute-start(bf16[4,64,2048]{2,1,0:T(8,128)(2,1)S(1)} %collective-permute-done.5.refs_2_.refs_4_.refs_5_), channel_id=1, source_target_pairs={{4,0},{8,12},{5,1},{9,13},{6,2},{10,14},{7,3},{11,15},{20,16},{24,... | collective-permute-start | bytes 3145736 | tf_op jit(solution)/shard_map/ppermute | solution.py:227
  29.6 2.1 %sum_near.1.refs_6_ = f32[2,128,64]{2,1,0:T(8,128)S(1)} custom-call(s32[33]{0:T(128)S(1)} %get-tuple-element.20.scalar_ref, bf16[256,2048]{1,0:T(8,128)(2,1)S(1)} %get-tuple-element.21.refs_0_, bf16[4,64,2048]{2,1,0:T(8,128)(2,1)S(1)} %own_half.1.refs_1_.refs_3_.refs_4_, bf16[4,64,2048]{2,1,0:T(8,128)(2,1)S(1)} %collective-permute-done.5.refs_2_.refs_4_.refs_5_, ...), custom_call_target="tpu_custom_call" | custom-call | bytes 4194304 | tf_op jit(solution)/shard_map/sum_near/pallas_call | solution.py:168
  31.7 3.6 %collective-permute-done.1.refs_2_ = bf16[256,2048]{1,0:T(8,128)(2,1)S(1)} collective-permute-done((bf16[256,2048]{1,0:T(8,128)(2,1)S(1)}, bf16[256,2048]{1,0:T(8,128)(2,1)S(1)}, u32[]{:S(2)}, u32[]{:S(2)}) %collective-permute-start.1) | collective-permute-done | bytes 1048608 | tf_op jit(solution)/shard_map/ppermute | solution.py:233
  35.4 2.3 %sum_side.1.refs_10_ = f32[2,128,64]{2,1,0:T(8,128)S(1)} custom-call(s32[33]{0:T(128)S(1)} %get-tuple-element.20.scalar_ref, bf16[256,2048]{1,0:T(8,128)(2,1)S(1)} %get-tuple-element.21.refs_0_, bf16[256,2048]{1,0:T(8,128)(2,1)S(1)} %collective-permute-done.refs_1_, bf16[256,2048]{1,0:T(8,128)(2,1)S(1)} %collective-permute-done.1.refs_2_, ...), custom_call_target="tpu_custom_call" | custom-call | bytes 4194304 | tf_op jit(solution)/shard_map/sum_side/pallas_call | solution.py:168
  37.7 7.2 %collective-permute-start.9 = (bf16[192,2048]{1,0:T(8,128)(2,1)S(1)}, bf16[192,2048]{1,0:T(8,128)(2,1)S(1)}, u32[]{:S(2)}, u32[]{:S(2)}) collective-permute-start(bf16[192,2048]{1,0:T(8,128)(2,1)S(1)} %pad_maximum_fusion), channel_id=1, source_target_pairs={{0,4},{12,8},{1,5},{13,9},{2,6},{14,10},{3,7},{15,11},{16,20},{28,... | collective-permute-start | bytes 2359304 | tf_op jit(solution)/shard_map/ppermute | solution.py:242
  45.6 1.3 %collective-permute-start.6 = (bf16[2,64,2048]{2,1,0:T(8,128)(2,1)S(1)}, bf16[2,64,2048]{2,1,0:T(8,128)(2,1)S(1)}, u32[]{:S(2)}, u32[]{:S(2)}) collective-permute-start(bf16[2,64,2048]{2,1,0:T(8,128)(2,1)S(1)} %collective-permute-done.4.refs_7_), channel_id=1, source_target_pairs={{4,0},{8,12},{5,1},{9,13},{6,2},{10,14},{7,3},{11,15},{20,16},{24,... | collective-permute-start | bytes 1572872 | tf_op jit(solution)/shard_map/ppermute | solution.py:227
  46.9 8.4 %collective-permute-done.2.refs_3_ = bf16[256,2048]{1,0:T(8,128)(2,1)S(1)} collective-permute-done((bf16[256,2048]{1,0:T(8,128)(2,1)S(1)}, bf16[256,2048]{1,0:T(8,128)(2,1)S(1)}, u32[]{:S(2)}, u32[]{:S(2)}) %collective-permute-start.2) | collective-permute-done | bytes 1048608 | tf_op jit(solution)/shard_map/ppermute | solution.py:234
  55.4 6.0 %collective-permute-start.10 = (bf16[64,2048]{1,0:T(8,128)(2,1)S(1)}, bf16[64,2048]{1,0:T(8,128)(2,1)S(1)}, u32[]{:S(2)}, u32[]{:S(2)}) collective-permute-start(bf16[64,2048]{1,0:T(8,128)(2,1)S(1)} %slice.44), channel_id=1, source_target_pairs={{0,4},{12,8},{1,5},{13,9},{2,6},{14,10},{3,7},{15,11},{16,20},{28,... | collective-permute-start | bytes 786440 | tf_op jit(solution)/shard_map/ppermute | solution.py:244
  62.0 1.3 %collective-permute-start.11 = (f32[96,128]{1,0:T(8,128)S(1)}, f32[96,128]{1,0:T(8,128)S(1)}, u32[]{:S(2)}, u32[]{:S(2)}) collective-permute-start(f32[96,128]{1,0:T(8,128)S(1)} %sum_away.1), channel_id=1, source_target_pairs={{4,0},{8,12},{5,1},{9,13},{6,2},{10,14},{7,3},{11,15},{20,16},{24,... | collective-permute-start | bytes 147464 | tf_op jit(solution)/shard_map/ppermute | solution.py:247
  63.3 3.2 %sum_most.1.refs_5_ = f32[2,128,64]{2,1,0:T(8,128)S(1)} custom-call(s32[33]{0:T(128)S(1)} %get-tuple-element.20.scalar_ref, bf16[256,2048]{1,0:T(8,128)(2,1)S(1)} %get-tuple-element.21.refs_0_, bf16[256,2048]{1,0:T(8,128)(2,1)S(1)} %collective-permute-done.refs_1_, bf16[256,2048]{1,0:T(8,128)(2,1)S(1)} %collective-permute-done.1.refs_2_, ...), custom_call_target="tpu_custom_call" | custom-call | bytes 4194304 | tf_op jit(solution)/shard_map/sum_most/pallas_call | solution.py:168
  66.5 1.3 %collective-permute-done.10.refs_0_ = bf16[64,2048]{1,0:T(8,128)(2,1)S(1)} collective-permute-done((bf16[64,2048]{1,0:T(8,128)(2,1)S(1)}, bf16[64,2048]{1,0:T(8,128)(2,1)S(1)}, u32[]{:S(2)}, u32[]{:S(2)}) %collective-permute-start.10) | collective-permute-done | bytes 262176 | tf_op jit(solution)/shard_map/ppermute | solution.py:244
  68.5 1.3 %collective-permute-start.15 = (f32[32,128]{1,0:T(8,128)S(1)}, f32[32,128]{1,0:T(8,128)S(1)}, u32[]{:S(2)}, u32[]{:S(2)}) collective-permute-start(f32[32,128]{1,0:T(8,128)S(1)} %sum_last_away.1), channel_id=1, source_target_pairs={{4,3},{5,2},{6,1},{7,0},{8,15},{9,14},{10,13},{11,12},{20,19},{21,... | collective-permute-start | bytes 49160 | tf_op jit(solution)/shard_map/ppermute | solution.py:251
  69.8 1.2 %sum_last.1 = (f32[32,128]{1,0:T(8,128)S(1)}, f32[32,128]{1,0:T(8,128)S(1)}, f32[32,128]{1,0:T(8,128)S(1)}, f32[32,128]{1,0:T(8,128)S(1)}) custom-call(s32[33]{0:T(128)S(1)} %get-tuple-element.20.scalar_ref, bf16[256,2048]{1,0:T(8,128)(2,1)S(1)} %get-tuple-element.21.refs_0_, bf16[256,2048]{1,0:T(8,128)(2,1)S(1)} %collective-permute-done.refs_1_, ...), custom_call_target="tpu_custom_call" | custom-call | bytes 4194304 | tf_op jit(solution)/shard_map/sum_last/pallas_call | solution.py:168
  71.2 1.6 %collective-permute-start.14 = (f32[32,128]{1,0:T(8,128)S(1)}, f32[32,128]{1,0:T(8,128)S(1)}, u32[]{:S(2)}, u32[]{:S(2)}) collective-permute-start(f32[32,128]{1,0:T(8,128)S(1)} %get-tuple-element.32), channel_id=1, source_target_pairs={{0,3},{1,2},{2,1},{3,0},{4,7},{5,6},{6,5},{7,4},{8,11},{9,10},{10,... | collective-permute-start | bytes 49160 | tf_op jit(solution)/shard_map/ppermute | solution.py:255
  73.2 0.8 %collective-permute-done.12 = f32[32,128]{1,0:T(8,128)S(1)} collective-permute-done((f32[32,128]{1,0:T(8,128)S(1)}, f32[32,128]{1,0:T(8,128)S(1)}, u32[]{:S(2)}, u32[]{:S(2)}) %collective-permute-start.12) | collective-permute-done | bytes 16416 | tf_op jit(solution)/shard_map/ppermute | solution.py:254
  74.1 1.0 %collective-permute-done.13 = f32[32,128]{1,0:T(8,128)S(1)} collective-permute-done((f32[32,128]{1,0:T(8,128)S(1)}, f32[32,128]{1,0:T(8,128)S(1)}, u32[]{:S(2)}, u32[]{:S(2)}) %collective-permute-start.13) | collective-permute-done | bytes 16416 | tf_op jit(solution)/shard_map/ppermute | solution.py:255
  (36 shorter events, 4.4 us)
Async XLA Ops:
  0.0 5.1 %copy-start.3 = (s32[32]{0:T(128)S(1)}, s32[32]{0:T(128)}, u32[]{:S(2)}) copy-start(s32[32]{0:T(128)} %param.7) | copy-start | bytes 388
  0.0 5.1 %copy-start.1 = (s32[16]{0:T(128)S(1)}, s32[16]{0:T(128)}, u32[]{:S(2)}) copy-start(s32[16]{0:T(128)} %param.8) | copy-start | bytes 196
  0.0 5.1 %copy-start.2 = (s32[16]{0:T(128)S(1)}, s32[16]{0:T(128)}, u32[]{:S(2)}) copy-start(s32[16]{0:T(128)} %param.9) | copy-start | bytes 196
  1.3 26.2 %collective-permute-start.3 = (bf16[4,64,2048]{2,1,0:T(8,128)(2,1)S(1)}, bf16[4,64,2048]{2,1,0:T(8,128)(2,1)S(1)}, u32[]{:S(2)}, u32[]{:S(2)}) collective-permute-start(bf16[4,64,2048]{2,1,0:T(8,128)(2,1)S(1)} %own_half.1.refs_1_.refs_3_.refs_4_), channel_id=1, source_target_pairs={{0,4},{4,0},{8,12},{12,8},{1,5},{5,1},{9,13},{13,9},{2,6},{6,2},{1... | collective-permute-start | bytes 3145736 | tf_op jit(solution)/shard_map/ppermute | solution.py:227
  4.4 23.9 %collective-permute-start.5 = (bf16[4,64,2048]{2,1,0:T(8,128)(2,1)S(1)}, bf16[4,64,2048]{2,1,0:T(8,128)(2,1)S(1)}, u32[]{:S(2)}, u32[]{:S(2)}) collective-permute-start(bf16[4,64,2048]{2,1,0:T(8,128)(2,1)S(1)} %own_half.1.refs_1_.refs_3_.refs_4_), channel_id=1, source_target_pairs={{4,8},{8,4},{5,9},{9,5},{6,10},{10,6},{7,11},{11,7},{20,24},{24,20... | collective-permute-start | bytes 3145736 | tf_op jit(solution)/shard_map/ppermute | solution.py:227
  5.2 2.2 %copy-start = (bf16[32,16,4096]{2,1,0:T(8,128)(2,1)S(1)}, bf16[32,16,4096]{2,1,0:T(8,128)(2,1)}, u32[]{:S(2)}) copy-start(bf16[32,16,4096]{2,1,0:T(8,128)(2,1)} %param.5) | copy-start | bytes 12582916
  9.2 26.1 %collective-permute-start.1 = (bf16[256,2048]{1,0:T(8,128)(2,1)S(1)}, bf16[256,2048]{1,0:T(8,128)(2,1)S(1)}, u32[]{:S(2)}, u32[]{:S(2)}) collective-permute-start(bf16[256,2048]{1,0:T(8,128)(2,1)S(1)} %get-tuple-element.21.refs_0_), channel_id=1, source_target_pairs={{0,2},{1,3},{2,0},{3,1},{4,6},{5,7},{6,4},{7,5},{8,10},{9,11},{10,... | collective-permute-start | bytes 3145736 | tf_op jit(solution)/shard_map/ppermute | solution.py:233
  10.7 24.6 %collective-permute-start = (bf16[256,2048]{1,0:T(8,128)(2,1)S(1)}, bf16[256,2048]{1,0:T(8,128)(2,1)S(1)}, u32[]{:S(2)}, u32[]{:S(2)}) collective-permute-start(bf16[256,2048]{1,0:T(8,128)(2,1)S(1)} %get-tuple-element.22), channel_id=1, source_target_pairs={{0,1},{1,0},{2,3},{3,2},{4,5},{5,4},{6,7},{7,6},{8,9},{9,8},{10,11... | collective-permute-start | bytes 3145736 | tf_op jit(solution)/shard_map/ppermute | solution.py:203
  10.7 44.6 %collective-permute-start.2 = (bf16[256,2048]{1,0:T(8,128)(2,1)S(1)}, bf16[256,2048]{1,0:T(8,128)(2,1)S(1)}, u32[]{:S(2)}, u32[]{:S(2)}) collective-permute-start(bf16[256,2048]{1,0:T(8,128)(2,1)S(1)} %get-tuple-element.22), channel_id=1, source_target_pairs={{0,3},{1,2},{2,1},{3,0},{4,7},{5,6},{6,5},{7,4},{8,11},{9,10},{10,... | collective-permute-start | bytes 3145736 | tf_op jit(solution)/shard_map/ppermute | solution.py:234
  27.6 18.0 %collective-permute-start.4 = (bf16[2,64,2048]{2,1,0:T(8,128)(2,1)S(1)}, bf16[2,64,2048]{2,1,0:T(8,128)(2,1)S(1)}, u32[]{:S(2)}, u32[]{:S(2)}) collective-permute-start(bf16[2,64,2048]{2,1,0:T(8,128)(2,1)S(1)} %get-tuple-element.34), channel_id=1, source_target_pairs={{4,8},{8,4},{5,9},{9,5},{6,10},{10,6},{7,11},{11,7},{20,24},{24,20... | collective-permute-start | bytes 1572872 | tf_op jit(solution)/shard_map/ppermute | solution.py:227
  28.3 35.0 %collective-permute-start.8 = (bf16[4,64,2048]{2,1,0:T(8,128)(2,1)S(1)}, bf16[4,64,2048]{2,1,0:T(8,128)(2,1)S(1)}, u32[]{:S(2)}, u32[]{:S(2)}) collective-permute-start(bf16[4,64,2048]{2,1,0:T(8,128)(2,1)S(1)} %collective-permute-done.5.refs_2_.refs_4_.refs_5_), channel_id=1, source_target_pairs={{4,0},{8,12},{5,1},{9,13},{6,2},{10,14},{7,3},{11,15},{20,16},{24,... | collective-permute-start | bytes 3145736 | tf_op jit(solution)/shard_map/ppermute | solution.py:227
  37.7 23.6 %collective-permute-start.9 = (bf16[192,2048]{1,0:T(8,128)(2,1)S(1)}, bf16[192,2048]{1,0:T(8,128)(2,1)S(1)}, u32[]{:S(2)}, u32[]{:S(2)}) collective-permute-start(bf16[192,2048]{1,0:T(8,128)(2,1)S(1)} %pad_maximum_fusion), channel_id=1, source_target_pairs={{0,4},{12,8},{1,5},{13,9},{2,6},{14,10},{3,7},{15,11},{16,20},{28,... | collective-permute-start | bytes 2359304 | tf_op jit(solution)/shard_map/ppermute | solution.py:242
  44.9 16.5 %collective-permute-start.7 = (bf16[2,64,2048]{2,1,0:T(8,128)(2,1)S(1)}, bf16[2,64,2048]{2,1,0:T(8,128)(2,1)S(1)}, u32[]{:S(2)}, u32[]{:S(2)}) collective-permute-start(bf16[2,64,2048]{2,1,0:T(8,128)(2,1)S(1)} %get-tuple-element.33), channel_id=1, source_target_pairs={{4,8},{8,4},{5,9},{9,5},{6,10},{10,6},{7,11},{11,7},{20,24},{24,20... | collective-permute-start | bytes 1572872 | tf_op jit(solution)/shard_map/ppermute | solution.py:227
  45.6 24.2 %collective-permute-start.6 = (bf16[2,64,2048]{2,1,0:T(8,128)(2,1)S(1)}, bf16[2,64,2048]{2,1,0:T(8,128)(2,1)S(1)}, u32[]{:S(2)}, u32[]{:S(2)}) collective-permute-start(bf16[2,64,2048]{2,1,0:T(8,128)(2,1)S(1)} %collective-permute-done.4.refs_7_), channel_id=1, source_target_pairs={{4,0},{8,12},{5,1},{9,13},{6,2},{10,14},{7,3},{11,15},{20,16},{24,... | collective-permute-start | bytes 1572872 | tf_op jit(solution)/shard_map/ppermute | solution.py:227
  55.4 12.5 %collective-permute-start.10 = (bf16[64,2048]{1,0:T(8,128)(2,1)S(1)}, bf16[64,2048]{1,0:T(8,128)(2,1)S(1)}, u32[]{:S(2)}, u32[]{:S(2)}) collective-permute-start(bf16[64,2048]{1,0:T(8,128)(2,1)S(1)} %slice.44), channel_id=1, source_target_pairs={{0,4},{12,8},{1,5},{13,9},{2,6},{14,10},{3,7},{15,11},{16,20},{28,... | collective-permute-start | bytes 786440 | tf_op jit(solution)/shard_map/ppermute | solution.py:244
  62.0 7.8 %collective-permute-start.11 = (f32[96,128]{1,0:T(8,128)S(1)}, f32[96,128]{1,0:T(8,128)S(1)}, u32[]{:S(2)}, u32[]{:S(2)}) collective-permute-start(f32[96,128]{1,0:T(8,128)S(1)} %sum_away.1), channel_id=1, source_target_pairs={{4,0},{8,12},{5,1},{9,13},{6,2},{10,14},{7,3},{11,15},{20,16},{24,... | collective-permute-start | bytes 147464 | tf_op jit(solution)/shard_map/ppermute | solution.py:247
  68.5 6.6 %collective-permute-start.15 = (f32[32,128]{1,0:T(8,128)S(1)}, f32[32,128]{1,0:T(8,128)S(1)}, u32[]{:S(2)}, u32[]{:S(2)}) collective-permute-start(f32[32,128]{1,0:T(8,128)S(1)} %sum_last_away.1), channel_id=1, source_target_pairs={{4,3},{5,2},{6,1},{7,0},{8,15},{9,14},{10,13},{11,12},{20,19},{21,... | collective-permute-start | bytes 49160 | tf_op jit(solution)/shard_map/ppermute | solution.py:251
  71.0 4.1 %collective-permute-start.13 = (f32[32,128]{1,0:T(8,128)S(1)}, f32[32,128]{1,0:T(8,128)S(1)}, u32[]{:S(2)}, u32[]{:S(2)}) collective-permute-start(f32[32,128]{1,0:T(8,128)S(1)} %get-tuple-element.31), channel_id=1, source_target_pairs={{0,2},{1,3},{2,0},{3,1},{4,6},{5,7},{6,4},{7,5},{8,10},{9,11},{10,... | collective-permute-start | bytes 49160 | tf_op jit(solution)/shard_map/ppermute | solution.py:255
  71.2 3.9 %collective-permute-start.14 = (f32[32,128]{1,0:T(8,128)S(1)}, f32[32,128]{1,0:T(8,128)S(1)}, u32[]{:S(2)}, u32[]{:S(2)}) collective-permute-start(f32[32,128]{1,0:T(8,128)S(1)} %get-tuple-element.32), channel_id=1, source_target_pairs={{0,3},{1,2},{2,1},{3,0},{4,7},{5,6},{6,5},{7,4},{8,11},{9,10},{10,... | collective-permute-start | bytes 49160 | tf_op jit(solution)/shard_map/ppermute | solution.py:255
  72.7 1.3 %collective-permute-start.12 = (f32[32,128]{1,0:T(8,128)S(1)}, f32[32,128]{1,0:T(8,128)S(1)}, u32[]{:S(2)}, u32[]{:S(2)}) collective-permute-start(f32[32,128]{1,0:T(8,128)S(1)} %get-tuple-element.30), channel_id=1, source_target_pairs={{0,1},{1,0},{2,3},{3,2},{4,5},{5,4},{6,7},{7,6},{8,9},{9,8},{10,11... | collective-permute-start | bytes 49160 | tf_op jit(solution)/shard_map/ppermute | solution.py:254

commit v6 on v5

--- a/solution.py
+++ b/solution.py
@@ -120,6 +120,7 @@
         out_shape=[packed, packed, jax.ShapeDtypeStruct((2 * slots + 1,), jnp.int32)],
         scratch_shapes=[pltpu.VMEM((rows // 16, live * 16, 16 * slots), amplitudes.dtype)],
         compiler_params=pltpu.CompilerParams(vmem_limit_bytes=VMEM_LIMIT),
+        cost_estimate=pl.CostEstimate(flops=0, bytes_accessed=3 * amplitudes.size, transcendentals=0),
         name="pack",
     )(scalars, amplitudes.reshape(rows * slots, tile))
 

time: 76.2 us -> 76.2 us (level)
  no operation moved by 1% of the time
where the time goes in v6:
time: 76.2 us; the launch traced here: 75.9 us
  waiting for transfers between devices  31.4 us (41%)
  starting transfers between devices  27.9 us (37%)
  Pallas kernels  13 us (17%)
  local copies, waits for them, and re-layouts  2.43 us (3%)
  other arithmetic  0.84 us (1%)
    ppermute x6, waiting for transfers between devices, send(): lax.ppermute(after(array, *earlier), 'pair', pairs)  16.1 us
    pallas_call x6, Pallas kernels, add_positions(): pl.pallas_call(functools.partial(sum_kernel, rows, slots, tuple(tiles), w...  10 us
    ppermute x1, waiting for transfers between devices, on_line(): tiles.append(lax.ppermute(other, ('ints', 'rep'), across))  8.44 us
    ppermute x6, starting transfers between devices, send(): lax.ppermute(after(array, *earlier), 'pair', pairs)  7.78 us
    ppermute x1, starting transfers between devices, on_line(): heads = lax.ppermute(after(heads, sums), 'pair', INWARD)  7.15 us
    ppermute x1, starting transfers between devices, on_line(): last_heads = lax.ppermute(tiles[3][:low], 'pair', INWARD)  5.97 us
    ppermute x1, waiting for transfers between devices, on_line(): tiles.append(lax.ppermute(mine, ('ints', 'rep'), beside))  3.65 us
    unnamed x8, local copies, waits for them, and re-layouts  2.21 us
  transfers between devices with their start and end apart: 16, of which 6 were waited for; matrix products, arithmetic and copies ran while one was open for 0% of the time, Pallas kernels for 15%

profile of v6, /device:TPU:0, one launch (start us, length us, event | category | flops | bytes accessed | tf_op | source)
XLA Modules:
  0.0 75.9 jit_solution(16358732957463102450)
XLA Ops:
  0.0 1.3 %own_half.1.refs_1_.refs_3_.refs_4_ = bf16[4,64,2048]{2,1,0:T(8,128)(2,1)S(1)} custom-call(bf16[64,16384]{1,0:T(8,128)(2,1)} %integrals_ref.1), custom_call_target="tpu_custom_call" | custom-call | tf_op jit(solution)/shard_map/own_half/pallas_call | solution.py:55
  1.3 3.1 %collective-permute-start.3 = (bf16[4,64,2048]{2,1,0:T(8,128)(2,1)S(1)}, bf16[4,64,2048]{2,1,0:T(8,128)(2,1)S(1)}, u32[]{:S(2)}, u32[]{:S(2)}) collective-permute-start(bf16[4,64,2048]{2,1,0:T(8,128)(2,1)S(1)} %own_half.1.refs_1_.refs_3_.refs_4_), channel_id=1, source_target_pairs={{0,4},{4,0},{8,12},{12,8},{1,5},{5,1},{9,13},{13,9},{2,6},{6,2},{1... | collective-permute-start | bytes 3145736 | tf_op jit(solution)/shard_map/ppermute | solution.py:228
  4.4 0.7 collective-permute-start.5
  5.2 2.2 %copy-done = bf16[32,16,4096]{2,1,0:T(8,128)(2,1)S(1)} copy-done((bf16[32,16,4096]{2,1,0:T(8,128)(2,1)S(1)}, bf16[32,16,4096]{2,1,0:T(8,128)(2,1)}, u32[]{:S(2)}) %copy-start) | copy-done | bytes 4194328
  7.4 1.8 %pack.1 = (bf16[256,2048]{1,0:T(8,128)(2,1)S(1)}, bf16[256,2048]{1,0:T(8,128)(2,1)S(1)}, s32[33]{0:T(128)S(1)}) custom-call(s32[66]{0:T(128)S(1)} %concatenate.12.scalar_ref, bf16[512,4096]{1,0:T(8,128)(2,1)S(1)} %bitcast.3), custom_call_target="tpu_custom_call" | custom-call | bytes 6291456 | tf_op jit(solution)/shard_map/pack/pallas_call | solution.py:116
  9.2 1.6 %collective-permute-start.1 = (bf16[256,2048]{1,0:T(8,128)(2,1)S(1)}, bf16[256,2048]{1,0:T(8,128)(2,1)S(1)}, u32[]{:S(2)}, u32[]{:S(2)}) collective-permute-start(bf16[256,2048]{1,0:T(8,128)(2,1)S(1)} %get-tuple-element.21.refs_0_), channel_id=1, source_target_pairs={{0,2},{1,3},{2,0},{3,1},{4,6},{5,7},{6,4},{7,5},{8,10},{9,11},{10,... | collective-permute-start | bytes 3145736 | tf_op jit(solution)/shard_map/ppermute | solution.py:234
  11.4 16.1 %collective-permute-done.3.refs_3_.refs_5_.refs_6_ = bf16[4,64,2048]{2,1,0:T(8,128)(2,1)S(1)} collective-permute-done((bf16[4,64,2048]{2,1,0:T(8,128)(2,1)S(1)}, bf16[4,64,2048]{2,1,0:T(8,128)(2,1)S(1)}, u32[]{:S(2)}, u32[]{:S(2)}) %collective-permute-start.3) | collective-permute-done | bytes 1048608 | tf_op jit(solution)/shard_map/ppermute | solution.py:228
  27.6 0.7 collective-permute-start.4
  28.3 1.3 %collective-permute-start.8 = (bf16[4,64,2048]{2,1,0:T(8,128)(2,1)S(1)}, bf16[4,64,2048]{2,1,0:T(8,128)(2,1)S(1)}, u32[]{:S(2)}, u32[]{:S(2)}) collective-permute-start(bf16[4,64,2048]{2,1,0:T(8,128)(2,1)S(1)} %collective-permute-done.5.refs_2_.refs_4_.refs_5_), channel_id=1, source_target_pairs={{4,0},{8,12},{5,1},{9,13},{6,2},{10,14},{7,3},{11,15},{20,16},{24,... | collective-permute-start | bytes 3145736 | tf_op jit(solution)/shard_map/ppermute | solution.py:228
  29.6 2.1 %sum_near.1.refs_6_ = f32[2,128,64]{2,1,0:T(8,128)S(1)} custom-call(s32[33]{0:T(128)S(1)} %get-tuple-element.20.scalar_ref, bf16[256,2048]{1,0:T(8,128)(2,1)S(1)} %get-tuple-element.21.refs_0_, bf16[4,64,2048]{2,1,0:T(8,128)(2,1)S(1)} %own_half.1.refs_1_.refs_3_.refs_4_, bf16[4,64,2048]{2,1,0:T(8,128)(2,1)S(1)} %collective-permute-done.5.refs_2_.refs_4_.refs_5_, ...), custom_call_target="tpu_custom_call" | custom-call | bytes 4194304 | tf_op jit(solution)/shard_map/sum_near/pallas_call | solution.py:169
  31.7 3.6 %collective-permute-done.1.refs_2_ = bf16[256,2048]{1,0:T(8,128)(2,1)S(1)} collective-permute-done((bf16[256,2048]{1,0:T(8,128)(2,1)S(1)}, bf16[256,2048]{1,0:T(8,128)(2,1)S(1)}, u32[]{:S(2)}, u32[]{:S(2)}) %collective-permute-start.1) | collective-permute-done | bytes 1048608 | tf_op jit(solution)/shard_map/ppermute | solution.py:234
  35.4 2.3 %sum_side.1.refs_10_ = f32[2,128,64]{2,1,0:T(8,128)S(1)} custom-call(s32[33]{0:T(128)S(1)} %get-tuple-element.20.scalar_ref, bf16[256,2048]{1,0:T(8,128)(2,1)S(1)} %get-tuple-element.21.refs_0_, bf16[256,2048]{1,0:T(8,128)(2,1)S(1)} %collective-permute-done.refs_1_, bf16[256,2048]{1,0:T(8,128)(2,1)S(1)} %collective-permute-done.1.refs_2_, ...), custom_call_target="tpu_custom_call" | custom-call | bytes 4194304 | tf_op jit(solution)/shard_map/sum_side/pallas_call | solution.py:169
  37.7 7.2 %collective-permute-start.9 = (bf16[192,2048]{1,0:T(8,128)(2,1)S(1)}, bf16[192,2048]{1,0:T(8,128)(2,1)S(1)}, u32[]{:S(2)}, u32[]{:S(2)}) collective-permute-start(bf16[192,2048]{1,0:T(8,128)(2,1)S(1)} %pad_maximum_fusion), channel_id=1, source_target_pairs={{0,4},{12,8},{1,5},{13,9},{2,6},{14,10},{3,7},{15,11},{16,20},{28,... | collective-permute-start | bytes 2359304 | tf_op jit(solution)/shard_map/ppermute | solution.py:243
  45.6 1.3 %collective-permute-start.6 = (bf16[2,64,2048]{2,1,0:T(8,128)(2,1)S(1)}, bf16[2,64,2048]{2,1,0:T(8,128)(2,1)S(1)}, u32[]{:S(2)}, u32[]{:S(2)}) collective-permute-start(bf16[2,64,2048]{2,1,0:T(8,128)(2,1)S(1)} %collective-permute-done.4.refs_7_), channel_id=1, source_target_pairs={{4,0},{8,12},{5,1},{9,13},{6,2},{10,14},{7,3},{11,15},{20,16},{24,... | collective-permute-start | bytes 1572872 | tf_op jit(solution)/shard_map/ppermute | solution.py:228
  46.9 8.4 %collective-permute-done.2.refs_3_ = bf16[256,2048]{1,0:T(8,128)(2,1)S(1)} collective-permute-done((bf16[256,2048]{1,0:T(8,128)(2,1)S(1)}, bf16[256,2048]{1,0:T(8,128)(2,1)S(1)}, u32[]{:S(2)}, u32[]{:S(2)}) %collective-permute-start.2) | collective-permute-done | bytes 1048608 | tf_op jit(solution)/shard_map/ppermute | solution.py:235
  55.4 6.0 %collective-permute-start.10 = (bf16[64,2048]{1,0:T(8,128)(2,1)S(1)}, bf16[64,2048]{1,0:T(8,128)(2,1)S(1)}, u32[]{:S(2)}, u32[]{:S(2)}) collective-permute-start(bf16[64,2048]{1,0:T(8,128)(2,1)S(1)} %slice.44), channel_id=1, source_target_pairs={{0,4},{12,8},{1,5},{13,9},{2,6},{14,10},{3,7},{15,11},{16,20},{28,... | collective-permute-start | bytes 786440 | tf_op jit(solution)/shard_map/ppermute | solution.py:245
  62.0 1.3 %collective-permute-start.11 = (f32[96,128]{1,0:T(8,128)S(1)}, f32[96,128]{1,0:T(8,128)S(1)}, u32[]{:S(2)}, u32[]{:S(2)}) collective-permute-start(f32[96,128]{1,0:T(8,128)S(1)} %sum_away.1), channel_id=1, source_target_pairs={{4,0},{8,12},{5,1},{9,13},{6,2},{10,14},{7,3},{11,15},{20,16},{24,... | collective-permute-start | bytes 147464 | tf_op jit(solution)/shard_map/ppermute | solution.py:248
  63.3 3.2 %sum_most.1.refs_5_ = f32[2,128,64]{2,1,0:T(8,128)S(1)} custom-call(s32[33]{0:T(128)S(1)} %get-tuple-element.20.scalar_ref, bf16[256,2048]{1,0:T(8,128)(2,1)S(1)} %get-tuple-element.21.refs_0_, bf16[256,2048]{1,0:T(8,128)(2,1)S(1)} %collective-permute-done.refs_1_, bf16[256,2048]{1,0:T(8,128)(2,1)S(1)} %collective-permute-done.1.refs_2_, ...), custom_call_target="tpu_custom_call" | custom-call | bytes 4194304 | tf_op jit(solution)/shard_map/sum_most/pallas_call | solution.py:169
  66.5 1.3 %collective-permute-done.10.refs_0_ = bf16[64,2048]{1,0:T(8,128)(2,1)S(1)} collective-permute-done((bf16[64,2048]{1,0:T(8,128)(2,1)S(1)}, bf16[64,2048]{1,0:T(8,128)(2,1)S(1)}, u32[]{:S(2)}, u32[]{:S(2)}) %collective-permute-start.10) | collective-permute-done | bytes 262176 | tf_op jit(solution)/shard_map/ppermute | solution.py:245
  68.5 1.3 %collective-permute-start.15 = (f32[32,128]{1,0:T(8,128)S(1)}, f32[32,128]{1,0:T(8,128)S(1)}, u32[]{:S(2)}, u32[]{:S(2)}) collective-permute-start(f32[32,128]{1,0:T(8,128)S(1)} %sum_last_away.1), channel_id=1, source_target_pairs={{4,3},{5,2},{6,1},{7,0},{8,15},{9,14},{10,13},{11,12},{20,19},{21,... | collective-permute-start | bytes 49160 | tf_op jit(solution)/shard_map/ppermute | solution.py:252
  69.8 1.2 %sum_last.1 = (f32[32,128]{1,0:T(8,128)S(1)}, f32[32,128]{1,0:T(8,128)S(1)}, f32[32,128]{1,0:T(8,128)S(1)}, f32[32,128]{1,0:T(8,128)S(1)}) custom-call(s32[33]{0:T(128)S(1)} %get-tuple-element.20.scalar_ref, bf16[256,2048]{1,0:T(8,128)(2,1)S(1)} %get-tuple-element.21.refs_0_, bf16[256,2048]{1,0:T(8,128)(2,1)S(1)} %collective-permute-done.refs_1_, ...), custom_call_target="tpu_custom_call" | custom-call | bytes 4194304 | tf_op jit(solution)/shard_map/sum_last/pallas_call | solution.py:169
  71.2 1.6 %collective-permute-start.14 = (f32[32,128]{1,0:T(8,128)S(1)}, f32[32,128]{1,0:T(8,128)S(1)}, u32[]{:S(2)}, u32[]{:S(2)}) collective-permute-start(f32[32,128]{1,0:T(8,128)S(1)} %get-tuple-element.32), channel_id=1, source_target_pairs={{0,3},{1,2},{2,1},{3,0},{4,7},{5,6},{6,5},{7,4},{8,11},{9,10},{10,... | collective-permute-start | bytes 49160 | tf_op jit(solution)/shard_map/ppermute | solution.py:256
  73.2 0.8 %collective-permute-done.12 = f32[32,128]{1,0:T(8,128)S(1)} collective-permute-done((f32[32,128]{1,0:T(8,128)S(1)}, f32[32,128]{1,0:T(8,128)S(1)}, u32[]{:S(2)}, u32[]{:S(2)}) %collective-permute-start.12) | collective-permute-done | bytes 16416 | tf_op jit(solution)/shard_map/ppermute | solution.py:255
  74.1 1.0 %collective-permute-done.13 = f32[32,128]{1,0:T(8,128)S(1)} collective-permute-done((f32[32,128]{1,0:T(8,128)S(1)}, f32[32,128]{1,0:T(8,128)S(1)}, u32[]{:S(2)}, u32[]{:S(2)}) %collective-permute-start.13) | collective-permute-done | bytes 16416 | tf_op jit(solution)/shard_map/ppermute | solution.py:256
  (36 shorter events, 4.4 us)
Async XLA Ops:
  0.0 5.1 %copy-start.3 = (s32[32]{0:T(128)S(1)}, s32[32]{0:T(128)}, u32[]{:S(2)}) copy-start(s32[32]{0:T(128)} %param.7) | copy-start | bytes 388
  0.0 5.1 %copy-start.1 = (s32[16]{0:T(128)S(1)}, s32[16]{0:T(128)}, u32[]{:S(2)}) copy-start(s32[16]{0:T(128)} %param.8) | copy-start | bytes 196
  0.0 5.1 %copy-start.2 = (s32[16]{0:T(128)S(1)}, s32[16]{0:T(128)}, u32[]{:S(2)}) copy-start(s32[16]{0:T(128)} %param.9) | copy-start | bytes 196
  1.3 26.2 %collective-permute-start.3 = (bf16[4,64,2048]{2,1,0:T(8,128)(2,1)S(1)}, bf16[4,64,2048]{2,1,0:T(8,128)(2,1)S(1)}, u32[]{:S(2)}, u32[]{:S(2)}) collective-permute-start(bf16[4,64,2048]{2,1,0:T(8,128)(2,1)S(1)} %own_half.1.refs_1_.refs_3_.refs_4_), channel_id=1, source_target_pairs={{0,4},{4,0},{8,12},{12,8},{1,5},{5,1},{9,13},{13,9},{2,6},{6,2},{1... | collective-permute-start | bytes 3145736 | tf_op jit(solution)/shard_map/ppermute | solution.py:228
  4.4 23.9 %collective-permute-start.5 = (bf16[4,64,2048]{2,1,0:T(8,128)(2,1)S(1)}, bf16[4,64,2048]{2,1,0:T(8,128)(2,1)S(1)}, u32[]{:S(2)}, u32[]{:S(2)}) collective-permute-start(bf16[4,64,2048]{2,1,0:T(8,128)(2,1)S(1)} %own_half.1.refs_1_.refs_3_.refs_4_), channel_id=1, source_target_pairs={{4,8},{8,4},{5,9},{9,5},{6,10},{10,6},{7,11},{11,7},{20,24},{24,20... | collective-permute-start | bytes 3145736 | tf_op jit(solution)/shard_map/ppermute | solution.py:228
  5.2 2.2 %copy-start = (bf16[32,16,4096]{2,1,0:T(8,128)(2,1)S(1)}, bf16[32,16,4096]{2,1,0:T(8,128)(2,1)}, u32[]{:S(2)}) copy-start(bf16[32,16,4096]{2,1,0:T(8,128)(2,1)} %param.5) | copy-start | bytes 12582916
  9.2 26.1 %collective-permute-start.1 = (bf16[256,2048]{1,0:T(8,128)(2,1)S(1)}, bf16[256,2048]{1,0:T(8,128)(2,1)S(1)}, u32[]{:S(2)}, u32[]{:S(2)}) collective-permute-start(bf16[256,2048]{1,0:T(8,128)(2,1)S(1)} %get-tuple-element.21.refs_0_), channel_id=1, source_target_pairs={{0,2},{1,3},{2,0},{3,1},{4,6},{5,7},{6,4},{7,5},{8,10},{9,11},{10,... | collective-permute-start | bytes 3145736 | tf_op jit(solution)/shard_map/ppermute | solution.py:234
  10.7 24.6 %collective-permute-start = (bf16[256,2048]{1,0:T(8,128)(2,1)S(1)}, bf16[256,2048]{1,0:T(8,128)(2,1)S(1)}, u32[]{:S(2)}, u32[]{:S(2)}) collective-permute-start(bf16[256,2048]{1,0:T(8,128)(2,1)S(1)} %get-tuple-element.22), channel_id=1, source_target_pairs={{0,1},{1,0},{2,3},{3,2},{4,5},{5,4},{6,7},{7,6},{8,9},{9,8},{10,11... | collective-permute-start | bytes 3145736 | tf_op jit(solution)/shard_map/ppermute | solution.py:204
  10.7 44.6 %collective-permute-start.2 = (bf16[256,2048]{1,0:T(8,128)(2,1)S(1)}, bf16[256,2048]{1,0:T(8,128)(2,1)S(1)}, u32[]{:S(2)}, u32[]{:S(2)}) collective-permute-start(bf16[256,2048]{1,0:T(8,128)(2,1)S(1)} %get-tuple-element.22), channel_id=1, source_target_pairs={{0,3},{1,2},{2,1},{3,0},{4,7},{5,6},{6,5},{7,4},{8,11},{9,10},{10,... | collective-permute-start | bytes 3145736 | tf_op jit(solution)/shard_map/ppermute | solution.py:235
  27.6 18.0 %collective-permute-start.4 = (bf16[2,64,2048]{2,1,0:T(8,128)(2,1)S(1)}, bf16[2,64,2048]{2,1,0:T(8,128)(2,1)S(1)}, u32[]{:S(2)}, u32[]{:S(2)}) collective-permute-start(bf16[2,64,2048]{2,1,0:T(8,128)(2,1)S(1)} %get-tuple-element.34), channel_id=1, source_target_pairs={{4,8},{8,4},{5,9},{9,5},{6,10},{10,6},{7,11},{11,7},{20,24},{24,20... | collective-permute-start | bytes 1572872 | tf_op jit(solution)/shard_map/ppermute | solution.py:228
  28.3 35.0 %collective-permute-start.8 = (bf16[4,64,2048]{2,1,0:T(8,128)(2,1)S(1)}, bf16[4,64,2048]{2,1,0:T(8,128)(2,1)S(1)}, u32[]{:S(2)}, u32[]{:S(2)}) collective-permute-start(bf16[4,64,2048]{2,1,0:T(8,128)(2,1)S(1)} %collective-permute-done.5.refs_2_.refs_4_.refs_5_), channel_id=1, source_target_pairs={{4,0},{8,12},{5,1},{9,13},{6,2},{10,14},{7,3},{11,15},{20,16},{24,... | collective-permute-start | bytes 3145736 | tf_op jit(solution)/shard_map/ppermute | solution.py:228
  37.7 23.6 %collective-permute-start.9 = (bf16[192,2048]{1,0:T(8,128)(2,1)S(1)}, bf16[192,2048]{1,0:T(8,128)(2,1)S(1)}, u32[]{:S(2)}, u32[]{:S(2)}) collective-permute-start(bf16[192,2048]{1,0:T(8,128)(2,1)S(1)} %pad_maximum_fusion), channel_id=1, source_target_pairs={{0,4},{12,8},{1,5},{13,9},{2,6},{14,10},{3,7},{15,11},{16,20},{28,... | collective-permute-start | bytes 2359304 | tf_op jit(solution)/shard_map/ppermute | solution.py:243
  44.9 16.5 %collective-permute-start.7 = (bf16[2,64,2048]{2,1,0:T(8,128)(2,1)S(1)}, bf16[2,64,2048]{2,1,0:T(8,128)(2,1)S(1)}, u32[]{:S(2)}, u32[]{:S(2)}) collective-permute-start(bf16[2,64,2048]{2,1,0:T(8,128)(2,1)S(1)} %get-tuple-element.33), channel_id=1, source_target_pairs={{4,8},{8,4},{5,9},{9,5},{6,10},{10,6},{7,11},{11,7},{20,24},{24,20... | collective-permute-start | bytes 1572872 | tf_op jit(solution)/shard_map/ppermute | solution.py:228
  45.6 24.2 %collective-permute-start.6 = (bf16[2,64,2048]{2,1,0:T(8,128)(2,1)S(1)}, bf16[2,64,2048]{2,1,0:T(8,128)(2,1)S(1)}, u32[]{:S(2)}, u32[]{:S(2)}) collective-permute-start(bf16[2,64,2048]{2,1,0:T(8,128)(2,1)S(1)} %collective-permute-done.4.refs_7_), channel_id=1, source_target_pairs={{4,0},{8,12},{5,1},{9,13},{6,2},{10,14},{7,3},{11,15},{20,16},{24,... | collective-permute-start | bytes 1572872 | tf_op jit(solution)/shard_map/ppermute | solution.py:228
  55.4 12.5 %collective-permute-start.10 = (bf16[64,2048]{1,0:T(8,128)(2,1)S(1)}, bf16[64,2048]{1,0:T(8,128)(2,1)S(1)}, u32[]{:S(2)}, u32[]{:S(2)}) collective-permute-start(bf16[64,2048]{1,0:T(8,128)(2,1)S(1)} %slice.44), channel_id=1, source_target_pairs={{0,4},{12,8},{1,5},{13,9},{2,6},{14,10},{3,7},{15,11},{16,20},{28,... | collective-permute-start | bytes 786440 | tf_op jit(solution)/shard_map/ppermute | solution.py:245
  62.0 7.8 %collective-permute-start.11 = (f32[96,128]{1,0:T(8,128)S(1)}, f32[96,128]{1,0:T(8,128)S(1)}, u32[]{:S(2)}, u32[]{:S(2)}) collective-permute-start(f32[96,128]{1,0:T(8,128)S(1)} %sum_away.1), channel_id=1, source_target_pairs={{4,0},{8,12},{5,1},{9,13},{6,2},{10,14},{7,3},{11,15},{20,16},{24,... | collective-permute-start | bytes 147464 | tf_op jit(solution)/shard_map/ppermute | solution.py:248
  68.5 6.6 %collective-permute-start.15 = (f32[32,128]{1,0:T(8,128)S(1)}, f32[32,128]{1,0:T(8,128)S(1)}, u32[]{:S(2)}, u32[]{:S(2)}) collective-permute-start(f32[32,128]{1,0:T(8,128)S(1)} %sum_last_away.1), channel_id=1, source_target_pairs={{4,3},{5,2},{6,1},{7,0},{8,15},{9,14},{10,13},{11,12},{20,19},{21,... | collective-permute-start | bytes 49160 | tf_op jit(solution)/shard_map/ppermute | solution.py:252
  71.0 4.1 %collective-permute-start.13 = (f32[32,128]{1,0:T(8,128)S(1)}, f32[32,128]{1,0:T(8,128)S(1)}, u32[]{:S(2)}, u32[]{:S(2)}) collective-permute-start(f32[32,128]{1,0:T(8,128)S(1)} %get-tuple-element.31), channel_id=1, source_target_pairs={{0,2},{1,3},{2,0},{3,1},{4,6},{5,7},{6,4},{7,5},{8,10},{9,11},{10,... | collective-permute-start | bytes 49160 | tf_op jit(solution)/shard_map/ppermute | solution.py:256
  71.2 3.9 %collective-permute-start.14 = (f32[32,128]{1,0:T(8,128)S(1)}, f32[32,128]{1,0:T(8,128)S(1)}, u32[]{:S(2)}, u32[]{:S(2)}) collective-permute-start(f32[32,128]{1,0:T(8,128)S(1)} %get-tuple-element.32), channel_id=1, source_target_pairs={{0,3},{1,2},{2,1},{3,0},{4,7},{5,6},{6,5},{7,4},{8,11},{9,10},{10,... | collective-permute-start | bytes 49160 | tf_op jit(solution)/shard_map/ppermute | solution.py:256
  72.7 1.3 %collective-permute-start.12 = (f32[32,128]{1,0:T(8,128)S(1)}, f32[32,128]{1,0:T(8,128)S(1)}, u32[]{:S(2)}, u32[]{:S(2)}) collective-permute-start(f32[32,128]{1,0:T(8,128)S(1)} %get-tuple-element.30), channel_id=1, source_target_pairs={{0,1},{1,0},{2,3},{3,2},{4,5},{5,4},{6,7},{7,6},{8,9},{9,8},{10,11... | collective-permute-start | bytes 49160 | tf_op jit(solution)/shard_map/ppermute | solution.py:255
